TPU v7x, 128 devices: a whole 4x4x4 slice. The times are simulated.
128 devices in a mesh: blk: 8 (over y, core), sub: 16 (over x, z).
Axes of the slice: x: 4, y: 4, z: 4, core: 2. Of those that a mesh axis runs over, the one named last changes fastest.
Arguments:
- points: bfloat16 [131072, 384], P(('blk', 'sub')), may hold values from -6 to 6
- hilbert_pos: int32 [131072], P(('blk', 'sub')), may hold values from 0 to 131071, as said below
- segment_ids: int32 [131072], P(('blk', 'sub')), may hold values from 0 to 255, never falling along the last dimension, each value on 1 to 1024 neighbouring positions
- cotangent: bfloat16 [131072, 384], P(('blk', 'sub')), may hold values from -6 to 6
- w_qkv: bfloat16 [384, 1152], replicated, may hold values from -3 to 3
- w_proj: bfloat16 [384, 384], replicated, may hold values from -0.3125 to 0.3125
- w_fc1: bfloat16 [384, 1536], replicated, may hold values from -0.3125 to 0.3125
- w_fc2: bfloat16 [1536, 384], replicated, may hold values from -0.15625 to 0.15625
Outputs:
- output: bfloat16 [131072, 384], P(('blk', 'sub'))
- grad_points: bfloat16 [131072, 384], P(('blk', 'sub'))
- grad_qkv: float32 [384, 1152], replicated
- grad_proj: float32 [384, 384], replicated
- grad_fc1: float32 [384, 1536], replicated
- grad_fc2: float32 [1536, 384], replicated
Inputs may be any that keep to these rules, and one draw needn't show every extreme that they name: hilbert_pos is a permutation of all positions; the 1024 points of one device land on the blocks of 1024 Hilbert positions of at most 64 devices, consecutive in device order with wrap-around; at most 32 of them on any one device's block, and 32 is reached in every draw.
All inputs are finite; a program needn't handle non-finite values.
Results may differ from a plain program's by a relative error of at most 0.02.
The roundings to bfloat16 on the way count: a program that leaves them out, or rounds other values in their place, can miss the bound.
Values may be sent and summed in bfloat16 or wider, within the bound.
No kernel may reach another device: no remote copies, remote signals or barrier semaphores. Data moves between devices by JAX's collectives and lax.ppermute only.
A program may use at most 128 MiB of HBM per device.

v0:
```python
import math

import jax
import jax.numpy as jnp
from jax import lax
from jax.sharding import PartitionSpec as P

HEADS = 12
PATCH = 1024


EPSILON = 1e-05


def norm_rows(values):
    centred = values - jnp.mean(values, axis=-1, keepdims=True)
    spread = jnp.mean(centred * centred, axis=-1, keepdims=True)
    return centred * lax.rsqrt(spread + EPSILON)


def attend(packed, segments):
    length = packed.shape[0]
    features = packed.shape[1] // 3
    head_dim = features // HEADS
    split_heads = packed.reshape(length, 3, HEADS, head_dim).transpose(1, 2, 0, 3)
    allowed = segments[:, None] == segments[None, :]
    scaling = 1.0 / math.sqrt(head_dim)

    def one_head(triple):
        queries, keys, values = triple
        scores = jnp.dot(queries, keys.T, preferred_element_type=jnp.float32) * scaling
        scores = jnp.where(allowed, scores, -1e30)
        shifted = jnp.exp(scores - jnp.max(scores, axis=-1, keepdims=True))
        weights = (shifted / jnp.sum(shifted, axis=-1, keepdims=True)).astype(jnp.bfloat16)
        return jnp.dot(weights, values, preferred_element_type=jnp.float32).astype(jnp.bfloat16)

    mixed = lax.map(jax.checkpoint(one_head), (split_heads[0], split_heads[1], split_heads[2]))
    return mixed.transpose(1, 0, 2).reshape(length, features)


def attention_half(inputs, segments, w_qkv, w_proj):
    row_count, features = inputs.shape
    normed = norm_rows(inputs.astype(jnp.float32)).astype(jnp.bfloat16)
    packed = jnp.dot(normed, w_qkv, preferred_element_type=jnp.float32).astype(jnp.bfloat16)
    patches = row_count // PATCH
    attended = lax.map(
        lambda pair: attend(pair[0], pair[1]),
        (packed.reshape(patches, PATCH, 3 * features), segments.reshape(patches, PATCH)),
    )
    attended = attended.reshape(row_count, features)
    return (
        inputs.astype(jnp.float32) + jnp.dot(attended, w_proj, preferred_element_type=jnp.float32)
    ).astype(jnp.bfloat16)


def mlp_half(middle, w_fc1, w_fc2):
    normed_again = norm_rows(middle.astype(jnp.float32)).astype(jnp.bfloat16)
    hidden = jax.nn.gelu(
        jnp.dot(normed_again, w_fc1, preferred_element_type=jnp.float32), approximate=False
    ).astype(jnp.bfloat16)
    return (
        middle.astype(jnp.float32) + jnp.dot(hidden, w_fc2, preferred_element_type=jnp.float32)
    ).astype(jnp.bfloat16)


def on_device(points, hilbert_pos, segment_ids, cotangent, w_qkv, w_proj, w_fc1, w_fc2):
    row_count, features = points.shape
    shards = lax.axis_size(("blk", "sub"))
    capacity = 4 * row_count // shards
    target = hilbert_pos // row_count
    offset = hilbert_pos - target * row_count
    member = (target[:, None] == jnp.arange(shards, dtype=jnp.int32)[None, :]).astype(jnp.int32)
    slot_rank = jnp.sum((jnp.cumsum(member, axis=0) - member) * member, axis=1)
    slot_index = target * capacity + slot_rank
    send_rows = (
        jnp.zeros((shards * capacity, features), jnp.bfloat16)
        .at[slot_index]
        .set(points)
        .reshape(shards, capacity, features)
    )
    send_grad = (
        jnp.zeros((shards * capacity, features), jnp.bfloat16)
        .at[slot_index]
        .set(cotangent)
        .reshape(shards, capacity, features)
    )
    send_slot = (
        jnp.zeros((shards * capacity,), jnp.int32)
        .at[slot_index]
        .set(offset + 1)
        .reshape(shards, capacity)
    )
    received = (
        lax.all_to_all(send_rows, ("blk", "sub"), split_axis=0, concat_axis=0, tiled=True),
        lax.all_to_all(send_grad, ("blk", "sub"), split_axis=0, concat_axis=0, tiled=True),
        lax.all_to_all(send_slot, ("blk", "sub"), split_axis=0, concat_axis=0, tiled=True),
    )
    arrived = received[2].reshape(-1)
    landing = jnp.where(arrived > 0, arrived - 1, row_count)
    ordered = (
        jnp.zeros((row_count, features), jnp.bfloat16)
        .at[landing]
        .set(received[0].reshape(-1, features), mode="drop")
    )
    ordered_grad = (
        jnp.zeros((row_count, features), jnp.bfloat16)
        .at[landing]
        .set(received[1].reshape(-1, features), mode="drop")
    )
    middle, pull_attention = jax.vjp(
        lambda values, first, second: attention_half(values, segment_ids, first, second),
        ordered,
        w_qkv,
        w_proj,
    )
    result, pull_mlp = jax.vjp(mlp_half, middle, w_fc1, w_fc2)
    source_row = jnp.minimum(landing, row_count - 1)
    grad_middle, grad_first, grad_second = pull_mlp(ordered_grad)
    grad_inputs, grad_query, grad_output = pull_attention(grad_middle)
    output_home, grad_home = (
        lax.all_to_all(
            result[source_row].reshape(shards, capacity, features),
            ("blk", "sub"),
            split_axis=0,
            concat_axis=0,
            tiled=True,
        ),
        lax.all_to_all(
            grad_inputs[source_row].reshape(shards, capacity, features),
            ("blk", "sub"),
            split_axis=0,
            concat_axis=0,
            tiled=True,
        ),
    )
    totals = lax.psum(
        (
            grad_query.astype(jnp.float32),
            grad_output.astype(jnp.float32),
            grad_first.astype(jnp.float32),
            grad_second.astype(jnp.float32),
        ),
        ("blk", "sub"),
    )
    output = output_home.reshape(-1, features)[slot_index]
    grad_points = grad_home.reshape(-1, features)[slot_index]
    return (output, grad_points, totals[0], totals[1], totals[2], totals[3])


def solution(mesh):
    placed = (
        P(("blk", "sub"), None),
        P(("blk", "sub")),
        P(("blk", "sub")),
        P(("blk", "sub"), None),
        P(),
        P(),
        P(),
        P(),
    )
    return jax.shard_map(
        on_device,
        mesh=mesh,
        in_specs=placed,
        out_specs=(P(("blk", "sub"), None), P(("blk", "sub"), None), P(), P(), P(), P()),
        check_vma=False,
    )
```

profile of v0, /device:TPU:1, one launch (start us, length us, event | category | flops | bytes accessed | tf_op | source)
XLA Modules:
  0.0 665.5 jit_solution(11841794782152640577)
XLA Ops:
  10.1 4.3 scatter_custom_fusion
  15.2 11.5 %all-to-all-start = ((s32[128,1,32]{2,1,0:T(1,128)}), s32[128,1,32]{2,1,0:T(1,128)S(1)}, u32[]{:S(2)}, u32[]{:S(2)}) async-start(s32[128,1,32]{2,1,0:T(1,128)} %bitcast.4), calls=%async_computation | async-start | bytes 131072 | tf_op jit(solution)/shard_map/all_to_all | solution.py:96
  26.7 7.7 %scatter_custom_fusion.1 = bf16[4096,384]{1,0:T(8,128)(2,1)} fusion(s32[1024]{0:T(1024)S(1)} %get-tuple-element.407, bf16[1024,384]{1,0:T(8,128)(2,1)} %param.12, bf16[]{:T(256)} %constant.227.clone.1), kind=kCustom, calls=%fused_computation.138 | custom fusion | bytes 3146240 | tf_op jit(solution)/shard_map/scatter | solution.py:78
  36.1 8.4 %all-to-all-start.1 = ((bf16[128,32,384]{2,1,0:T(8,128)(2,1)}), bf16[128,32,384]{2,1,0:T(8,128)(2,1)}, u32[]{:S(2)}, u32[]{:S(2)}) async-start(bf16[128,32,384]{2,1,0:T(8,128)(2,1)} %bitcast.143), calls=%async_computation.1 | async-start | bytes 6291456 | tf_op jit(solution)/shard_map/all_to_all | solution.py:94
  44.6 7.7 %scatter_custom_fusion.3 = bf16[4096,384]{1,0:T(8,128)(2,1)} fusion(s32[1024]{0:T(1024)S(1)} %get-tuple-element.407, bf16[1024,384]{1,0:T(8,128)(2,1)} %param.15, bf16[]{:T(256)} %constant.227.clone.1), kind=kCustom, calls=%fused_computation.136 | custom fusion | bytes 3146240 | tf_op jit(solution)/shard_map/scatter | solution.py:84
  53.2 32.0 %all-to-all-done.1 = bf16[128,32,384]{2,1,0:T(8,128)(2,1)} async-done(((bf16[128,32,384]{2,1,0:T(8,128)(2,1)}), bf16[128,32,384]{2,1,0:T(8,128)(2,1)}, u32[]{:S(2)}, u32[]{:S(2)}) %all-to-all-start.1) | async-done | bytes 3145760 | tf_op jit(solution)/shard_map/all_to_all | solution.py:94
  85.2 5.6 all-to-all-start.3
  90.8 18.5 %scatter_custom_fusion.2 = bf16[1024,384]{1,0:T(8,128)(2,1)S(1)} fusion(s32[4096]{0:T(1024)S(1)} %bitcast.154, bf16[4096,384]{1,0:T(8,128)(2,1)} %bitcast.7, bf16[]{:T(256)} %constant.227.clone.1), kind=kCustom, calls=%fused_computation.162 | custom fusion | bytes 786944 | tf_op jit(solution)/shard_map/scatter | solution.py:103
  111.3 4.1 convolution_convert_fusion.1
  115.4 4.3 copy.38
  131.8 61.3 %while.51 = (s32[]{:T(128)}, bf16[12,1024,32]{1,2,0:T(8,128)(2,1)S(1)}, bf16[12,1024,32]{2,1,0:T(8,128)(2,1)}, bf16[12,1024,32]{2,1,0:T(8,128)(2,1)}, bf16[12,10...) while((s32[]{:T(128)}, bf16[12,1024,32]{1,2,0:T(8,128)(2,1)S(1)}, ...), condition=%wide.region_11.12_spmd.clone, body=%wide.region_8.11_spmd.clone.sunk | while | flops 149977088 | bytes 13477965 | solution.py:37
  196.1 18.8 %scatter_custom_fusion.4 = bf16[1024,384]{1,0:T(8,128)(2,1)S(1)} fusion(s32[4096]{0:T(1024)} %bitcast.155, bf16[4096,384]{1,0:T(8,128)(2,1)} %bitcast.20, bf16[]{:T(256)} %constant.227.clone.1), kind=kCustom, calls=%fused_computation.160 | custom fusion | bytes 786944 | tf_op jit(solution)/shard_map/scatter | solution.py:108
  216.0 16.7 %multiply_convert_fusion = (bf16[1024,1536]{1,0:T(8,128)(2,1)}, f32[1024,1536]{1,0:T(8,128)S(1)}, f32[1024,1536]{1,0:T(8,128)S(1)}) fusion(bf16[384,1536]{1,0:T(8,128)(2,1)S(1)} %copy-done, bf16[1024,384]{0,1:T(8,128)(2,1)S(1)} %get-tuple-element.430, f32[1024]{0:T(1024)S(1)} %fusion.111, f32[1024]{0:T(1024)S(1)} %broadcast_multiply_fusion), kind=kOutput, calls=%fused_computation.85 | convolution fusion | flops 1311768576 | bytes 17702912 | tf_op jit(solution)/shard_map/jvp()/dot_general | solution.py:59
  243.3 162.7 %while.52 = (s32[]{:T(128)}, bf16[12,1024,32]{1,2,0:T(8,128)(2,1)S(1)}, bf16[12,1024,32]{1,2,0:T(8,128)(2,1)S(1)}, bf16[12,1024,32]{1,2,0:T(8,128)(2,1)}, bf16[1...) while((s32[]{:T(128)}, ...), condition=%wide.region_24.25_spmd.clone, body=%wide.region_18.24_spmd.clone.sunk | while | flops 379682816 | bytes 46780556 | solution.py:37
  410.3 17.2 %gather_fusion.2 = bf16[4096,384]{1,0:T(8,128)(2,1)} fusion(bf16[1024,384]{1,0:T(8,128)(2,1)S(1)} %copy.49, s32[4096]{0:T(1024)S(1)} %copy-done.16), kind=kCustom, calls=%fused_computation.2 | custom fusion | bytes 6307840 | tf_op jit(solution)/shard_map/gather | solution.py:129
  427.6 10.3 %all-to-all-start.4 = ((bf16[128,32,384]{2,1,0:T(8,128)(2,1)}), bf16[128,32,384]{2,1,0:T(8,128)(2,1)}, u32[]{:S(2)}, u32[]{:S(2)}) async-start(bf16[128,32,384]{2,1,0:T(8,128)(2,1)} %bitcast.140), calls=%async_computation.4 | async-start | bytes 6291456 | tf_op jit(solution)/shard_map/all_to_all | solution.py:128
  439.4 4.1 fusion.64
  454.5 17.0 %gather_fusion = bf16[4096,384]{1,0:T(8,128)(2,1)} fusion(bf16[1024,384]{1,0:T(8,128)(2,1)S(1)} %copy.43, s32[4096]{0:T(1024)S(1)} %copy-done.16), kind=kCustom, calls=%fused_computation | custom fusion | bytes 6307840 | tf_op jit(solution)/shard_map/gather | solution.py:122
  471.6 9.9 %all-to-all-done.4 = bf16[128,32,384]{2,1,0:T(8,128)(2,1)} async-done(((bf16[128,32,384]{2,1,0:T(8,128)(2,1)}), bf16[128,32,384]{2,1,0:T(8,128)(2,1)}, u32[]{:S(2)}, u32[]{:S(2)}) %all-to-all-start.4) | async-done | bytes 3145760 | tf_op jit(solution)/shard_map/all_to_all | solution.py:128
  481.5 5.0 all-to-all-start.2
  486.5 7.3 %gather_fusion.3 = bf16[1024,384]{1,0:T(8,128)(2,1)} fusion(bf16[4096,384]{1,0:T(8,128)(2,1)} %bitcast.29, s32[1024]{0:T(1024)S(1)} %copy-done.21), kind=kCustom, calls=%fused_computation.3 | custom fusion | bytes 1576960 | tf_op jit(solution)/shard_map/gather | solution.py:146
  493.8 36.7 %all-to-all-done.2 = bf16[128,32,384]{2,1,0:T(8,128)(2,1)S(1)} async-done(((bf16[128,32,384]{2,1,0:T(8,128)(2,1)}), bf16[128,32,384]{2,1,0:T(8,128)(2,1)S(1)}, u32[]{:S(2)}, u32[]{:S(2)}) %all-to-all-start.2) | async-done | bytes 3145760 | tf_op jit(solution)/shard_map/all_to_all | solution.py:121
  530.5 5.0 gather_fusion.1
  535.5 115.2 %all-reduce.6.cloned.1.call-done = (f32[384,1152]{1,0:T(8,128)}, f32[384,384]{1,0:T(8,128)}, f32[384,1536]{1,0:T(8,128)}, f32[1536,384]{1,0:T(8,128)}) async-done(((f32[384,1152]{1,0:T(8,128)}, f32[384,384]{1,0:T(8,128)}, f32[384,1536]{1,0:T(8,128)}, f32[1536,384]{1,0:T(8,128)}), (f32[384,1152]{1,0:T(8,128)}, f32[384,384]{1,0:T(8,128)}, f32[384,1536]{1,0:T(8,128)}, ...) | async-done | bytes 7077904 | tf_op jit(solution)/shard_map/psum | solution.py:136
  (323 shorter events, 281.5 us)
Async XLA Ops:
  7.2 208.9 %copy-start = (bf16[384,1536]{1,0:T(8,128)(2,1)S(1)}, bf16[384,1536]{1,0:T(8,128)(2,1)}, u32[]{:S(2)}) copy-start(bf16[384,1536]{1,0:T(8,128)(2,1)} %param.18) | copy-start | bytes 3538948
  15.2 21.0 %all-to-all-start = ((s32[128,1,32]{2,1,0:T(1,128)}), s32[128,1,32]{2,1,0:T(1,128)S(1)}, u32[]{:S(2)}, u32[]{:S(2)}) async-start(s32[128,1,32]{2,1,0:T(1,128)} %bitcast.4), calls=%async_computation | async-start | bytes 131072 | tf_op jit(solution)/shard_map/all_to_all | solution.py:96
  36.1 49.1 %all-to-all-start.1 = ((bf16[128,32,384]{2,1,0:T(8,128)(2,1)}), bf16[128,32,384]{2,1,0:T(8,128)(2,1)}, u32[]{:S(2)}, u32[]{:S(2)}) async-start(bf16[128,32,384]{2,1,0:T(8,128)(2,1)} %bitcast.143), calls=%async_computation.1 | async-start | bytes 6291456 | tf_op jit(solution)/shard_map/all_to_all | solution.py:94
  52.6 38.2 %copy-start.28 = (s32[4096,1]{0,1:T(1,128)}, s32[4096,1]{0,1:T(1,128)S(1)}, u32[]{:S(2)}) copy-start(s32[4096,1]{0,1:T(1,128)S(1)} %get-tuple-element.425) | copy-start | bytes 49156
  85.2 110.8 %all-to-all-start.3 = ((bf16[128,32,384]{2,1,0:T(8,128)(2,1)}), bf16[128,32,384]{2,1,0:T(8,128)(2,1)}, u32[]{:S(2)}, u32[]{:S(2)}) async-start(bf16[128,32,384]{2,1,0:T(8,128)(2,1)} %bitcast.142), calls=%async_computation.3 | async-start | bytes 6291456 | tf_op jit(solution)/shard_map/all_to_all | solution.py:95
  109.7 84.4 %copy-start.2 = (bf16[1024,384]{0,1:T(8,128)(2,1)}, bf16[1024,384]{0,1:T(8,128)(2,1)S(1)}, u32[]{:S(2)}) copy-start(bf16[1024,384]{0,1:T(8,128)(2,1)S(1)} %copy.37) | copy-start | bytes 2359300
  126.2 5.5 copy-start.14
  131.8 62.2 %copy-start.15 = (bf16[384,384]{1,0:T(8,128)(2,1)S(1)}, bf16[384,384]{1,0:T(8,128)(2,1)}, u32[]{:S(2)}) copy-start(bf16[384,384]{1,0:T(8,128)(2,1)} %param.17) | copy-start | bytes 884740
  195.8 42.4 %copy-start.4 = (bf16[1024,384]{0,1:T(8,128)(2,1)}, bf16[1024,384]{0,1:T(8,128)(2,1)S(1)}, u32[]{:S(2)}) copy-start(bf16[1024,384]{0,1:T(8,128)(2,1)S(1)} %get-tuple-element.430) | copy-start | bytes 2359300
  195.8 42.4 %copy-start.19 = (f32[1024]{0:T(1024)}, f32[1024]{0:T(1024)S(1)}, u32[]{:S(2)}) copy-start(f32[1024]{0:T(1024)S(1)} %broadcast_multiply_fusion) | copy-start | bytes 12292
  196.1 42.1 %copy-start.24 = (f32[1024]{0:T(1024)}, f32[1024]{0:T(1024)S(1)}, u32[]{:S(2)}) copy-start(f32[1024]{0:T(1024)S(1)} %fusion.111) | copy-start | bytes 12292
  214.8 17.9 %copy-start.6 = (bf16[1024,384]{1,0:T(8,128)(2,1)}, bf16[1024,384]{1,0:T(8,128)(2,1)S(1)}, u32[]{:S(2)}) copy-start(bf16[1024,384]{1,0:T(8,128)(2,1)S(1)} %scatter_custom_fusion.4) | copy-start | bytes 2359300
  216.0 16.7 %copy-start.29 = (bf16[1536,384]{1,0:T(8,128)(2,1)S(1)}, bf16[1536,384]{1,0:T(8,128)(2,1)}, u32[]{:S(2)}) copy-start(bf16[1536,384]{1,0:T(8,128)(2,1)} %param.19) | copy-start | bytes 3538948
  427.6 10.4 %copy-start.9 = (bf16[12,1024,32]{1,2,0:T(8,128)(2,1)S(1)}, bf16[12,1024,32]{1,2,0:T(8,128)(2,1)}, u32[]{:S(2)}) copy-start(bf16[12,1024,32]{1,2,0:T(8,128)(2,1)} %copy-done.8) | copy-start | bytes 2359300
  427.6 53.9 %all-to-all-start.4 = ((bf16[128,32,384]{2,1,0:T(8,128)(2,1)}), bf16[128,32,384]{2,1,0:T(8,128)(2,1)}, u32[]{:S(2)}, u32[]{:S(2)}) async-start(bf16[128,32,384]{2,1,0:T(8,128)(2,1)} %bitcast.140), calls=%async_computation.4 | async-start | bytes 6291456 | tf_op jit(solution)/shard_map/all_to_all | solution.py:128
  437.9 5.6 copy-start.7
  437.9 212.8 %all-reduce.6.cloned.1.call-start = ((), (), s32[]{:S(2)}) async-start(), calls=%async_computation.5 | async-start | bytes 14155776 | tf_op jit(solution)/shard_map/psum | solution.py:136
  438.0 5.5 copy-start.32
  443.5 3.3 copy-start.34
  471.6 14.9 %copy-start.21 = (s32[1024]{0:T(1024)S(1)}, s32[1024]{0:T(1024)}, u32[]{:S(2)}) copy-start(s32[1024]{0:T(1024)} %get-tuple-element.406) | copy-start | bytes 12292
  481.5 49.0 %all-to-all-start.2 = ((bf16[128,32,384]{2,1,0:T(8,128)(2,1)}), bf16[128,32,384]{2,1,0:T(8,128)(2,1)S(1)}, u32[]{:S(2)}, u32[]{:S(2)}) async-start(bf16[128,32,384]{2,1,0:T(8,128)(2,1)} %bitcast.141), calls=%async_computation.2 | async-start | bytes 6291456 | tf_op jit(solution)/shard_map/all_to_all | solution.py:121
  650.7 5.0 copy-start.12
  650.7 6.4 copy-start.11
  653.7 4.8 copy-start.1
  (17 other events, 28.7 us)
Sparse Core Ops, SparseCore 0:
  449.7 200.9 all-reduce.5
where the time goes:
time: 676 us; the launch traced here: 666 us
  waiting for transfers between devices  196 us (29%)
  matrix products  189 us (28%)
  local copies, waits for them, and re-layouts  164 us (24%)
  other arithmetic  59.2 us (9%)
  starting transfers between devices  40.8 us (6%)
  between operations  14.8 us (2%)
    psum x1, waiting for transfers between devices, on_device(): lax.psum((grad_query.astype(jnp.float32), grad_output.astype(jnp.float32)...  115 us
    dot_general x48, matrix products, one_head(): jnp.dot(queries, keys.T, preferred_element_type=jnp.float32) * scaling  87 us
    dot_general x36, matrix products, one_head(): jnp.dot(weights, values, preferred_element_type=jnp.float32)  57.9 us
    all_to_all x1, waiting for transfers between devices, on_device(): lax.all_to_all(result[source_row].reshape(shards, capacity, features), ('...  36.7 us
    all_to_all x1, waiting for transfers between devices, on_device(): lax.all_to_all(send_rows, ('blk', 'sub'), split_axis=0, concat_axis=0, ti...  32 us
    squeeze x24, local copies, waits for them, and re-layouts, attend(): lax.map(jax.checkpoint(one_head), (split_heads[0], split_heads[1], split_...  25.7 us
    reduce_sum x12, other arithmetic, one_head(): shifted = jnp.exp(scores - jnp.max(scores, axis=-1, keepdims=True))  23.8 us
    dot_general x3, matrix products, mlp_half(): jnp.dot(normed_again, w_fc1, preferred_element_type=jnp.float32)  20.9 us
  transfers between devices with their start and end apart: 6, of which 5 were waited for; matrix products, arithmetic and copies ran while one was open for 25% of the time, Pallas kernels for 0%

commit v1 on v0

v1 whole, which is shorter than its diff:
```python
import math

import jax
import jax.numpy as jnp
from jax import lax
from jax.experimental import pallas as pl
from jax.experimental.pallas import tpu as pltpu
from jax.sharding import PartitionSpec as P

AXES = ("blk", "sub")
ROWS = 1024
D = 384
FF = 1536
LANES = 128
HEAD_DIM = 32
GROUPS = D // LANES
HEADS_PER_GROUP = LANES // HEAD_DIM
SHARDS = 128
CAP = 32
SLOTS = SHARDS * CAP
STEP_SHARDS = 16
STEP_SLOTS = STEP_SHARDS * CAP
STEPS = SHARDS // STEP_SHARDS
WIRE_ROWS = 3 * CAP + 2
EPSILON = 1e-05
SCALING = 1.0 / math.sqrt(HEAD_DIM)
LOG2E = 1.4426950408889634
MASKED = -1e30
TILE = 256
BF = jnp.bfloat16
F32 = jnp.float32
VMEM_LIMIT = 56 * 1024 * 1024

NT = (((1,), (1,)), ((), ()))


def dot(a, b):
    return jnp.dot(a, b, preferred_element_type=F32)


def dot_nt(a, b):
    return lax.dot_general(a, b, NT, preferred_element_type=F32)


def iota(shape, axis):
    return lax.broadcasted_iota(jnp.int32, shape, axis)


def params(grid_dims=1):
    return pltpu.CompilerParams(
        vmem_limit_bytes=VMEM_LIMIT,
        dimension_semantics=("arbitrary",) * grid_dims,
    )


def cost(flops, bytes_accessed, transcendentals=0):
    return pl.CostEstimate(
        flops=int(flops), bytes_accessed=int(bytes_accessed), transcendentals=int(transcendentals)
    )


def row_to_column(row):
    return jnp.broadcast_to(row, (8, row.shape[1])).T[:, 0:1]


def one_hot_slots(slot_row, first):
    ids = iota((STEP_SLOTS, ROWS), 0) + first
    return (ids == slot_row).astype(F32).astype(BF)


def pack_points_kernel(lane_ref, pos_ref, x_ref, out_ref, slot_ref, high_s, low_s):
    step = pl.program_id(0)

    @pl.when(step == 0)
    def _():
        pos = pos_ref[...]
        target = pos >> 10
        offset = pos & (ROWS - 1)
        member = iota((SHARDS, ROWS), 0) == target
        member_bf = member.astype(F32).astype(BF)
        before = (iota((ROWS, ROWS), 0) < iota((ROWS, ROWS), 1)).astype(F32).astype(BF)
        earlier = dot(member_bf, before)
        rank = jnp.sum(jnp.where(member, earlier, 0.0), axis=0, keepdims=True).astype(jnp.int32)
        slot_ref[...] = target * CAP + rank
        lane = (iota((LANES, ROWS), 0) == rank + lane_ref[0]).astype(F32).astype(BF)
        high = ((offset >> 5) + 1).astype(F32)
        low = (offset & 31).astype(F32)
        high_s[...] = dot_nt(jnp.where(member, high, 0.0).astype(BF), lane)
        low_s[...] = dot_nt(jnp.where(member, low, 0.0).astype(BF), lane)

    picked = dot(one_hot_slots(slot_ref[...], step * STEP_SLOTS), x_ref[...]).astype(BF)
    for piece in range(3):
        out_ref[:, piece * CAP : (piece + 1) * CAP, :] = picked[
            :, piece * LANES : (piece + 1) * LANES
        ].reshape(STEP_SHARDS, CAP, LANES)
    first = pl.multiple_of(step * STEP_SHARDS, STEP_SHARDS)
    high = high_s[pl.ds(first, STEP_SHARDS), :]
    low = low_s[pl.ds(first, STEP_SHARDS), :]
    for s in range(STEP_SHARDS):
        pair = jnp.concatenate([high[s : s + 1], low[s : s + 1]], axis=0)
        out_ref[s, 3 * CAP : WIRE_ROWS, :] = pair.astype(BF)


def pack_points(first_lane, pos_row, points):
    return pl.pallas_call(
        pack_points_kernel,
        grid=(STEPS,),
        in_specs=[
            pl.BlockSpec(memory_space=pltpu.SMEM),
            pl.BlockSpec((1, ROWS), lambda i: (0, 0)),
            pl.BlockSpec((ROWS, D), lambda i: (0, 0)),
        ],
        out_specs=[
            pl.BlockSpec((STEP_SHARDS, WIRE_ROWS, LANES), lambda i: (i, 0, 0)),
            pl.BlockSpec((1, ROWS), lambda i: (0, 0)),
        ],
        out_shape=[
            jax.ShapeDtypeStruct((SHARDS, WIRE_ROWS, LANES), BF),
            jax.ShapeDtypeStruct((1, ROWS), jnp.int32),
        ],
        scratch_shapes=[pltpu.VMEM((SHARDS, LANES), F32), pltpu.VMEM((SHARDS, LANES), F32)],
        compiler_params=params(),
        cost_estimate=cost(2 * SLOTS * ROWS * D, 8 * SLOTS * D),
        name="pack_points",
    )(first_lane, pos_row, points)


def pack_rows_kernel(slot_ref, x_ref, out_ref):
    picked = dot(one_hot_slots(slot_ref[...], pl.program_id(0) * STEP_SLOTS), x_ref[...])
    out_ref[...] = picked.astype(BF).reshape(STEP_SHARDS, CAP, D)


def pack_rows(slot_row, values):
    return pl.pallas_call(
        pack_rows_kernel,
        grid=(STEPS,),
        in_specs=[
            pl.BlockSpec((1, ROWS), lambda i: (0, 0)),
            pl.BlockSpec((ROWS, D), lambda i: (0, 0)),
        ],
        out_specs=pl.BlockSpec((STEP_SHARDS, CAP, D), lambda i: (i, 0, 0)),
        out_shape=jax.ShapeDtypeStruct((SHARDS, CAP, D), BF),
        compiler_params=params(),
        cost_estimate=cost(2 * SLOTS * ROWS * D, 4 * SLOTS * D),
        name="pack_rows",
    )(slot_row, values)


def unpack_rows_kernel(slot_ref, home_ref, out_ref, column_s, total_s):
    step = pl.program_id(0)

    @pl.when(step == 0)
    def _():
        column_s[...] = jnp.broadcast_to(
            row_to_column(slot_ref[...].astype(F32)).astype(jnp.int32), (ROWS, LANES)
        )
        total_s[...] = jnp.zeros_like(total_s)

    wide = jnp.concatenate([column_s[...]] * (STEP_SLOTS // LANES), axis=1)
    hot = (iota((ROWS, STEP_SLOTS), 1) + step * STEP_SLOTS == wide).astype(F32).astype(BF)
    total_s[...] += dot(hot, home_ref[...].reshape(STEP_SLOTS, D))

    @pl.when(step == STEPS - 1)
    def _():
        out_ref[...] = total_s[...].astype(BF)


def unpack_rows(slot_row, home):
    return pl.pallas_call(
        unpack_rows_kernel,
        grid=(STEPS,),
        in_specs=[
            pl.BlockSpec((1, ROWS), lambda i: (0, 0)),
            pl.BlockSpec((STEP_SHARDS, CAP, D), lambda i: (i, 0, 0)),
        ],
        out_specs=pl.BlockSpec((ROWS, D), lambda i: (0, 0)),
        out_shape=jax.ShapeDtypeStruct((ROWS, D), BF),
        scratch_shapes=[pltpu.VMEM((ROWS, LANES), jnp.int32), pltpu.VMEM((ROWS, D), F32)],
        compiler_params=params(),
        cost_estimate=cost(2 * SLOTS * ROWS * D, 4 * SLOTS * D),
        name="unpack_rows",
    )(slot_row, home)


def norm_parts(values):
    centred = values - jnp.mean(values, axis=-1, keepdims=True)
    spread = jnp.mean(centred * centred, axis=-1, keepdims=True)
    scale = lax.rsqrt(spread + EPSILON)
    return centred * scale, scale


def norm_pull(normed, scale, upstream):
    across = jnp.mean(upstream, axis=-1, keepdims=True)
    along = jnp.mean(upstream * normed, axis=-1, keepdims=True)
    return scale * (upstream - across - normed * along)


def landing_one_hot(landing):
    return (iota((ROWS, STEP_SLOTS), 0) == landing).astype(F32).astype(BF)


def land_points_kernel(recv_ref, w_ref, ordered_ref, packed_ref, landing_ref, total_s):
    step = pl.program_id(0)

    @pl.when(step == 0)
    def _():
        total_s[...] = jnp.zeros_like(total_s)

    pieces = []
    for group in range(STEP_SHARDS // 4):
        pair = recv_ref[4 * group, 3 * CAP : WIRE_ROWS, :].astype(F32)
        for other in range(1, 4):
            pair = pair + recv_ref[4 * group + other, 3 * CAP : WIRE_ROWS, :].astype(F32)
        pieces.append((pair[0:1] - 1.0) * 32.0 + pair[1:2])
    landing = jnp.concatenate(pieces, axis=1).astype(jnp.int32)
    landing_ref[0] = landing
    rows = jnp.concatenate(
        [
            recv_ref[:, piece * CAP : (piece + 1) * CAP, :].reshape(STEP_SLOTS, LANES)
            for piece in range(3)
        ],
        axis=1,
    )
    total_s[...] += dot(landing_one_hot(landing), rows)

    @pl.when(step == STEPS - 1)
    def _():
        ordered = total_s[...]
        ordered_ref[...] = ordered.astype(BF)
        normed, _ = norm_parts(ordered)
        packed_ref[...] = dot(normed.astype(BF), w_ref[...]).astype(BF)


def land_points(received, w_qkv):
    return pl.pallas_call(
        land_points_kernel,
        grid=(STEPS,),
        in_specs=[
            pl.BlockSpec((STEP_SHARDS, WIRE_ROWS, LANES), lambda i: (i, 0, 0)),
            pl.BlockSpec((D, 3 * D), lambda i: (0, 0)),
        ],
        out_specs=[
            pl.BlockSpec((ROWS, D), lambda i: (0, 0)),
            pl.BlockSpec((ROWS, 3 * D), lambda i: (0, 0)),
            pl.BlockSpec((1, 1, STEP_SLOTS), lambda i: (i, 0, 0)),
        ],
        out_shape=[
            jax.ShapeDtypeStruct((ROWS, D), BF),
            jax.ShapeDtypeStruct((ROWS, 3 * D), BF),
            jax.ShapeDtypeStruct((STEPS, 1, STEP_SLOTS), jnp.int32),
        ],
        scratch_shapes=[pltpu.VMEM((ROWS, D), F32)],
        compiler_params=params(),
        cost_estimate=cost(2 * SLOTS * ROWS * D + 6 * ROWS * D * D, 6 * SLOTS * D),
        name="land_points",
    )(received, w_qkv)


def land_rows_kernel(landing_ref, recv_ref, out_ref, total_s):
    step = pl.program_id(0)

    @pl.when(step == 0)
    def _():
        total_s[...] = jnp.zeros_like(total_s)

    total_s[...] += dot(landing_one_hot(landing_ref[0]), recv_ref[...].reshape(STEP_SLOTS, D))

    @pl.when(step == STEPS - 1)
    def _():
        out_ref[...] = total_s[...].astype(BF)


def land_rows(landing, received):
    return pl.pallas_call(
        land_rows_kernel,
        grid=(STEPS,),
        in_specs=[
            pl.BlockSpec((1, 1, STEP_SLOTS), lambda i: (i, 0, 0)),
            pl.BlockSpec((STEP_SHARDS, CAP, D), lambda i: (i, 0, 0)),
        ],
        out_specs=pl.BlockSpec((ROWS, D), lambda i: (0, 0)),
        out_shape=jax.ShapeDtypeStruct((ROWS, D), BF),
        scratch_shapes=[pltpu.VMEM((ROWS, D), F32)],
        compiler_params=params(),
        cost_estimate=cost(2 * SLOTS * ROWS * D, 4 * SLOTS * D),
        name="land_rows",
    )(landing, received)


def return_one_hot(landing):
    column = row_to_column(landing.astype(F32)).astype(jnp.int32)
    return (iota((STEP_SLOTS, ROWS), 1) == column).astype(F32).astype(BF)


def return_rows_kernel(landing_ref, x_ref, out_ref):
    picked = dot(return_one_hot(landing_ref[0]), x_ref[...])
    out_ref[...] = picked.astype(BF).reshape(STEP_SHARDS, CAP, D)


def return_rows(landing, values):
    return pl.pallas_call(
        return_rows_kernel,
        grid=(STEPS,),
        in_specs=[
            pl.BlockSpec((1, 1, STEP_SLOTS), lambda i: (i, 0, 0)),
            pl.BlockSpec((ROWS, D), lambda i: (0, 0)),
        ],
        out_specs=pl.BlockSpec((STEP_SHARDS, CAP, D), lambda i: (i, 0, 0)),
        out_shape=jax.ShapeDtypeStruct((SHARDS, CAP, D), BF),
        compiler_params=params(),
        cost_estimate=cost(2 * SLOTS * ROWS * D, 4 * SLOTS * D),
        name="return_rows",
    )(landing, values)


def three_parts(values):
    high = values.astype(BF)
    rest = values - high.astype(F32)
    middle = rest.astype(BF)
    return high, middle, (rest - middle.astype(F32)).astype(BF)


def write_bias(bias_s, column_ref, row_ref):
    bias_s[...] = jnp.where(column_ref[...] == row_ref[...], 0.0, MASKED)


def head_of_lane():
    return iota((ROWS, LANES), 1) // HEAD_DIM


def roll_lanes(values, by):
    return pltpu.roll(values.astype(F32), by % LANES, 1)


def query_side(q, head, owner, shift=None):
    near, far = (head + 1) % HEADS_PER_GROUP, (head + 2) % HEADS_PER_GROUP
    high, middle, low = (part.astype(F32) for part in three_parts(q * (SCALING * LOG2E)))
    first = jnp.where(owner == head, high, 0.0)
    second = jnp.where(
        owner == near,
        roll_lanes(middle, HEAD_DIM),
        jnp.where(owner == far, roll_lanes(low, 2 * HEAD_DIM), 0.0),
    )
    if shift is not None:
        lane = iota((ROWS, LANES), 1) - head * HEAD_DIM
        parts = [part.astype(F32) for part in three_parts(-shift)]
        for at, part in enumerate(parts):
            second = jnp.where(lane == at, part, second)
    return jnp.concatenate([first.astype(BF), second.astype(BF)], axis=1)


def key_side(k, head, owner, shifted):
    near, far = (head + 1) % HEADS_PER_GROUP, (head + 2) % HEADS_PER_GROUP
    second = jnp.where(
        owner == near,
        roll_lanes(k, HEAD_DIM),
        jnp.where(owner == far, roll_lanes(k, 2 * HEAD_DIM), 0.0),
    )
    if shifted:
        lane = iota((ROWS, LANES), 1) - head * HEAD_DIM
        second = jnp.where((lane >= 0) & (lane < 3), 1.0, second)
    return jnp.concatenate([k.astype(BF), second.astype(BF)], axis=1)


def attend_kernel(column_ref, row_ref, q_ref, k_ref, v_ref, mixed_ref, exact_ref, level_ref, bias_s):
    @pl.when(pl.program_id(0) == 0)
    def _():
        write_bias(bias_s, column_ref, row_ref)

    owner = head_of_lane()
    q, k, v = (ref[...].astype(F32) for ref in (q_ref, k_ref, v_ref))
    owner_tile = owner[:TILE]
    for head in range(HEADS_PER_GROUP):
        queries = query_side(q, head, owner)
        keys = key_side(k, head, owner, False)
        values = jnp.concatenate(
            [jnp.where(owner == head, v, 0.0).astype(BF), jnp.ones((ROWS, LANES), BF)], axis=1
        )
        for tile in range(ROWS // TILE):
            rows = slice(tile * TILE, (tile + 1) * TILE)
            scores = dot_nt(queries[rows], keys) + bias_s[rows, :]
            most = jnp.max(scores, axis=-1, keepdims=True)
            raised = jnp.exp2(scores - most).astype(BF)
            both = dot(raised, values)
            total = both[:, LANES:]
            result = both[:, :LANES] / total
            level = most + jnp.log2(total)
            if head == 0:
                exact_ref[rows, :] = result
                level_ref[rows, :] = level
            else:
                mine = owner_tile == head
                exact_ref[rows, :] = jnp.where(mine, result, exact_ref[rows, :])
                level_ref[rows, :] = jnp.where(mine, level, level_ref[rows, :])
    mixed_ref[...] = exact_ref[...].astype(BF)


def group_spec(first=0):
    return pl.BlockSpec((ROWS, LANES), lambda g: (0, first + g))


def whole(shape):
    return pl.BlockSpec(shape, lambda g: (0,) * len(shape))


def attend(segment_column, segment_row, packed):
    return pl.pallas_call(
        attend_kernel,
        grid=(GROUPS,),
        in_specs=[
            whole((ROWS, 1)),
            whole((1, ROWS)),
            group_spec(0),
            group_spec(GROUPS),
            group_spec(2 * GROUPS),
        ],
        out_specs=[group_spec()] * 3,
        out_shape=[
            jax.ShapeDtypeStruct((ROWS, D), BF),
            jax.ShapeDtypeStruct((ROWS, D), F32),
            jax.ShapeDtypeStruct((ROWS, D), F32),
        ],
        scratch_shapes=[pltpu.VMEM((ROWS, ROWS), F32)],
        compiler_params=params(),
        cost_estimate=cost(24e9, 8 * ROWS * D, 12 * ROWS * ROWS),
        name="attend",
    )(segment_column, segment_row, packed, packed, packed)


def attend_back_kernel(
    column_ref,
    row_ref,
    q_ref,
    k_ref,
    v_ref,
    up_ref,
    exact_ref,
    level_ref,
    dq_ref,
    dk_ref,
    dv_ref,
    bias_s,
    dqt_s,
    dk_s,
    dv_s,
):
    @pl.when(pl.program_id(0) == 0)
    def _():
        write_bias(bias_s, column_ref, row_ref)

    owner = head_of_lane()
    q, k, v, up = (ref[...].astype(F32) for ref in (q_ref, k_ref, v_ref, up_ref))
    level = level_ref[...]
    keys_t = k.T.astype(BF)
    from_head = iota((LANES, LANES), 0) // HEAD_DIM
    to_head = iota((LANES, LANES), 1) // HEAD_DIM
    spread = ((from_head + 1) % HEADS_PER_GROUP == to_head).astype(F32).astype(BF)
    delta = sum(dot(part, spread) for part in three_parts(up * exact_ref[...]))
    delta_parts = [part.astype(F32) for part in three_parts(-delta)]
    for head in range(HEADS_PER_GROUP):
        mine = owner == head
        near = (head + 1) % HEADS_PER_GROUP
        lane = iota((ROWS, LANES), 1) - near * HEAD_DIM
        queries = query_side(q, head, owner, level)
        keys = key_side(k, head, owner, True)
        up_mine = jnp.where(mine, up, 0.0)
        up_side = up_mine
        for at, part in enumerate(delta_parts):
            up_side = jnp.where(lane == at, part, up_side)
        up_side = up_side.astype(BF)
        up_mine = up_mine.astype(BF)
        value_side = jnp.where((lane >= 0) & (lane < 3), 1.0, v).astype(BF)
        query_mine = jnp.where(mine, q, 0.0).astype(BF)
        head_rows = slice(head * HEAD_DIM, (head + 1) * HEAD_DIM)
        for tile in range(ROWS // TILE):
            rows = slice(tile * TILE, (tile + 1) * TILE)
            weights = jnp.exp2(dot_nt(keys[rows], queries) + bias_s[rows, :])
            pulled = weights * dot_nt(value_side[rows], up_side)
            pulled = pulled.astype(BF)
            dv_part = dot(weights.astype(BF), up_mine)
            dk_part = dot(pulled, query_mine)
            dq_part = dot(keys_t[head_rows, rows], pulled)
            if head == 0:
                dv_s[rows, :] = dv_part
                dk_s[rows, :] = dk_part
            else:
                dv_s[rows, :] += dv_part
                dk_s[rows, :] += dk_part
            if tile == 0:
                dqt_s[head_rows, :] = dq_part
            else:
                dqt_s[head_rows, :] += dq_part
    dq_ref[...] = (dqt_s[...] * SCALING).T.astype(BF)
    dk_ref[...] = (dk_s[...] * SCALING).astype(BF)
    dv_ref[...] = dv_s[...].astype(BF)


def attend_back(segment_column, segment_row, packed, upstream, exact, level):
    return pl.pallas_call(
        attend_back_kernel,
        grid=(GROUPS,),
        in_specs=[
            whole((ROWS, 1)),
            whole((1, ROWS)),
            group_spec(0),
            group_spec(GROUPS),
            group_spec(2 * GROUPS),
            group_spec(),
            group_spec(),
            group_spec(),
        ],
        out_specs=[group_spec()] * 3,
        out_shape=[jax.ShapeDtypeStruct((ROWS, D), BF)] * 3,
        scratch_shapes=[
            pltpu.VMEM((ROWS, ROWS), F32),
            pltpu.VMEM((LANES, ROWS), F32),
            pltpu.VMEM((ROWS, LANES), F32),
            pltpu.VMEM((ROWS, LANES), F32),
        ],
        compiler_params=params(),
        cost_estimate=cost(60e9, 16 * ROWS * D, 12 * ROWS * ROWS),
        name="attend_back",
    )(segment_column, segment_row, packed, packed, packed, upstream, exact, level)


FF_STEP = 512
FF_STEPS = FF // FF_STEP


def mlp_kernel(
    ordered_ref,
    mixed_ref,
    up_ref,
    w_proj_ref,
    w1_ref,
    w2_ref,
    block_ref,
    d_middle_ref,
    d_mixed_ref,
    d_proj_ref,
    d_w1_ref,
    d_w2_ref,
    middle_s,
    normed_s,
    normed_t_s,
    up_t_s,
    out_s,
    d_normed_s,
):
    step = pl.program_id(0)
    up = up_ref[...]

    @pl.when(step == 0)
    def _():
        middle = (
            ordered_ref[...].astype(F32) + dot(mixed_ref[...], w_proj_ref[...])
        ).astype(BF)
        middle_s[...] = middle
        normed, _ = norm_parts(middle.astype(F32))
        normed = normed.astype(BF)
        normed_s[...] = normed
        normed_t_s[...] = normed.astype(F32).T.astype(BF)
        up_t_s[...] = up.astype(F32).T.astype(BF)
        out_s[...] = jnp.zeros_like(out_s)
        d_normed_s[...] = jnp.zeros_like(d_normed_s)

    w1, w2 = w1_ref[...], w2_ref[...]
    before = dot(normed_s[...], w1)
    d_hidden = dot_nt(up, w2).astype(BF).astype(F32)
    half = 0.5 * (1.0 + lax.erf(before * math.sqrt(0.5)))
    density = jnp.exp(before * before * -0.5) * (1.0 / math.sqrt(2.0 * math.pi))
    hidden = (before * half).astype(BF)
    d_before = (d_hidden * (half + before * density)).astype(BF)
    out_s[...] += dot(hidden, w2)
    d_w2_ref[...] = dot(up_t_s[...], hidden).T.astype(BF)
    d_w1_ref[...] = dot(normed_t_s[...], d_before).astype(BF)
    d_normed_s[...] += dot_nt(d_before, w1)

    @pl.when(step == FF_STEPS - 1)
    def _():
        middle = middle_s[...].astype(F32)
        block_ref[...] = (middle + out_s[...]).astype(BF)
        normed, scale = norm_parts(middle)
        pulled = norm_pull(normed, scale, d_normed_s[...].astype(BF).astype(F32)).astype(BF)
        d_middle = (up.astype(F32) + pulled.astype(F32)).astype(BF)
        d_middle_ref[...] = d_middle
        d_mixed_ref[...] = dot_nt(d_middle, w_proj_ref[...]).astype(BF)
        d_proj_ref[...] = dot(mixed_ref[...].astype(F32).T.astype(BF), d_middle).astype(BF)


def mlp(ordered, mixed, upstream, w_proj, w_fc1, w_fc2):
    rows = whole((ROWS, D))
    return pl.pallas_call(
        mlp_kernel,
        grid=(FF_STEPS,),
        in_specs=[
            rows,
            rows,
            rows,
            whole((D, D)),
            pl.BlockSpec((D, FF_STEP), lambda i: (0, i)),
            pl.BlockSpec((FF_STEP, D), lambda i: (i, 0)),
        ],
        out_specs=[
            rows,
            rows,
            rows,
            whole((D, D)),
            pl.BlockSpec((D, FF_STEP), lambda i: (0, i)),
            pl.BlockSpec((FF_STEP, D), lambda i: (i, 0)),
        ],
        out_shape=[
            jax.ShapeDtypeStruct((ROWS, D), BF),
            jax.ShapeDtypeStruct((ROWS, D), BF),
            jax.ShapeDtypeStruct((ROWS, D), BF),
            jax.ShapeDtypeStruct((D, D), BF),
            jax.ShapeDtypeStruct((D, FF), BF),
            jax.ShapeDtypeStruct((FF, D), BF),
        ],
        scratch_shapes=[
            pltpu.VMEM((ROWS, D), BF),
            pltpu.VMEM((ROWS, D), BF),
            pltpu.VMEM((D, ROWS), BF),
            pltpu.VMEM((D, ROWS), BF),
            pltpu.VMEM((ROWS, D), F32),
            pltpu.VMEM((ROWS, D), F32),
        ],
        compiler_params=params(),
        cost_estimate=cost(12 * ROWS * D * FF, 20 * ROWS * D, 2 * ROWS * FF),
        name="mlp",
    )(ordered, mixed, upstream, w_proj, w_fc1, w_fc2)


def inputs_back_kernel(ordered_ref, dq_ref, dk_ref, dv_ref, d_middle_ref, w_ref, out_ref):
    normed, scale = norm_parts(ordered_ref[...].astype(F32))
    d_normed = (
        dot_nt(dq_ref[...], w_ref[:, :D])
        + dot_nt(dk_ref[...], w_ref[:, D : 2 * D])
        + dot_nt(dv_ref[...], w_ref[:, 2 * D :])
    )
    pulled = norm_pull(normed, scale, d_normed.astype(BF).astype(F32)).astype(BF)
    out_ref[...] = (d_middle_ref[...].astype(F32) + pulled.astype(F32)).astype(BF)


def inputs_back(ordered, dq, dk, dv, d_middle, w_qkv):
    rows = whole((ROWS, D))
    return pl.pallas_call(
        inputs_back_kernel,
        grid=(1,),
        in_specs=[rows] * 5 + [whole((D, 3 * D))],
        out_specs=rows,
        out_shape=jax.ShapeDtypeStruct((ROWS, D), BF),
        compiler_params=params(),
        cost_estimate=cost(6 * ROWS * D * D, 14 * ROWS * D),
        name="inputs_back",
    )(ordered, dq, dk, dv, d_middle, w_qkv)


def qkv_back_kernel(ordered_ref, dq_ref, dk_ref, dv_ref, out_ref):
    normed, _ = norm_parts(ordered_ref[...].astype(F32))
    normed_t = normed.astype(BF).astype(F32).T.astype(BF)
    for at, ref in enumerate((dq_ref, dk_ref, dv_ref)):
        out_ref[:, at * D : (at + 1) * D] = dot(normed_t, ref[...]).astype(BF)


def qkv_back(ordered, dq, dk, dv):
    rows = whole((ROWS, D))
    return pl.pallas_call(
        qkv_back_kernel,
        grid=(1,),
        in_specs=[rows] * 4,
        out_specs=whole((D, 3 * D)),
        out_shape=jax.ShapeDtypeStruct((D, 3 * D), BF),
        compiler_params=params(),
        cost_estimate=cost(6 * ROWS * D * D, 14 * ROWS * D),
        name="qkv_back",
    )(ordered, dq, dk, dv)


def exchange(values):
    return lax.all_to_all(values, AXES, split_axis=0, concat_axis=0, tiled=True)


def total_of(values):
    return lax.psum(values, AXES)


def on_device(points, hilbert_pos, segment_ids, cotangent, w_qkv, w_proj, w_fc1, w_fc2):
    first_lane = ((lax.axis_index(AXES) % 4) * CAP).astype(jnp.int32).reshape(1)
    segment_row = segment_ids.reshape(1, ROWS)
    segment_column = segment_ids.reshape(ROWS, 1)
    wire, slot_row = pack_points(first_lane, hilbert_pos.reshape(1, ROWS), points)
    ordered, packed, landing = land_points(exchange(wire), w_qkv)
    up_received = exchange(pack_rows(slot_row, cotangent))
    mixed, exact, level = attend(segment_column, segment_row, packed)
    upstream = land_rows(landing, up_received)
    block, d_middle, d_mixed, d_proj, d_w1, d_w2 = mlp(
        ordered, mixed, upstream, w_proj, w_fc1, w_fc2
    )
    output_home = exchange(return_rows(landing, block))
    total_proj, total_w1, total_w2 = total_of((d_proj, d_w1, d_w2))
    dq, dk, dv = attend_back(segment_column, segment_row, packed, d_mixed, exact, level)
    grad_home = exchange(
        return_rows(landing, inputs_back(ordered, dq, dk, dv, d_middle, w_qkv))
    )
    d_qkv, total_w2 = lax.optimization_barrier((qkv_back(ordered, dq, dk, dv), total_w2))
    total_qkv = total_of(d_qkv)
    output = unpack_rows(slot_row, output_home)
    grad_points = unpack_rows(slot_row, grad_home)
    return (
        output,
        grad_points,
        total_qkv.astype(F32),
        total_proj.astype(F32),
        total_w1.astype(F32),
        total_w2.astype(F32),
    )


def solution(mesh):
    placed = (P(AXES, None), P(AXES), P(AXES), P(AXES, None), P(), P(), P(), P())
    return jax.shard_map(
        on_device,
        mesh=mesh,
        in_specs=placed,
        out_specs=(P(AXES, None), P(AXES, None), P(), P(), P(), P()),
        check_vma=False,
    )
```

time: 676 us -> 614 us (0.908)
  waiting for transfers between devices: 196 us -> 392 us
  matrix products: 189 us -> 0 us
  Pallas kernels: 0 us -> 163 us
  local copies, waits for them, and re-layouts: 164 us -> 5.71 us
  other arithmetic: 59.2 us -> 7.65 us
  starting transfers between devices: 40.8 us -> 27.4 us
    psum x1 -> x2, waiting for transfers between devices: 115 us -> 317 us  [total_of(): return lax.psum(values, AXES)]
    dot_general x96 -> x0, matrix products: 189 us -> none  [the longest x48 87 us: one_head(): jnp.dot(queries, keys.T, preferred_element_type=jnp.float32) * scaling]
    pallas_call x0 -> x13, Pallas kernels: none -> 163 us  [the longest x1 39.3 us: attend_back(): pl.pallas_call(attend_back_kernel, grid=(GROUPS,), in_specs=[whole((ROWS,...]
    scatter x7 -> x0, local copies, waits for them, and re-layouts: 58.4 us -> none  [the longest x2 19.9 us: on_device(): ordered_grad = jnp.zeros((row_count, features), jnp.bfloat16).at[landing]...]
    gather x4 -> x0, local copies, waits for them, and re-layouts: 46.6 us -> none  [the longest x1 17.2 us: on_device(): grad_inputs[source_row].reshape(shards, capacity, features)]
    reduce_sum x42 -> x0, other arithmetic: 45.4 us -> none  [the longest x12 23.8 us: one_head(): shifted = jnp.exp(scores - jnp.max(scores, axis=-1, keepdims=True))]
    squeeze x25 -> x0, local copies, waits for them, and re-layouts: 28.5 us -> none  [the longest x24 25.7 us: attend(): lax.map(jax.checkpoint(one_head), (split_heads[0], split_heads[1], split_...]
    unnamed x77 -> x10, local copies, waits for them, and re-layouts: 20.8 us -> 4.69 us
  transfers between devices with their start and end apart: 6 -> 6, of which waited for: 5 -> 5; matrix products, arithmetic and copies ran while one was open for 25% -> 1% of each run, Pallas kernels for 0% -> 10%
where the time goes in v1:
time: 614 us; the launch traced here: 610 us
  waiting for transfers between devices  392 us (64%)
  Pallas kernels  163 us (27%)
  starting transfers between devices  27.4 us (4%)
  between operations  14.4 us (2%)
  other arithmetic  7.65 us (1%)
    psum x2, waiting for transfers between devices, total_of(): return lax.psum(values, AXES)  317 us
    all_to_all x4, waiting for transfers between devices, exchange(): return lax.all_to_all(values, AXES, split_axis=0, concat_axis=0, tiled=True)  74.3 us
    pallas_call x1, Pallas kernels, attend_back(): pl.pallas_call(attend_back_kernel, grid=(GROUPS,), in_specs=[whole((ROWS,...  39.3 us
    all_to_all x4, starting transfers between devices, exchange(): return lax.all_to_all(values, AXES, split_axis=0, concat_axis=0, tiled=True)  27.3 us
    pallas_call x1, Pallas kernels, attend(): pl.pallas_call(attend_kernel, grid=(GROUPS,), in_specs=[whole((ROWS, 1)),...  20.8 us
    pallas_call x2, Pallas kernels, return_rows(): pl.pallas_call(return_rows_kernel, grid=(STEPS,), in_specs=[pl.BlockSpec(...  19.8 us
    pallas_call x2, Pallas kernels, unpack_rows(): pl.pallas_call(unpack_rows_kernel, grid=(STEPS,), in_specs=[pl.BlockSpec(...  18.1 us
    pallas_call x1, Pallas kernels, mlp(): pl.pallas_call(mlp_kernel, grid=(FF_STEPS,), in_specs=[rows, rows, rows,...  17.7 us
  transfers between devices with their start and end apart: 6, of which 5 were waited for; matrix products, arithmetic and copies ran while one was open for 1% of the time, Pallas kernels for 10%

profile of v1, /device:TPU:1, one launch (start us, length us, event | category | flops | bytes accessed | tf_op | source)
XLA Modules:
  0.0 609.6 jit_solution(7682150362171943625)
XLA Ops:
  7.2 8.5 %pack_points.1 = (bf16[128,98,128]{2,1,0:T(8,128)(2,1)}, s32[1,1024]{1,0:T(1,128)}) custom-call(s32[1]{0:T(128)} %bitcast.lane_ref, s32[1,1024]{1,0:T(1,128)} %bitcast.7, bf16[1024,384]{1,0:T(8,128)(2,1)} %x_ref.2), custom_call_target="tpu_custom_call" | custom-call | flops 3221225472 | bytes 12582912 | tf_op jit(solution)/shard_map/pack_points/pallas_call | solution.py:105
  15.7 11.5 %all-to-all-start = ((bf16[128,98,128]{2,1,0:T(8,128)(2,1)}), bf16[128,98,128]{2,1,0:T(8,128)(2,1)S(1)}, u32[]{:S(2)}, u32[]{:S(2)}) async-start(bf16[128,98,128]{2,1,0:T(8,128)(2,1)} %get-tuple-element.26), calls=%async_computation | async-start | bytes 6815744 | tf_op jit(solution)/shard_map/all_to_all | solution.py:681
  27.2 7.8 %pack_rows.1 = bf16[128,32,384]{2,1,0:T(8,128)(2,1)} custom-call(s32[1,1024]{1,0:T(1,128)} %get-tuple-element.25.slot_ref, bf16[1024,384]{1,0:T(8,128)(2,1)} %x_ref.3), custom_call_target="tpu_custom_call" | custom-call | flops 3221225472 | bytes 6291456 | tf_op jit(solution)/shard_map/pack_rows/pallas_call | solution.py:134
  35.0 36.1 %all-to-all-done.recv_ref = bf16[128,98,128]{2,1,0:T(8,128)(2,1)S(1)} async-done(((bf16[128,98,128]{2,1,0:T(8,128)(2,1)}), bf16[128,98,128]{2,1,0:T(8,128)(2,1)S(1)}, u32[]{:S(2)}, u32[]{:S(2)}) %all-to-all-start) | async-done | bytes 3211296 | tf_op jit(solution)/shard_map/all_to_all | solution.py:681
  72.8 5.9 all-to-all-start.1
  79.7 11.6 %land_points.1 = (bf16[1024,384]{1,0:T(8,128)(2,1)}, bf16[1024,1152]{1,0:T(8,128)(2,1)}, s32[8,1,512]{2,1,0:T(1,128)}) custom-call(bf16[128,98,128]{2,1,0:T(8,128)(2,1)} %copy-done, bf16[384,1152]{1,0:T(8,128)(2,1)} %w_ref.3), custom_call_target="tpu_custom_call" | custom-call | flops 4127195136 | bytes 9437184 | tf_op jit(solution)/shard_map/land_points/pallas_call | solution.py:235
  91.3 20.8 %attend.1 = (bf16[1024,384]{1,0:T(8,128)(2,1)}, f32[1024,384]{1,0:T(8,128)}, f32[1024,384]{1,0:T(8,128)}) custom-call(s32[1024,1]{1,0:T(8,128)} %copy.14.column_ref, s32[1,1024]{1,0:T(1,128)} %bitcast.4, bf16[1024,1152]{1,0:T(8,128)(2,1)} %get-tuple-element.29.q_ref.k_ref.v_ref, bf16[1024,1152]{1,0:T(8,128)(2,1)} %get-tuple-element.29.q_ref.k_ref.v_ref, ...), custom_call_target="tpu_custom_call" | custom-call | flops 24000000000 | bytes 3145728 | tf_op jit(solution)/shard_map/attend/pallas_call | solution.py:407
  112.1 7.2 %all-to-all-done.1.recv_ref = bf16[128,32,384]{2,1,0:T(8,128)(2,1)} async-done(((bf16[128,32,384]{2,1,0:T(8,128)(2,1)}), bf16[128,32,384]{2,1,0:T(8,128)(2,1)}, u32[]{:S(2)}, u32[]{:S(2)}) %all-to-all-start.1) | async-done | bytes 3145760 | tf_op jit(solution)/shard_map/all_to_all | solution.py:681
  119.3 8.7 %land_rows.1.up_ref = bf16[1024,384]{1,0:T(8,128)(2,1)} custom-call(s32[8,1,512]{2,1,0:T(1,128)} %get-tuple-element.27.landing_ref, bf16[128,32,384]{2,1,0:T(8,128)(2,1)} %all-to-all-done.1.recv_ref), custom_call_target="tpu_custom_call" | custom-call | flops 3221225472 | bytes 6291456 | tf_op jit(solution)/shard_map/land_rows/pallas_call | solution.py:274
  128.0 17.7 %mlp.1 = (bf16[1024,384]{1,0:T(8,128)(2,1)}, bf16[1024,384]{1,0:T(8,128)(2,1)}, bf16[1024,384]{1,0:T(8,128)(2,1)}, bf16[384,384]{1,0:T(8,128)(2,1)}, bf16[384,15...) custom-call(bf16[1024,384]{1,0:T(8,128)(2,1)} %get-tuple-element.28.ordered_ref, ...), custom_call_target="tpu_custom_call" | custom-call | flops 7247757312 | bytes 7864320 | tf_op jit(solution)/shard_map/mlp/pallas_call | solution.py:593
  145.7 39.3 %attend_back.1 = (bf16[1024,384]{1,0:T(8,128)(2,1)}, bf16[1024,384]{1,0:T(8,128)(2,1)}, bf16[1024,384]{1,0:T(8,128)(2,1)}) custom-call(s32[1024,1]{1,0:T(8,128)} %copy.14.column_ref, s32[1,1024]{1,0:T(1,128)} %bitcast.5, bf16[1024,1152]{1,0:T(8,128)(2,1)} %get-tuple-element.29.q_ref.k_ref.v_ref, bf16[1024,1152]{1,0:T(8,128)(2,1)} %get-tuple-element.29.q_ref.k_ref.v_ref, ...), custom_call_target="tpu_custom_call" | custom-call | flops 60000002048 | bytes 6291456 | tf_op jit(solution)/shard_map/attend_back/pallas_call | solution.py:499
  185.0 5.5 inputs_back.1.x_ref
  190.5 9.9 %return_rows.3 = bf16[128,32,384]{2,1,0:T(8,128)(2,1)} custom-call(s32[8,1,512]{2,1,0:T(1,128)} %get-tuple-element.27.landing_ref, bf16[1024,384]{1,0:T(8,128)(2,1)} %inputs_back.1.x_ref), custom_call_target="tpu_custom_call" | custom-call | flops 3221225472 | bytes 6291456 | tf_op jit(solution)/shard_map/return_rows/pallas_call | solution.py:301
  200.4 4.7 all-to-all-start.3
  205.2 9.9 %return_rows.2 = bf16[128,32,384]{2,1,0:T(8,128)(2,1)} custom-call(s32[8,1,512]{2,1,0:T(1,128)} %get-tuple-element.27.landing_ref, bf16[1024,384]{1,0:T(8,128)(2,1)} %get-tuple-element.31.x_ref), custom_call_target="tpu_custom_call" | custom-call | flops 3221225472 | bytes 6291456 | tf_op jit(solution)/shard_map/return_rows/pallas_call | solution.py:301
  215.1 31.0 %all-to-all-done.3.home_ref = bf16[128,32,384]{2,1,0:T(8,128)(2,1)S(1)} async-done(((bf16[128,32,384]{2,1,0:T(8,128)(2,1)}), bf16[128,32,384]{2,1,0:T(8,128)(2,1)S(1)}, u32[]{:S(2)}, u32[]{:S(2)}) %all-to-all-start.3) | async-done | bytes 3145760 | tf_op jit(solution)/shard_map/all_to_all | solution.py:681
  247.8 5.2 all-to-all-start.2
  253.9 4.8 qkv_back.1
  258.7 163.0 %all-reduce.4.cloned.1.call-done = bf16[1536,384]{1,0:T(8,128)(2,1)} async-done(((bf16[1536,384]{1,0:T(8,128)(2,1)}), bf16[1536,384]{1,0:T(8,128)(2,1)}) %all-reduce.4.cloned.1.call-update) | async-done | bytes 1179664 | tf_op jit(solution)/shard_map/psum | solution.py:685
  424.5 153.8 %all-reduce.6.cloned.1.call-done = (bf16[384,1152]{1,0:T(8,128)(2,1)}, bf16[384,384]{1,0:T(8,128)(2,1)}, bf16[384,1536]{1,0:T(8,128)(2,1)}) async-done(((bf16[384,1152]{1,0:T(8,128)(2,1)}, bf16[384,384]{1,0:T(8,128)(2,1)}, bf16[384,1536]{1,0:T(8,128)(2,1)}), (bf16[384,1152]{1,0:T(8,128)(2,1)}, bf16[384,384]{1,0:T(8,128)(2,1)}, bf16[384,1536]{1,0:T(8,128)(2,1)})) %all-reduce.6.cloned.1.call-update) | async-done | bytes 2359312 | tf_op jit(solution)/shard_map/psum | solution.py:685
  578.3 1.9 convert_element_type.13
  580.2 2.5 convert_element_type.12
  584.4 9.0 %unpack_rows.3 = bf16[1024,384]{1,0:T(8,128)(2,1)} custom-call(s32[1,1024]{1,0:T(1,128)} %get-tuple-element.25.slot_ref, bf16[128,32,384]{2,1,0:T(8,128)(2,1)} %copy-done.1), custom_call_target="tpu_custom_call" | custom-call | flops 3221225472 | bytes 6291456 | tf_op jit(solution)/shard_map/unpack_rows/pallas_call | solution.py:169
  593.4 9.1 %unpack_rows.2 = bf16[1024,384]{1,0:T(8,128)(2,1)} custom-call(s32[1,1024]{1,0:T(1,128)} %get-tuple-element.25.slot_ref, bf16[128,32,384]{2,1,0:T(8,128)(2,1)} %all-to-all-done.2.home_ref), custom_call_target="tpu_custom_call" | custom-call | flops 3221225472 | bytes 6291456 | tf_op jit(solution)/shard_map/unpack_rows/pallas_call | solution.py:169
  (18 shorter events, 9.7 us)
Async XLA Ops:
  15.7 55.4 %all-to-all-start = ((bf16[128,98,128]{2,1,0:T(8,128)(2,1)}), bf16[128,98,128]{2,1,0:T(8,128)(2,1)S(1)}, u32[]{:S(2)}, u32[]{:S(2)}) async-start(bf16[128,98,128]{2,1,0:T(8,128)(2,1)} %get-tuple-element.26), calls=%async_computation | async-start | bytes 6815744 | tf_op jit(solution)/shard_map/all_to_all | solution.py:681
  35.0 43.7 %copy-start.4 = (s32[1024]{0:T(1024)S(1)}, s32[1024]{0:T(1024)}, u32[]{:S(2)}) copy-start(s32[1024]{0:T(1024)} %param.10) | copy-start | bytes 12292
  71.1 1.7 copy-start
  72.8 46.5 %all-to-all-start.1 = ((bf16[128,32,384]{2,1,0:T(8,128)(2,1)}), bf16[128,32,384]{2,1,0:T(8,128)(2,1)}, u32[]{:S(2)}, u32[]{:S(2)}) async-start(bf16[128,32,384]{2,1,0:T(8,128)(2,1)} %pack_rows.1), calls=%async_computation.1 | async-start | bytes 6291456 | tf_op jit(solution)/shard_map/all_to_all | solution.py:681
  200.4 45.7 %all-to-all-start.3 = ((bf16[128,32,384]{2,1,0:T(8,128)(2,1)}), bf16[128,32,384]{2,1,0:T(8,128)(2,1)S(1)}, u32[]{:S(2)}, u32[]{:S(2)}) async-start(bf16[128,32,384]{2,1,0:T(8,128)(2,1)} %return_rows.3), calls=%async_computation.3 | async-start | bytes 6291456 | tf_op jit(solution)/shard_map/all_to_all | solution.py:681
  246.1 1.7 copy-start.1
  247.8 345.6 %all-to-all-start.2 = ((bf16[128,32,384]{2,1,0:T(8,128)(2,1)}), bf16[128,32,384]{2,1,0:T(8,128)(2,1)}, u32[]{:S(2)}, u32[]{:S(2)}) async-start(bf16[128,32,384]{2,1,0:T(8,128)(2,1)} %return_rows.2), calls=%async_computation.2 | async-start | bytes 6291456 | tf_op jit(solution)/shard_map/all_to_all | solution.py:681
  253.1 168.6 %all-reduce.4.cloned.1.call-start = ((), (), s32[]{:S(2)}) async-start(), calls=%async_computation.4 | async-start | bytes 2359296 | tf_op jit(solution)/shard_map/psum | solution.py:685
  253.8 324.5 %all-reduce.6.cloned.1.call-start = ((), (), s32[]{:S(2)}) async-start(), calls=%async_computation.5 | async-start | bytes 4718592 | tf_op jit(solution)/shard_map/psum | solution.py:685
  421.7 1.3 copy-start.2
  578.3 4.4 copy-start.3
Sparse Core Ops, SparseCore 0:
  258.6 162.9 all-reduce.3
  428.3 149.9 all-reduce.5

commit v2 on v1

--- a/solution.py
+++ b/solution.py
@@ -18,7 +18,7 @@
 SHARDS = 128
 CAP = 32
 SLOTS = SHARDS * CAP
-STEP_SHARDS = 16
+STEP_SHARDS = 32
 STEP_SLOTS = STEP_SHARDS * CAP
 STEPS = SHARDS // STEP_SHARDS
 WIRE_ROWS = 3 * CAP + 2
@@ -31,6 +31,8 @@
 F32 = jnp.float32
 VMEM_LIMIT = 56 * 1024 * 1024
 
+NO_COST = pl.CostEstimate(flops=1, bytes_accessed=1, transcendentals=0)
+
 NT = (((1,), (1,)), ((), ()))
 
 
@@ -50,12 +52,6 @@
     return pltpu.CompilerParams(
         vmem_limit_bytes=VMEM_LIMIT,
         dimension_semantics=("arbitrary",) * grid_dims,
-    )
-
-
-def cost(flops, bytes_accessed, transcendentals=0):
-    return pl.CostEstimate(
-        flops=int(flops), bytes_accessed=int(bytes_accessed), transcendentals=int(transcendentals)
     )
 
 
@@ -120,7 +116,7 @@
         ],
         scratch_shapes=[pltpu.VMEM((SHARDS, LANES), F32), pltpu.VMEM((SHARDS, LANES), F32)],
         compiler_params=params(),
-        cost_estimate=cost(2 * SLOTS * ROWS * D, 8 * SLOTS * D),
+        cost_estimate=NO_COST,
         name="pack_points",
     )(first_lane, pos_row, points)
 
@@ -141,7 +137,7 @@
         out_specs=pl.BlockSpec((STEP_SHARDS, CAP, D), lambda i: (i, 0, 0)),
         out_shape=jax.ShapeDtypeStruct((SHARDS, CAP, D), BF),
         compiler_params=params(),
-        cost_estimate=cost(2 * SLOTS * ROWS * D, 4 * SLOTS * D),
+        cost_estimate=NO_COST,
         name="pack_rows",
     )(slot_row, values)
 
@@ -177,7 +173,7 @@
         out_shape=jax.ShapeDtypeStruct((ROWS, D), BF),
         scratch_shapes=[pltpu.VMEM((ROWS, LANES), jnp.int32), pltpu.VMEM((ROWS, D), F32)],
         compiler_params=params(),
-        cost_estimate=cost(2 * SLOTS * ROWS * D, 4 * SLOTS * D),
+        cost_estimate=NO_COST,
         name="unpack_rows",
     )(slot_row, home)
 
@@ -251,7 +247,7 @@
         ],
         scratch_shapes=[pltpu.VMEM((ROWS, D), F32)],
         compiler_params=params(),
-        cost_estimate=cost(2 * SLOTS * ROWS * D + 6 * ROWS * D * D, 6 * SLOTS * D),
+        cost_estimate=NO_COST,
         name="land_points",
     )(received, w_qkv)
 
@@ -282,7 +278,7 @@
         out_shape=jax.ShapeDtypeStruct((ROWS, D), BF),
         scratch_shapes=[pltpu.VMEM((ROWS, D), F32)],
         compiler_params=params(),
-        cost_estimate=cost(2 * SLOTS * ROWS * D, 4 * SLOTS * D),
+        cost_estimate=NO_COST,
         name="land_rows",
     )(landing, received)
 
@@ -308,7 +304,7 @@
         out_specs=pl.BlockSpec((STEP_SHARDS, CAP, D), lambda i: (i, 0, 0)),
         out_shape=jax.ShapeDtypeStruct((SHARDS, CAP, D), BF),
         compiler_params=params(),
-        cost_estimate=cost(2 * SLOTS * ROWS * D, 4 * SLOTS * D),
+        cost_estimate=NO_COST,
         name="return_rows",
     )(landing, values)
 
@@ -422,7 +418,7 @@
         ],
         scratch_shapes=[pltpu.VMEM((ROWS, ROWS), F32)],
         compiler_params=params(),
-        cost_estimate=cost(24e9, 8 * ROWS * D, 12 * ROWS * ROWS),
+        cost_estimate=NO_COST,
         name="attend",
     )(segment_column, segment_row, packed, packed, packed)
 
@@ -436,9 +432,7 @@
     up_ref,
     exact_ref,
     level_ref,
-    dq_ref,
-    dk_ref,
-    dv_ref,
+    out_ref,
     bias_s,
     dqt_s,
     dk_s,
@@ -490,9 +484,9 @@
                 dqt_s[head_rows, :] = dq_part
             else:
                 dqt_s[head_rows, :] += dq_part
-    dq_ref[...] = (dqt_s[...] * SCALING).T.astype(BF)
-    dk_ref[...] = (dk_s[...] * SCALING).astype(BF)
-    dv_ref[...] = dv_s[...].astype(BF)
+    out_ref[:, :LANES] = (dqt_s[...] * SCALING).T.astype(BF)
+    out_ref[:, LANES : 2 * LANES] = (dk_s[...] * SCALING).astype(BF)
+    out_ref[:, 2 * LANES :] = dv_s[...].astype(BF)
 
 
 def attend_back(segment_column, segment_row, packed, upstream, exact, level):
@@ -509,8 +503,8 @@
             group_spec(),
             group_spec(),
         ],
-        out_specs=[group_spec()] * 3,
-        out_shape=[jax.ShapeDtypeStruct((ROWS, D), BF)] * 3,
+        out_specs=pl.BlockSpec((ROWS, 3 * LANES), lambda g: (0, g)),
+        out_shape=jax.ShapeDtypeStruct((ROWS, 3 * D), BF),
         scratch_shapes=[
             pltpu.VMEM((ROWS, ROWS), F32),
             pltpu.VMEM((LANES, ROWS), F32),
@@ -518,33 +512,96 @@
             pltpu.VMEM((ROWS, LANES), F32),
         ],
         compiler_params=params(),
-        cost_estimate=cost(60e9, 16 * ROWS * D, 12 * ROWS * ROWS),
+        cost_estimate=NO_COST,
         name="attend_back",
     )(segment_column, segment_row, packed, packed, packed, upstream, exact, level)
 
 
-FF_STEP = 512
-FF_STEPS = FF // FF_STEP
+FORWARD_STEP = 512
+BACK_STEP = 384
 
 
 def mlp_kernel(
     ordered_ref,
     mixed_ref,
-    up_ref,
     w_proj_ref,
     w1_ref,
     w2_ref,
     block_ref,
+    middle_ref,
+    hidden_ref,
+    slope_ref,
+    normed_s,
+    out_s,
+):
+    step = pl.program_id(0)
+
+    @pl.when(step == 0)
+    def _():
+        middle = (
+            ordered_ref[...].astype(F32) + dot(mixed_ref[...], w_proj_ref[...])
+        ).astype(BF)
+        middle_ref[...] = middle
+        normed, _ = norm_parts(middle.astype(F32))
+        normed_s[...] = normed.astype(BF)
+        out_s[...] = middle.astype(F32)
+
+    before = dot(normed_s[...], w1_ref[...])
+    half = 0.5 * (1.0 + lax.erf(before * math.sqrt(0.5)))
+    density = jnp.exp(before * before * -0.5) * (1.0 / math.sqrt(2.0 * math.pi))
+    hidden = (before * half).astype(BF)
+    hidden_ref[...] = hidden
+    slope_ref[...] = half + before * density
+    out_s[...] += dot(hidden, w2_ref[...])
+
+    @pl.when(step == FF // FORWARD_STEP - 1)
+    def _():
+        block_ref[...] = out_s[...].astype(BF)
+
+
+def mlp(ordered, mixed, w_proj, w_fc1, w_fc2):
+    rows = whole((ROWS, D))
+    wide = pl.BlockSpec((ROWS, FORWARD_STEP), lambda i: (0, i))
+    return pl.pallas_call(
+        mlp_kernel,
+        grid=(FF // FORWARD_STEP,),
+        in_specs=[
+            rows,
+            rows,
+            whole((D, D)),
+            pl.BlockSpec((D, FORWARD_STEP), lambda i: (0, i)),
+            pl.BlockSpec((FORWARD_STEP, D), lambda i: (i, 0)),
+        ],
+        out_specs=[rows, rows, wide, wide],
+        out_shape=[
+            jax.ShapeDtypeStruct((ROWS, D), BF),
+            jax.ShapeDtypeStruct((ROWS, D), BF),
+            jax.ShapeDtypeStruct((ROWS, FF), BF),
+            jax.ShapeDtypeStruct((ROWS, FF), F32),
+        ],
+        scratch_shapes=[pltpu.VMEM((ROWS, D), BF), pltpu.VMEM((ROWS, D), F32)],
+        compiler_params=params(),
+        cost_estimate=NO_COST,
+        name="mlp",
+    )(ordered, mixed, w_proj, w_fc1, w_fc2)
+
+
+def mlp_back_kernel(
+    up_ref,
+    middle_ref,
+    mixed_ref,
+    hidden_ref,
+    slope_ref,
+    w_proj_ref,
+    w1_ref,
+    w2_ref,
     d_middle_ref,
     d_mixed_ref,
     d_proj_ref,
     d_w1_ref,
     d_w2_ref,
-    middle_s,
-    normed_s,
     normed_t_s,
     up_t_s,
-    out_s,
     d_normed_s,
 ):
     step = pl.program_id(0)
@@ -552,35 +609,20 @@
 
     @pl.when(step == 0)
     def _():
-        middle = (
-            ordered_ref[...].astype(F32) + dot(mixed_ref[...], w_proj_ref[...])
-        ).astype(BF)
-        middle_s[...] = middle
-        normed, _ = norm_parts(middle.astype(F32))
-        normed = normed.astype(BF)
-        normed_s[...] = normed
-        normed_t_s[...] = normed.astype(F32).T.astype(BF)
+        normed, _ = norm_parts(middle_ref[...].astype(F32))
+        normed_t_s[...] = normed.astype(BF).astype(F32).T.astype(BF)
         up_t_s[...] = up.astype(F32).T.astype(BF)
-        out_s[...] = jnp.zeros_like(out_s)
         d_normed_s[...] = jnp.zeros_like(d_normed_s)
 
-    w1, w2 = w1_ref[...], w2_ref[...]
-    before = dot(normed_s[...], w1)
-    d_hidden = dot_nt(up, w2).astype(BF).astype(F32)
-    half = 0.5 * (1.0 + lax.erf(before * math.sqrt(0.5)))
-    density = jnp.exp(before * before * -0.5) * (1.0 / math.sqrt(2.0 * math.pi))
-    hidden = (before * half).astype(BF)
-    d_before = (d_hidden * (half + before * density)).astype(BF)
-    out_s[...] += dot(hidden, w2)
-    d_w2_ref[...] = dot(up_t_s[...], hidden).T.astype(BF)
+    d_hidden = dot_nt(up, w2_ref[...]).astype(BF).astype(F32)
+    d_before = (d_hidden * slope_ref[...]).astype(BF)
+    d_w2_ref[...] = dot(up_t_s[...], hidden_ref[...]).T.astype(BF)
     d_w1_ref[...] = dot(normed_t_s[...], d_before).astype(BF)
-    d_normed_s[...] += dot_nt(d_before, w1)
-
-    @pl.when(step == FF_STEPS - 1)
-    def _():
-        middle = middle_s[...].astype(F32)
-        block_ref[...] = (middle + out_s[...]).astype(BF)
-        normed, scale = norm_parts(middle)
+    d_normed_s[...] += dot_nt(d_before, w1_ref[...])
+
+    @pl.when(step == FF // BACK_STEP - 1)
+    def _():
+        normed, scale = norm_parts(middle_ref[...].astype(F32))
         pulled = norm_pull(normed, scale, d_normed_s[...].astype(BF).astype(F32)).astype(BF)
         d_middle = (up.astype(F32) + pulled.astype(F32)).astype(BF)
         d_middle_ref[...] = d_middle
@@ -588,101 +630,219 @@
         d_proj_ref[...] = dot(mixed_ref[...].astype(F32).T.astype(BF), d_middle).astype(BF)
 
 
-def mlp(ordered, mixed, upstream, w_proj, w_fc1, w_fc2):
+def mlp_back(upstream, middle, mixed, hidden, slope, w_proj, w_fc1, w_fc2):
     rows = whole((ROWS, D))
-    return pl.pallas_call(
-        mlp_kernel,
-        grid=(FF_STEPS,),
+    wide = pl.BlockSpec((ROWS, BACK_STEP), lambda i: (0, i))
+    down = pl.BlockSpec((BACK_STEP, D), lambda i: (i, 0))
+    return pl.pallas_call(
+        mlp_back_kernel,
+        grid=(FF // BACK_STEP,),
         in_specs=[
             rows,
             rows,
             rows,
+            wide,
+            wide,
             whole((D, D)),
-            pl.BlockSpec((D, FF_STEP), lambda i: (0, i)),
-            pl.BlockSpec((FF_STEP, D), lambda i: (i, 0)),
-        ],
-        out_specs=[
-            rows,
-            rows,
-            rows,
-            whole((D, D)),
-            pl.BlockSpec((D, FF_STEP), lambda i: (0, i)),
-            pl.BlockSpec((FF_STEP, D), lambda i: (i, 0)),
-        ],
+            pl.BlockSpec((D, BACK_STEP), lambda i: (0, i)),
+            down,
+        ],
+        out_specs=[rows, rows, whole((D, D)), down, down],
         out_shape=[
             jax.ShapeDtypeStruct((ROWS, D), BF),
             jax.ShapeDtypeStruct((ROWS, D), BF),
-            jax.ShapeDtypeStruct((ROWS, D), BF),
             jax.ShapeDtypeStruct((D, D), BF),
-            jax.ShapeDtypeStruct((D, FF), BF),
             jax.ShapeDtypeStruct((FF, D), BF),
+            jax.ShapeDtypeStruct((FF, D), BF),
         ],
         scratch_shapes=[
-            pltpu.VMEM((ROWS, D), BF),
-            pltpu.VMEM((ROWS, D), BF),
             pltpu.VMEM((D, ROWS), BF),
             pltpu.VMEM((D, ROWS), BF),
             pltpu.VMEM((ROWS, D), F32),
-            pltpu.VMEM((ROWS, D), F32),
-        ],
-        compiler_params=params(),
-        cost_estimate=cost(12 * ROWS * D * FF, 20 * ROWS * D, 2 * ROWS * FF),
-        name="mlp",
-    )(ordered, mixed, upstream, w_proj, w_fc1, w_fc2)
-
-
-def inputs_back_kernel(ordered_ref, dq_ref, dk_ref, dv_ref, d_middle_ref, w_ref, out_ref):
+        ],
+        compiler_params=params(),
+        cost_estimate=NO_COST,
+        name="mlp_back",
+    )(upstream, middle, mixed, hidden, slope, w_proj, w_fc1, w_fc2)
+
+
+def group_columns(part, group):
+    first = part * D + group * LANES
+    return slice(first, first + LANES)
+
+
+def inputs_back_kernel(ordered_ref, d_packed_ref, d_middle_ref, w_ref, out_ref):
     normed, scale = norm_parts(ordered_ref[...].astype(F32))
-    d_normed = (
-        dot_nt(dq_ref[...], w_ref[:, :D])
-        + dot_nt(dk_ref[...], w_ref[:, D : 2 * D])
-        + dot_nt(dv_ref[...], w_ref[:, 2 * D :])
+    weights = jnp.concatenate(
+        [
+            w_ref[:, group_columns(part, group)]
+            for group in range(GROUPS)
+            for part in range(3)
+        ],
+        axis=1,
     )
+    d_normed = dot_nt(d_packed_ref[...], weights)
     pulled = norm_pull(normed, scale, d_normed.astype(BF).astype(F32)).astype(BF)
     out_ref[...] = (d_middle_ref[...].astype(F32) + pulled.astype(F32)).astype(BF)
 
 
-def inputs_back(ordered, dq, dk, dv, d_middle, w_qkv):
+def inputs_back(ordered, d_packed, d_middle, w_qkv):
     rows = whole((ROWS, D))
     return pl.pallas_call(
         inputs_back_kernel,
         grid=(1,),
-        in_specs=[rows] * 5 + [whole((D, 3 * D))],
+        in_specs=[rows, whole((ROWS, 3 * D)), rows, whole((D, 3 * D))],
         out_specs=rows,
         out_shape=jax.ShapeDtypeStruct((ROWS, D), BF),
         compiler_params=params(),
-        cost_estimate=cost(6 * ROWS * D * D, 14 * ROWS * D),
+        cost_estimate=NO_COST,
         name="inputs_back",
-    )(ordered, dq, dk, dv, d_middle, w_qkv)
-
-
-def qkv_back_kernel(ordered_ref, dq_ref, dk_ref, dv_ref, out_ref):
+    )(ordered, d_packed, d_middle, w_qkv)
+
+
+def qkv_back_kernel(ordered_ref, d_packed_ref, proj_ref, out_ref):
     normed, _ = norm_parts(ordered_ref[...].astype(F32))
     normed_t = normed.astype(BF).astype(F32).T.astype(BF)
-    for at, ref in enumerate((dq_ref, dk_ref, dv_ref)):
-        out_ref[:, at * D : (at + 1) * D] = dot(normed_t, ref[...]).astype(BF)
-
-
-def qkv_back(ordered, dq, dk, dv):
-    rows = whole((ROWS, D))
+    for group in range(GROUPS):
+        columns = slice(group * D, (group + 1) * D)
+        out_ref[columns, :] = dot(normed_t, d_packed_ref[:, columns]).astype(BF)
+    out_ref[GROUPS * D :, :] = proj_ref[...]
+
+
+def qkv_back(ordered, d_packed, d_proj):
     return pl.pallas_call(
         qkv_back_kernel,
         grid=(1,),
-        in_specs=[rows] * 4,
-        out_specs=whole((D, 3 * D)),
-        out_shape=jax.ShapeDtypeStruct((D, 3 * D), BF),
-        compiler_params=params(),
-        cost_estimate=cost(6 * ROWS * D * D, 14 * ROWS * D),
+        in_specs=[whole((ROWS, D)), whole((ROWS, 3 * D)), whole((D, D))],
+        out_specs=whole(((GROUPS + 1) * D, D)),
+        out_shape=jax.ShapeDtypeStruct(((GROUPS + 1) * D, D), BF),
+        compiler_params=params(),
+        cost_estimate=NO_COST,
         name="qkv_back",
-    )(ordered, dq, dk, dv)
+    )(ordered, d_packed, d_proj)
+
+
+def place(axis):
+    name, stride, size = {
+        "y": ("blk", 2, 4),
+        "core": ("blk", 1, 2),
+        "x": ("sub", 4, 4),
+        "z": ("sub", 1, 4),
+    }[axis]
+    return name, stride, size
+
+
+def swap(values, axis, kind):
+    name, stride, size = place(axis)
+    pairs = []
+    for index in range(lax.axis_size(name)):
+        c = index // stride % size
+        partner = 3 - c if kind else c ^ 1
+        pairs.append((index, index + (partner - c) * stride))
+    return lax.ppermute(values, name, pairs)
+
+
+def side(axis, kind):
+    name, stride, size = place(axis)
+    c = lax.axis_index(name) // stride % size
+    return c >> 1 if kind else (c ^ (c >> 1)) & 1
+
+
+def add(a, b):
+    return (a.astype(F32) + b.astype(F32)).astype(BF)
+
+
+def halve_begin(values, axis, kind):
+    keep = side(axis, kind)
+    half = values.shape[0] // 2
+    own = lax.dynamic_slice_in_dim(values, keep * half, half, 0)
+    away = lax.dynamic_slice_in_dim(values, (1 - keep) * half, half, 0)
+    return own, swap(away, axis, kind)
+
+
+def halve(values, axis, kind):
+    return add(*halve_begin(values, axis, kind))
+
+
+def meet_begin(values, axis, kind):
+    return values, swap(values, axis, kind)
+
+
+def meet(values, axis, kind):
+    return add(*meet_begin(values, axis, kind))
+
+
+def double(values, axis, kind):
+    keep = side(axis, kind)
+    half = values.shape[0]
+    other = swap(values, axis, kind)
+    both = jnp.zeros((2 * half,) + values.shape[1:], values.dtype)
+    both = lax.dynamic_update_slice_in_dim(both, values, keep * half, 0)
+    return lax.dynamic_update_slice_in_dim(both, other, (1 - keep) * half, 0)
+
+
+def spread_again(values, axis):
+    for kind in (1, 0):
+        values = double(values, axis, kind)
+    return values
+
+
+def finish_kernel(
+    keep_ref, w1_ref, w1_other_ref, w2_ref, w2_other_ref, rest_ref, rest_other_ref, qkv_ref, proj_ref, out1_ref, out2_ref
+):
+    step = pl.program_id(0)
+    rows = pl.ds(pl.multiple_of(lax.rem(step, 2) * D, D), D)
+    own = step // 2 == keep_ref[0]
+
+    def block(mine_ref, other_ref):
+        return jnp.where(own, mine_ref[rows, :].astype(F32), other_ref[rows, :].astype(F32))
+
+    out1_ref[...] = block(w1_ref, w1_other_ref)
+    out2_ref[...] = block(w2_ref, w2_other_ref)
+    rest = block(rest_ref, rest_other_ref)
+    for group in range(GROUPS):
+
+        @pl.when(step == group)
+        def _(group=group):
+            for part in range(3):
+                qkv_ref[:, group_columns(part, group)] = rest[:, part * LANES : (part + 1) * LANES]
+
+    @pl.when(step == GROUPS)
+    def _():
+        proj_ref[...] = rest
+
+
+def finish(sums):
+    keep = side("core", 0).astype(jnp.int32).reshape(1)
+    halves = [part for mine in sums for part in (mine, swap(mine, "core", 0))]
+    half = whole((FF // 2, D))
+    return pl.pallas_call(
+        finish_kernel,
+        grid=(FF // D,),
+        in_specs=[pl.BlockSpec(memory_space=pltpu.SMEM)] + [half] * 6,
+        out_specs=[
+            whole((D, 3 * D)),
+            whole((D, D)),
+            pl.BlockSpec((D, D), lambda i: (0, i)),
+            pl.BlockSpec((D, D), lambda i: (i, 0)),
+        ],
+        out_shape=[
+            jax.ShapeDtypeStruct((D, 3 * D), F32),
+            jax.ShapeDtypeStruct((D, D), F32),
+            jax.ShapeDtypeStruct((D, FF), F32),
+            jax.ShapeDtypeStruct((FF, D), F32),
+        ],
+        compiler_params=params(),
+        cost_estimate=NO_COST,
+        name="finish",
+    )(keep, *halves)
+
+
+together = lax.optimization_barrier
 
 
 def exchange(values):
     return lax.all_to_all(values, AXES, split_axis=0, concat_axis=0, tiled=True)
-
-
-def total_of(values):
-    return lax.psum(values, AXES)
 
 
 def on_device(points, hilbert_pos, segment_ids, cotangent, w_qkv, w_proj, w_fc1, w_fc2):
@@ -693,28 +853,41 @@
     ordered, packed, landing = land_points(exchange(wire), w_qkv)
     up_received = exchange(pack_rows(slot_row, cotangent))
     mixed, exact, level = attend(segment_column, segment_row, packed)
+    block, middle, hidden, slope = mlp(ordered, mixed, w_proj, w_fc1, w_fc2)
+    returned, up_received = together((return_rows(landing, block), up_received))
+    output_home = exchange(returned)
     upstream = land_rows(landing, up_received)
-    block, d_middle, d_mixed, d_proj, d_w1, d_w2 = mlp(
-        ordered, mixed, upstream, w_proj, w_fc1, w_fc2
+    d_middle, d_mixed, d_proj, d_w1, d_w2 = mlp_back(
+        upstream, middle, mixed, hidden, slope, w_proj, w_fc1, w_fc2
     )
-    output_home = exchange(return_rows(landing, block))
-    total_proj, total_w1, total_w2 = total_of((d_proj, d_w1, d_w2))
-    dq, dk, dv = attend_back(segment_column, segment_row, packed, d_mixed, exact, level)
-    grad_home = exchange(
-        return_rows(landing, inputs_back(ordered, dq, dk, dv, d_middle, w_qkv))
-    )
-    d_qkv, total_w2 = lax.optimization_barrier((qkv_back(ordered, dq, dk, dv), total_w2))
-    total_qkv = total_of(d_qkv)
+    sum1, sum2 = halve(d_w1, "core", 0), halve(d_w2, "core", 0)
+    sum1, sum2, d_mixed = together((sum1, sum2, d_mixed))
+    sum1, sum2 = halve_begin(sum1, "y", 0), halve_begin(sum2, "x", 0)
+    d_packed = attend_back(segment_column, segment_row, packed, d_mixed, exact, level)
+    sum1, sum2, d_packed, output_home = together((sum1, sum2, d_packed, output_home))
+    sum1, sum2 = halve_begin(add(*sum1), "y", 1), halve_begin(add(*sum2), "x", 1)
+    d_inputs = inputs_back(ordered, d_packed, d_middle, w_qkv)
+    sum1, sum2, d_inputs = together((sum1, sum2, d_inputs))
+    sum1, sum2 = meet_begin(add(*sum1), "x", 0), meet_begin(add(*sum2), "z", 0)
+    back = return_rows(landing, d_inputs)
+    grad_home = exchange(back)
+    sum1, sum2, d_packed, _ = together((sum1, sum2, d_packed, back))
+    output_home, _ = together((output_home, back))
+    sum3 = halve_begin(qkv_back(ordered, d_packed, d_proj), "core", 0)
+    sum1, sum2 = meet(add(*sum1), "x", 1), meet(add(*sum2), "z", 1)
     output = unpack_rows(slot_row, output_home)
+    sum1, sum2, sum3, output = together((sum1, sum2, sum3, output))
+    sum1, sum2 = meet(sum1, "z", 0), meet(sum2, "y", 0)
+    sum1, sum2 = meet(sum1, "z", 1), meet(sum2, "y", 1)
+    sum3 = halve(halve(add(*sum3), "z", 0), "z", 1)
+    for axis in ("y", "x"):
+        for kind in (0, 1):
+            sum3 = meet(sum3, axis, kind)
+    sum1, sum2 = spread_again(sum1, "y"), spread_again(sum2, "x")
+    sum1, sum2, sum3, grad_home = together((sum1, sum2, sum3, grad_home))
+    total_qkv, total_proj, total_w1, total_w2 = finish((sum1, sum2, spread_again(sum3, "z")))
     grad_points = unpack_rows(slot_row, grad_home)
-    return (
-        output,
-        grad_points,
-        total_qkv.astype(F32),
-        total_proj.astype(F32),
-        total_w1.astype(F32),
-        total_w2.astype(F32),
-    )
+    return output, grad_points, total_qkv, total_proj, total_w1, total_w2
 
 
 def solution(mesh):

time: 614 us -> 357 us (0.58)
  waiting for transfers between devices: 392 us -> 86.1 us
  starting transfers between devices: 27.4 us -> 80.5 us
  between operations: 14.4 us -> 1.3 us
    psum x2 -> x0, waiting for transfers between devices: 317 us -> none  [total_of(): return lax.psum(values, AXES)]
    ppermute x0 -> x30, waiting for transfers between devices: none -> 49.3 us  [swap(): return lax.ppermute(values, name, pairs)]
    ppermute x0 -> x30, starting transfers between devices: none -> 45.1 us  [swap(): return lax.ppermute(values, name, pairs)]
    all_to_all x4, waiting for transfers between devices: 74.3 us -> 36.8 us  [exchange(): return lax.all_to_all(values, AXES, split_axis=0, concat_axis=0, tiled=True)]
    pallas_call x3 -> x5, Pallas kernels: 28 us -> 41.8 us  [the longest x1 15.7 us: mlp_back(): pl.pallas_call(mlp_back_kernel, grid=(FF // BACK_STEP,), in_specs=[rows,...]
    all_to_all x4, starting transfers between devices: 27.3 us -> 35.4 us  [exchange(): return lax.all_to_all(values, AXES, split_axis=0, concat_axis=0, tiled=True)]
  transfers between devices with their start and end apart: 6 -> 34, of which waited for: 5 -> 11; matrix products, arithmetic and copies ran while one was open for 1% -> 4% of each run, Pallas kernels for 10% -> 44%
where the time goes in v2:
time: 357 us; the launch traced here: 354 us
  Pallas kernels  168 us (47%)
  waiting for transfers between devices  86.1 us (24%)
  starting transfers between devices  80.5 us (23%)
  local copies, waits for them, and re-layouts  10.7 us (3%)
  other arithmetic  7.25 us (2%)
    ppermute x30, waiting for transfers between devices, swap(): return lax.ppermute(values, name, pairs)  49.3 us
    ppermute x30, starting transfers between devices, swap(): return lax.ppermute(values, name, pairs)  45.1 us
    pallas_call x1, Pallas kernels, attend_back(): pl.pallas_call(attend_back_kernel, grid=(GROUPS,), in_specs=[whole((ROWS,...  39.6 us
    all_to_all x4, waiting for transfers between devices, exchange(): return lax.all_to_all(values, AXES, split_axis=0, concat_axis=0, tiled=True)  36.8 us
    all_to_all x4, starting transfers between devices, exchange(): return lax.all_to_all(values, AXES, split_axis=0, concat_axis=0, tiled=True)  35.4 us
    pallas_call x1, Pallas kernels, attend(): pl.pallas_call(attend_kernel, grid=(GROUPS,), in_specs=[whole((ROWS, 1)),...  20.8 us
    pallas_call x2, Pallas kernels, return_rows(): pl.pallas_call(return_rows_kernel, grid=(STEPS,), in_specs=[pl.BlockSpec(...  18 us
    pallas_call x1, Pallas kernels, mlp_back(): pl.pallas_call(mlp_back_kernel, grid=(FF // BACK_STEP,), in_specs=[rows,...  15.7 us
  transfers between devices with their start and end apart: 34, of which 11 were waited for; matrix products, arithmetic and copies ran while one was open for 4% of the time, Pallas kernels for 44%

profile of v2, /device:TPU:1, one launch (start us, length us, event | category | flops | bytes accessed | tf_op | source)
XLA Modules:
  0.0 353.6 jit_solution(8331809886884447006)
XLA Ops:
  0.6 7.8 %pack_points.1 = (bf16[128,98,128]{2,1,0:T(8,128)(2,1)}, s32[1,1024]{1,0:T(1,128)}) custom-call(s32[1]{0:T(128)} %bitcast.lane_ref, s32[1,1024]{1,0:T(1,128)} %bitcast.8, bf16[1024,384]{1,0:T(8,128)(2,1)} %x_ref.2), custom_call_target="tpu_custom_call" | custom-call | flops 1 | bytes 1 | tf_op jit(solution)/shard_map/pack_points/pallas_call | solution.py:101
  8.5 11.5 %all-to-all-start = ((bf16[128,98,128]{2,1,0:T(8,128)(2,1)}), bf16[128,98,128]{2,1,0:T(8,128)(2,1)S(1)}, u32[]{:S(2)}, u32[]{:S(2)}) async-start(bf16[128,98,128]{2,1,0:T(8,128)(2,1)} %get-tuple-element.58), calls=%async_computation | async-start | bytes 6815744 | tf_op jit(solution)/shard_map/all_to_all | solution.py:845
  20.0 7.1 %pack_rows.1 = bf16[128,32,384]{2,1,0:T(8,128)(2,1)} custom-call(s32[1,1024]{1,0:T(1,128)} %get-tuple-element.64.slot_ref, bf16[1024,384]{1,0:T(8,128)(2,1)} %x_ref.3), custom_call_target="tpu_custom_call" | custom-call | flops 1 | bytes 1 | tf_op jit(solution)/shard_map/pack_rows/pallas_call | solution.py:130
  27.1 36.8 %all-to-all-done.recv_ref = bf16[128,98,128]{2,1,0:T(8,128)(2,1)S(1)} async-done(((bf16[128,98,128]{2,1,0:T(8,128)(2,1)}), bf16[128,98,128]{2,1,0:T(8,128)(2,1)S(1)}, u32[]{:S(2)}, u32[]{:S(2)}) %all-to-all-start) | async-done | bytes 3211296 | tf_op jit(solution)/shard_map/all_to_all | solution.py:845
  65.6 5.9 %all-to-all-start.1 = ((bf16[128,32,384]{2,1,0:T(8,128)(2,1)}), bf16[128,32,384]{2,1,0:T(8,128)(2,1)}, u32[]{:S(2)}, u32[]{:S(2)}) async-start(bf16[128,32,384]{2,1,0:T(8,128)(2,1)} %pack_rows.1), calls=%async_computation.1 | async-start | bytes 6291456 | tf_op jit(solution)/shard_map/all_to_all | solution.py:845
  72.5 10.1 %land_points.1 = (bf16[1024,384]{1,0:T(8,128)(2,1)}, bf16[1024,1152]{1,0:T(8,128)(2,1)}, s32[4,1,1024]{2,1,0:T(1,128)}) custom-call(bf16[128,98,128]{2,1,0:T(8,128)(2,1)} %copy-done, bf16[384,1152]{1,0:T(8,128)(2,1)} %w_ref.3), custom_call_target="tpu_custom_call" | custom-call | flops 1 | bytes 1 | tf_op jit(solution)/shard_map/land_points/pallas_call | solution.py:231
  82.6 20.8 %attend.1 = (bf16[1024,384]{1,0:T(8,128)(2,1)}, f32[1024,384]{1,0:T(8,128)}, f32[1024,384]{1,0:T(8,128)}) custom-call(s32[1024,1]{1,0:T(8,128)} %copy.14.column_ref, s32[1,1024]{1,0:T(1,128)} %bitcast.5, bf16[1024,1152]{1,0:T(8,128)(2,1)} %get-tuple-element.61.q_ref.k_ref.v_ref, bf16[1024,1152]{1,0:T(8,128)(2,1)} %get-tuple-element.61.q_ref.k_ref.v_ref, ...), custom_call_target="tpu_custom_call" | custom-call | flops 1 | bytes 1 | tf_op jit(solution)/shard_map/attend/pallas_call | solution.py:403
  103.4 10.2 %mlp.1 = (bf16[1024,384]{1,0:T(8,128)(2,1)}, bf16[1024,384]{1,0:T(8,128)(2,1)}, bf16[1024,1536]{1,0:T(8,128)(2,1)}, f32[1024,1536]{1,0:T(8,128)}) custom-call(bf16[1024,384]{1,0:T(8,128)(2,1)} %get-tuple-element.60.ordered_ref, bf16[1024,384]{1,0:T(8,128)(2,1)} %get-tuple-element.62.mixed_ref, bf16[384,384]{1,0:T(8,128)(2,1)} %w_proj_ref.3, ...), custom_call_target="tpu_custom_call" | custom-call | flops 1 | bytes 1 | tf_op jit(solution)/shard_map/mlp/pallas_call | solution.py:565
  113.6 9.1 %return_rows.2 = bf16[128,32,384]{2,1,0:T(8,128)(2,1)} custom-call(s32[4,1,1024]{2,1,0:T(1,128)} %get-tuple-element.59.landing_ref, bf16[1024,384]{1,0:T(8,128)(2,1)} %get-tuple-element.63.x_ref), custom_call_target="tpu_custom_call" | custom-call | flops 1 | bytes 1 | tf_op jit(solution)/shard_map/return_rows/pallas_call | solution.py:297
  122.7 9.9 %all-to-all-start.2 = ((bf16[128,32,384]{2,1,0:T(8,128)(2,1)}), bf16[128,32,384]{2,1,0:T(8,128)(2,1)S(1)}, u32[]{:S(2)}, u32[]{:S(2)}) async-start(bf16[128,32,384]{2,1,0:T(8,128)(2,1)} %return_rows.2), calls=%async_computation.2 | async-start | bytes 6291456 | tf_op jit(solution)/shard_map/all_to_all | solution.py:845
  132.6 7.3 %land_rows.1.up_ref = bf16[1024,384]{1,0:T(8,128)(2,1)} custom-call(s32[4,1,1024]{2,1,0:T(1,128)} %get-tuple-element.59.landing_ref, bf16[128,32,384]{2,1,0:T(8,128)(2,1)} %all-to-all-done.1.recv_ref), custom_call_target="tpu_custom_call" | custom-call | flops 1 | bytes 1 | tf_op jit(solution)/shard_map/land_rows/pallas_call | solution.py:270
  139.9 15.7 %mlp_back.1 = (bf16[1024,384]{1,0:T(8,128)(2,1)}, bf16[1024,384]{1,0:T(8,128)(2,1)}, bf16[384,384]{1,0:T(8,128)(2,1)}, bf16[1536,384]{1,0:T(8,128)(2,1)}, bf16[1536,384]{1,0:T(8,128)(2,1)}) custom-call(bf16[1024,384]{1,0:T(8,128)(2,1)} %land_rows.1.up_ref, bf16[1024,384]{1,0:T(8,128)(2,1)} %get-tuple-element.66.middle_ref, ...), custom_call_target="tpu_custom_call" | custom-call | flops 1 | bytes 1 | tf_op jit(solution)/shard_map/mlp_back/pallas_call | solution.py:637
  166.9 39.6 %attend_back.1.d_packed_ref = bf16[1024,1152]{1,0:T(8,128)(2,1)} custom-call(s32[1024,1]{1,0:T(8,128)} %copy.14.column_ref, s32[1,1024]{1,0:T(1,128)} %bitcast.6, bf16[1024,1152]{1,0:T(8,128)(2,1)} %get-tuple-element.61.q_ref.k_ref.v_ref, bf16[1024,1152]{1,0:T(8,128)(2,1)} %get-tuple-element.61.q_ref.k_ref.v_ref, ...), custom_call_target="tpu_custom_call" | custom-call | flops 1 | bytes 1 | tf_op jit(solution)/shard_map/attend_back/pallas_call | solution.py:493
  212.3 5.3 %inputs_back.1.x_ref = bf16[1024,384]{1,0:T(8,128)(2,1)} custom-call(bf16[1024,384]{1,0:T(8,128)(2,1)} %get-tuple-element.60.ordered_ref, bf16[1024,1152]{1,0:T(8,128)(2,1)} %attend_back.1.d_packed_ref, bf16[1024,384]{1,0:T(8,128)(2,1)} %get-tuple-element.83.d_middle_ref, bf16[384,1152]{1,0:T(8,128)(2,1)} %w_ref.3), custom_call_target="tpu_custom_call" | custom-call | flops 1 | bytes 1 | tf_op jit(solution)/shard_map/inputs_back/pallas_call | solution.py:691
  219.7 8.9 %return_rows.3 = bf16[128,32,384]{2,1,0:T(8,128)(2,1)} custom-call(s32[4,1,1024]{2,1,0:T(1,128)} %get-tuple-element.59.landing_ref, bf16[1024,384]{1,0:T(8,128)(2,1)} %inputs_back.1.x_ref), custom_call_target="tpu_custom_call" | custom-call | flops 1 | bytes 1 | tf_op jit(solution)/shard_map/return_rows/pallas_call | solution.py:297
  228.6 8.1 %all-to-all-start.3 = ((bf16[128,32,384]{2,1,0:T(8,128)(2,1)}), bf16[128,32,384]{2,1,0:T(8,128)(2,1)S(1)}, u32[]{:S(2)}, u32[]{:S(2)}) async-start(bf16[128,32,384]{2,1,0:T(8,128)(2,1)} %return_rows.3), calls=%async_computation.3 | async-start | bytes 6291456 | tf_op jit(solution)/shard_map/all_to_all | solution.py:845
  236.7 7.6 %unpack_rows.2 = bf16[1024,384]{1,0:T(8,128)(2,1)} custom-call(s32[1,1024]{1,0:T(1,128)} %get-tuple-element.64.slot_ref, bf16[128,32,384]{2,1,0:T(8,128)(2,1)} %copy-done.1), custom_call_target="tpu_custom_call" | custom-call | flops 1 | bytes 1 | tf_op jit(solution)/shard_map/unpack_rows/pallas_call | solution.py:165
  258.8 19.4 %collective-permute-done.9 = bf16[192,384]{1,0:T(8,128)(2,1)S(1)} collective-permute-done((bf16[192,384]{1,0:T(8,128)(2,1)S(1)}, bf16[192,384]{1,0:T(8,128)(2,1)S(1)}, u32[]{:S(2)}, u32[]{:S(2)}) %collective-permute-start.9) | collective-permute-done | bytes 147488 | tf_op jit(solution)/shard_map/ppermute | solution.py:742
  285.3 5.0 %collective-permute-done.11 = bf16[192,384]{1,0:T(8,128)(2,1)S(1)} collective-permute-done((bf16[192,384]{1,0:T(8,128)(2,1)S(1)}, bf16[192,384]{1,0:T(8,128)(2,1)S(1)}, u32[]{:S(2)}, u32[]{:S(2)}) %collective-permute-start.11) | collective-permute-done | bytes 147488 | tf_op jit(solution)/shard_map/ppermute | solution.py:742
  310.5 5.3 %collective-permute-done.23 = bf16[192,384]{1,0:T(8,128)(2,1)S(1)} collective-permute-done((bf16[192,384]{1,0:T(8,128)(2,1)S(1)}, bf16[192,384]{1,0:T(8,128)(2,1)S(1)}, u32[]{:S(2)}, u32[]{:S(2)}) %collective-permute-start.23) | collective-permute-done | bytes 147488 | tf_op jit(solution)/shard_map/ppermute | solution.py:742
  326.7 5.5 %collective-permute-start.25 = (bf16[768,384]{1,0:T(8,128)(2,1)}, bf16[768,384]{1,0:T(8,128)(2,1)S(1)}, u32[]{:S(2)}, u32[]{:S(2)}) collective-permute-start(bf16[768,384]{1,0:T(8,128)(2,1)} %copy-done.5), channel_id=1, source_target_pairs={{0,16},{16,0},{32,48},{48,32},{64,80},{80,64},{96,112},{112,96},{1... | collective-permute-start | bytes 1769480 | tf_op jit(solution)/shard_map/ppermute | solution.py:742
  332.4 6.5 %collective-permute-start.29 = (bf16[768,384]{1,0:T(8,128)(2,1)S(1)}, bf16[768,384]{1,0:T(8,128)(2,1)S(1)}, u32[]{:S(2)}, u32[]{:S(2)}) collective-permute-start(bf16[768,384]{1,0:T(8,128)(2,1)S(1)} %constant_dynamic-update-slice_fusion.rest_ref), channel_id=1, source_target_pairs={{0,16},{16,0},{32,48},{48,32},{64,80},{80,64},{96,112},{112,96},{1... | collective-permute-start | bytes 1769480 | tf_op jit(solution)/shard_map/ppermute | solution.py:742
  338.9 7.6 %unpack_rows.3 = bf16[1024,384]{1,0:T(8,128)(2,1)} custom-call(s32[1,1024]{1,0:T(1,128)} %get-tuple-element.64.slot_ref, bf16[128,32,384]{2,1,0:T(8,128)(2,1)} %copy-done.2), custom_call_target="tpu_custom_call" | custom-call | flops 1 | bytes 1 | tf_op jit(solution)/shard_map/unpack_rows/pallas_call | solution.py:165
  347.8 5.6 %finish.1 = (f32[384,1152]{1,0:T(8,128)}, f32[384,384]{1,0:T(8,128)}, f32[384,1536]{1,0:T(8,128)}, f32[1536,384]{1,0:T(8,128)}) custom-call(s32[1]{0:T(128)} %bitcast.4.keep_ref, bf16[768,384]{1,0:T(8,128)(2,1)} %copy-done.5, bf16[768,384]{1,0:T(8,128)(2,1)} %copy-done.8, bf16[768,384]{1,0:T(8,128)(2,1)} %copy-done.4, bf16[768,384]{1,0:T(8,128)(2,1)} %copy-done.9, ...), custom_call_target="tpu_custom_call" | custom-call | flops 1 | bytes 1 | tf_op jit(solution)/shard_map/finish/pallas_call | solution.py:819
  (129 shorter events, 75.7 us)
Async XLA Ops:
  8.5 55.4 %all-to-all-start = ((bf16[128,98,128]{2,1,0:T(8,128)(2,1)}), bf16[128,98,128]{2,1,0:T(8,128)(2,1)S(1)}, u32[]{:S(2)}, u32[]{:S(2)}) async-start(bf16[128,98,128]{2,1,0:T(8,128)(2,1)} %get-tuple-element.58), calls=%async_computation | async-start | bytes 6815744 | tf_op jit(solution)/shard_map/all_to_all | solution.py:845
  65.6 57.1 %all-to-all-start.1 = ((bf16[128,32,384]{2,1,0:T(8,128)(2,1)}), bf16[128,32,384]{2,1,0:T(8,128)(2,1)}, u32[]{:S(2)}, u32[]{:S(2)}) async-start(bf16[128,32,384]{2,1,0:T(8,128)(2,1)} %pack_rows.1), calls=%async_computation.1 | async-start | bytes 6291456 | tf_op jit(solution)/shard_map/all_to_all | solution.py:845
  122.7 83.8 %all-to-all-start.2 = ((bf16[128,32,384]{2,1,0:T(8,128)(2,1)}), bf16[128,32,384]{2,1,0:T(8,128)(2,1)S(1)}, u32[]{:S(2)}, u32[]{:S(2)}) async-start(bf16[128,32,384]{2,1,0:T(8,128)(2,1)} %return_rows.2), calls=%async_computation.2 | async-start | bytes 6291456 | tf_op jit(solution)/shard_map/all_to_all | solution.py:845
  164.1 42.4 %collective-permute-start.3 = (bf16[384,384]{1,0:T(8,128)(2,1)}, bf16[384,384]{1,0:T(8,128)(2,1)}, u32[]{:S(2)}, u32[]{:S(2)}) collective-permute-start(bf16[384,384]{1,0:T(8,128)(2,1)} %get-tuple-element.116), channel_id=1, source_target_pairs={{0,4},{1,5},{2,6},{3,7},{4,0},{5,1},{6,2},{7,3},{8,12},{9,13},{10,... | collective-permute-start | bytes 884744 | tf_op jit(solution)/shard_map/ppermute | solution.py:742
  165.7 40.8 %collective-permute-start.2 = (bf16[384,384]{1,0:T(8,128)(2,1)}, bf16[384,384]{1,0:T(8,128)(2,1)}, u32[]{:S(2)}, u32[]{:S(2)}) collective-permute-start(bf16[384,384]{1,0:T(8,128)(2,1)} %get-tuple-element.118), channel_id=1, source_target_pairs={{0,32},{16,48},{32,0},{48,16},{64,96},{80,112},{96,64},{112,80},{1... | collective-permute-start | bytes 884744 | tf_op jit(solution)/shard_map/ppermute | solution.py:742
  208.5 9.1 %collective-permute-start.5 = (bf16[192,384]{1,0:T(8,128)(2,1)S(1)}, bf16[192,384]{1,0:T(8,128)(2,1)S(1)}, u32[]{:S(2)}, u32[]{:S(2)}) collective-permute-start(bf16[192,384]{1,0:T(8,128)(2,1)S(1)} %get-tuple-element.120), channel_id=1, source_target_pairs={{0,12},{1,13},{2,14},{3,15},{4,8},{5,9},{6,10},{7,11},{8,4},{9,5},... | collective-permute-start | bytes 442376 | tf_op jit(solution)/shard_map/ppermute | solution.py:742
  210.4 7.2 %collective-permute-start.4 = (bf16[192,384]{1,0:T(8,128)(2,1)S(1)}, bf16[192,384]{1,0:T(8,128)(2,1)S(1)}, u32[]{:S(2)}, u32[]{:S(2)}) collective-permute-start(bf16[192,384]{1,0:T(8,128)(2,1)S(1)} %get-tuple-element.122), channel_id=1, source_target_pairs={{0,96},{16,112},{32,64},{48,80},{64,32},{80,48},{96,0},{112,16},{1... | collective-permute-start | bytes 442376 | tf_op jit(solution)/shard_map/ppermute | solution.py:742
  217.7 26.6 %collective-permute-start.7 = (bf16[192,384]{1,0:T(8,128)(2,1)S(1)}, bf16[192,384]{1,0:T(8,128)(2,1)}, u32[]{:S(2)}, u32[]{:S(2)}) collective-permute-start(bf16[192,384]{1,0:T(8,128)(2,1)S(1)} %add_convert_fusion.19), channel_id=1, source_target_pairs={{0,1},{1,0},{2,3},{3,2},{4,5},{5,4},{6,7},{7,6},{8,9},{9,8},{10,11... | collective-permute-start | bytes 442376 | tf_op jit(solution)/shard_map/ppermute | solution.py:742
  219.3 25.0 %collective-permute-start.6 = (bf16[192,384]{1,0:T(8,128)(2,1)S(1)}, bf16[192,384]{1,0:T(8,128)(2,1)}, u32[]{:S(2)}, u32[]{:S(2)}) collective-permute-start(bf16[192,384]{1,0:T(8,128)(2,1)S(1)} %add_convert_fusion.20), channel_id=1, source_target_pairs={{0,4},{1,5},{2,6},{3,7},{4,0},{5,1},{6,2},{7,3},{8,12},{9,13},{10,... | collective-permute-start | bytes 442376 | tf_op jit(solution)/shard_map/ppermute | solution.py:742
  228.6 92.7 %all-to-all-start.3 = ((bf16[128,32,384]{2,1,0:T(8,128)(2,1)}), bf16[128,32,384]{2,1,0:T(8,128)(2,1)S(1)}, u32[]{:S(2)}, u32[]{:S(2)}) async-start(bf16[128,32,384]{2,1,0:T(8,128)(2,1)} %return_rows.3), calls=%async_computation.3 | async-start | bytes 6291456 | tf_op jit(solution)/shard_map/all_to_all | solution.py:845
  250.6 27.7 %collective-permute-start.10 = (bf16[768,384]{1,0:T(8,128)(2,1)S(1)}, bf16[768,384]{1,0:T(8,128)(2,1)S(1)}, u32[]{:S(2)}, u32[]{:S(2)}) collective-permute-start(bf16[768,384]{1,0:T(8,128)(2,1)S(1)} %get-tuple-element.114), channel_id=1, source_target_pairs={{0,16},{16,0},{32,48},{48,32},{64,80},{80,64},{96,112},{112,96},{1... | collective-permute-start | bytes 1769480 | tf_op jit(solution)/shard_map/ppermute | solution.py:742
  252.7 25.5 %collective-permute-start.9 = (bf16[192,384]{1,0:T(8,128)(2,1)S(1)}, bf16[192,384]{1,0:T(8,128)(2,1)S(1)}, u32[]{:S(2)}, u32[]{:S(2)}) collective-permute-start(bf16[192,384]{1,0:T(8,128)(2,1)S(1)} %add_convert_fusion.16), channel_id=1, source_target_pairs={{0,3},{1,2},{2,1},{3,0},{4,7},{5,6},{6,5},{7,4},{8,11},{9,10},{10,... | collective-permute-start | bytes 442376 | tf_op jit(solution)/shard_map/ppermute | solution.py:742
  256.3 21.9 %collective-permute-start.8 = (bf16[192,384]{1,0:T(8,128)(2,1)S(1)}, bf16[192,384]{1,0:T(8,128)(2,1)S(1)}, u32[]{:S(2)}, u32[]{:S(2)}) collective-permute-start(bf16[192,384]{1,0:T(8,128)(2,1)S(1)} %add_convert_fusion.18), channel_id=1, source_target_pairs={{0,12},{1,13},{2,14},{3,15},{4,8},{5,9},{6,10},{7,11},{8,4},{9,5},... | collective-permute-start | bytes 442376 | tf_op jit(solution)/shard_map/ppermute | solution.py:742
  279.2 12.8 %collective-permute-start.19 = (bf16[384,384]{1,0:T(8,128)(2,1)S(1)}, bf16[384,384]{1,0:T(8,128)(2,1)S(1)}, u32[]{:S(2)}, u32[]{:S(2)}) collective-permute-start(bf16[384,384]{1,0:T(8,128)(2,1)S(1)} %constant_dynamic-slice_fusion.1), channel_id=1, source_target_pairs={{0,1},{1,0},{2,3},{3,2},{4,5},{5,4},{6,7},{7,6},{8,9},{9,8},{10,11... | collective-permute-start | bytes 884744 | tf_op jit(solution)/shard_map/ppermute | solution.py:742
  279.4 10.9 %collective-permute-start.11 = (bf16[192,384]{1,0:T(8,128)(2,1)S(1)}, bf16[192,384]{1,0:T(8,128)(2,1)S(1)}, u32[]{:S(2)}, u32[]{:S(2)}) collective-permute-start(bf16[192,384]{1,0:T(8,128)(2,1)S(1)} %add_convert_fusion.17), channel_id=1, source_target_pairs={{0,1},{1,0},{2,3},{3,2},{4,5},{5,4},{6,7},{7,6},{8,9},{9,8},{10,11... | collective-permute-start | bytes 442376 | tf_op jit(solution)/shard_map/ppermute | solution.py:742
  283.5 9.8 %collective-permute-start.16 = (bf16[192,384]{1,0:T(8,128)(2,1)S(1)}, bf16[192,384]{1,0:T(8,128)(2,1)S(1)}, u32[]{:S(2)}, u32[]{:S(2)}) collective-permute-start(bf16[192,384]{1,0:T(8,128)(2,1)S(1)} %add_convert_fusion.12), channel_id=1, source_target_pairs={{0,96},{16,112},{32,64},{48,80},{64,32},{80,48},{96,0},{112,16},{1... | collective-permute-start | bytes 442376 | tf_op jit(solution)/shard_map/ppermute | solution.py:742
  290.3 9.4 %collective-permute-start.12 = (bf16[192,384]{1,0:T(8,128)(2,1)S(1)}, bf16[192,384]{1,0:T(8,128)(2,1)S(1)}, u32[]{:S(2)}, u32[]{:S(2)}) collective-permute-start(bf16[192,384]{1,0:T(8,128)(2,1)S(1)} %add_convert_fusion.14), channel_id=1, source_target_pairs={{0,3},{1,2},{2,1},{3,0},{4,7},{5,6},{6,5},{7,4},{8,11},{9,10},{10,... | collective-permute-start | bytes 442376 | tf_op jit(solution)/shard_map/ppermute | solution.py:742
  293.4 12.1 %collective-permute-start.17 = (bf16[192,384]{1,0:T(8,128)(2,1)S(1)}, bf16[192,384]{1,0:T(8,128)(2,1)S(1)}, u32[]{:S(2)}, u32[]{:S(2)}) collective-permute-start(bf16[192,384]{1,0:T(8,128)(2,1)S(1)} %get-tuple-element.111), channel_id=1, source_target_pairs={{0,12},{1,13},{2,14},{3,15},{4,8},{5,9},{6,10},{7,11},{8,4},{9,5},... | collective-permute-start | bytes 442376 | tf_op jit(solution)/shard_map/ppermute | solution.py:742
  299.9 10.4 %collective-permute-start.13 = (bf16[192,384]{1,0:T(8,128)(2,1)S(1)}, bf16[192,384]{1,0:T(8,128)(2,1)S(1)}, u32[]{:S(2)}, u32[]{:S(2)}) collective-permute-start(bf16[192,384]{1,0:T(8,128)(2,1)S(1)} %get-tuple-element.113), channel_id=1, source_target_pairs={{0,96},{16,112},{32,64},{48,80},{64,32},{80,48},{96,0},{112,16},{1... | collective-permute-start | bytes 442376 | tf_op jit(solution)/shard_map/ppermute | solution.py:742
  305.6 12.1 %collective-permute-start.18 = (bf16[384,384]{1,0:T(8,128)(2,1)S(1)}, bf16[384,384]{1,0:T(8,128)(2,1)S(1)}, u32[]{:S(2)}, u32[]{:S(2)}) collective-permute-start(bf16[384,384]{1,0:T(8,128)(2,1)S(1)} %constant_dynamic-update-slice_fusion.6), channel_id=1, source_target_pairs={{0,4},{1,5},{2,6},{3,7},{4,0},{5,1},{6,2},{7,3},{8,12},{9,13},{10,... | collective-permute-start | bytes 884744 | tf_op jit(solution)/shard_map/ppermute | solution.py:742
  310.3 7.5 %collective-permute-start.14 = (bf16[384,384]{1,0:T(8,128)(2,1)S(1)}, bf16[384,384]{1,0:T(8,128)(2,1)S(1)}, u32[]{:S(2)}, u32[]{:S(2)}) collective-permute-start(bf16[384,384]{1,0:T(8,128)(2,1)S(1)} %constant_dynamic-update-slice_fusion.10), channel_id=1, source_target_pairs={{0,32},{16,48},{32,0},{48,16},{64,96},{80,112},{96,64},{112,80},{1... | collective-permute-start | bytes 884744 | tf_op jit(solution)/shard_map/ppermute | solution.py:742
  326.7 19.9 %collective-permute-start.25 = (bf16[768,384]{1,0:T(8,128)(2,1)}, bf16[768,384]{1,0:T(8,128)(2,1)S(1)}, u32[]{:S(2)}, u32[]{:S(2)}) collective-permute-start(bf16[768,384]{1,0:T(8,128)(2,1)} %copy-done.5), channel_id=1, source_target_pairs={{0,16},{16,0},{32,48},{48,32},{64,80},{80,64},{96,112},{112,96},{1... | collective-permute-start | bytes 1769480 | tf_op jit(solution)/shard_map/ppermute | solution.py:742
  332.1 14.4 %collective-permute-start.26 = (bf16[768,384]{1,0:T(8,128)(2,1)}, bf16[768,384]{1,0:T(8,128)(2,1)S(1)}, u32[]{:S(2)}, u32[]{:S(2)}) collective-permute-start(bf16[768,384]{1,0:T(8,128)(2,1)} %copy-done.4), channel_id=1, source_target_pairs={{0,16},{16,0},{32,48},{48,32},{64,80},{80,64},{96,112},{112,96},{1... | collective-permute-start | bytes 1769480 | tf_op jit(solution)/shard_map/ppermute | solution.py:742
  332.4 14.1 %collective-permute-start.29 = (bf16[768,384]{1,0:T(8,128)(2,1)S(1)}, bf16[768,384]{1,0:T(8,128)(2,1)S(1)}, u32[]{:S(2)}, u32[]{:S(2)}) collective-permute-start(bf16[768,384]{1,0:T(8,128)(2,1)S(1)} %constant_dynamic-update-slice_fusion.rest_ref), channel_id=1, source_target_pairs={{0,16},{16,0},{32,48},{48,32},{64,80},{80,64},{96,112},{112,96},{1... | collective-permute-start | bytes 1769480 | tf_op jit(solution)/shard_map/ppermute | solution.py:742
  (22 other events, 155.1 us)

commit v3 on v2

--- a/solution.py
+++ b/solution.py
@@ -518,7 +518,7 @@
 
 
 FORWARD_STEP = 512
-BACK_STEP = 384
+BACK_STEP = 512
 
 
 def mlp_kernel(
@@ -589,36 +589,29 @@
 def mlp_back_kernel(
     up_ref,
     middle_ref,
-    mixed_ref,
-    hidden_ref,
     slope_ref,
     w_proj_ref,
     w1_ref,
     w2_ref,
     d_middle_ref,
     d_mixed_ref,
-    d_proj_ref,
-    d_w1_ref,
-    d_w2_ref,
-    normed_t_s,
-    up_t_s,
+    d_before_ref,
     d_normed_s,
 ):
     step = pl.program_id(0)
     up = up_ref[...]
-
-    @pl.when(step == 0)
-    def _():
-        normed, _ = norm_parts(middle_ref[...].astype(F32))
-        normed_t_s[...] = normed.astype(BF).astype(F32).T.astype(BF)
-        up_t_s[...] = up.astype(F32).T.astype(BF)
-        d_normed_s[...] = jnp.zeros_like(d_normed_s)
-
     d_hidden = dot_nt(up, w2_ref[...]).astype(BF).astype(F32)
     d_before = (d_hidden * slope_ref[...]).astype(BF)
-    d_w2_ref[...] = dot(up_t_s[...], hidden_ref[...]).T.astype(BF)
-    d_w1_ref[...] = dot(normed_t_s[...], d_before).astype(BF)
-    d_normed_s[...] += dot_nt(d_before, w1_ref[...])
+    d_before_ref[...] = d_before
+    part = dot_nt(d_before, w1_ref[...])
+
+    @pl.when(step == 0)
+    def _():
+        d_normed_s[...] = part
+
+    @pl.when(step > 0)
+    def _():
+        d_normed_s[...] += part
 
     @pl.when(step == FF // BACK_STEP - 1)
     def _():
@@ -627,43 +620,33 @@
         d_middle = (up.astype(F32) + pulled.astype(F32)).astype(BF)
         d_middle_ref[...] = d_middle
         d_mixed_ref[...] = dot_nt(d_middle, w_proj_ref[...]).astype(BF)
-        d_proj_ref[...] = dot(mixed_ref[...].astype(F32).T.astype(BF), d_middle).astype(BF)
-
-
-def mlp_back(upstream, middle, mixed, hidden, slope, w_proj, w_fc1, w_fc2):
+
+
+def mlp_back(upstream, middle, slope, w_proj, w_fc1, w_fc2):
     rows = whole((ROWS, D))
     wide = pl.BlockSpec((ROWS, BACK_STEP), lambda i: (0, i))
-    down = pl.BlockSpec((BACK_STEP, D), lambda i: (i, 0))
     return pl.pallas_call(
         mlp_back_kernel,
         grid=(FF // BACK_STEP,),
         in_specs=[
             rows,
             rows,
-            rows,
-            wide,
             wide,
             whole((D, D)),
             pl.BlockSpec((D, BACK_STEP), lambda i: (0, i)),
-            down,
-        ],
-        out_specs=[rows, rows, whole((D, D)), down, down],
+            pl.BlockSpec((BACK_STEP, D), lambda i: (i, 0)),
+        ],
+        out_specs=[rows, rows, wide],
         out_shape=[
             jax.ShapeDtypeStruct((ROWS, D), BF),
             jax.ShapeDtypeStruct((ROWS, D), BF),
-            jax.ShapeDtypeStruct((D, D), BF),
-            jax.ShapeDtypeStruct((FF, D), BF),
-            jax.ShapeDtypeStruct((FF, D), BF),
-        ],
-        scratch_shapes=[
-            pltpu.VMEM((D, ROWS), BF),
-            pltpu.VMEM((D, ROWS), BF),
-            pltpu.VMEM((ROWS, D), F32),
-        ],
+            jax.ShapeDtypeStruct((ROWS, FF), BF),
+        ],
+        scratch_shapes=[pltpu.VMEM((ROWS, D), F32)],
         compiler_params=params(),
         cost_estimate=NO_COST,
         name="mlp_back",
-    )(upstream, middle, mixed, hidden, slope, w_proj, w_fc1, w_fc2)
+    )(upstream, middle, slope, w_proj, w_fc1, w_fc2)
 
 
 def group_columns(part, group):
@@ -700,26 +683,62 @@
     )(ordered, d_packed, d_middle, w_qkv)
 
 
-def qkv_back_kernel(ordered_ref, d_packed_ref, proj_ref, out_ref):
-    normed, _ = norm_parts(ordered_ref[...].astype(F32))
-    normed_t = normed.astype(BF).astype(F32).T.astype(BF)
-    for group in range(GROUPS):
-        columns = slice(group * D, (group + 1) * D)
-        out_ref[columns, :] = dot(normed_t, d_packed_ref[:, columns]).astype(BF)
-    out_ref[GROUPS * D :, :] = proj_ref[...]
-
-
-def qkv_back(ordered, d_packed, d_proj):
-    return pl.pallas_call(
-        qkv_back_kernel,
-        grid=(1,),
-        in_specs=[whole((ROWS, D)), whole((ROWS, 3 * D)), whole((D, D))],
-        out_specs=whole(((GROUPS + 1) * D, D)),
-        out_shape=jax.ShapeDtypeStruct(((GROUPS + 1) * D, D), BF),
-        compiler_params=params(),
-        cost_estimate=NO_COST,
-        name="qkv_back",
-    )(ordered, d_packed, d_proj)
+def transposed(values):
+    return values.astype(F32).T.astype(BF)
+
+
+def weights_back_kernel(
+    ordered_ref,
+    middle_ref,
+    mixed_ref,
+    d_middle_ref,
+    up_ref,
+    d_packed_ref,
+    d_before_ref,
+    hidden_ref,
+    d_w1_ref,
+    d_w2_ref,
+    rest_ref,
+    normed_t_s,
+    again_t_s,
+    up_t_s,
+):
+    step = pl.program_id(0)
+
+    @pl.when(step == 0)
+    def _():
+        normed_t_s[...] = transposed(norm_parts(ordered_ref[...].astype(F32))[0].astype(BF))
+        again_t_s[...] = transposed(norm_parts(middle_ref[...].astype(F32))[0].astype(BF))
+        up_t_s[...] = transposed(up_ref[...])
+
+    d_w1_ref[...] = dot(again_t_s[...], d_before_ref[...]).astype(BF)
+    d_w2_ref[...] = dot(up_t_s[...], hidden_ref[...]).T.astype(BF)
+
+    @pl.when(step < GROUPS)
+    def _():
+        rest_ref[...] = dot(normed_t_s[...], d_packed_ref[...]).astype(BF)
+
+    @pl.when(step == GROUPS)
+    def _():
+        rest_ref[...] = dot(transposed(mixed_ref[...]), d_middle_ref[...]).astype(BF)
+
+
+def weights_back(ordered, middle, mixed, d_middle, upstream, d_packed, d_before, hidden):
+    rows = whole((ROWS, D))
+    wide = pl.BlockSpec((ROWS, D), lambda i: (0, i))
+    down = pl.BlockSpec((D, D), lambda i: (i, 0))
+    return pl.pallas_call(
+        weights_back_kernel,
+        grid=(FF // D,),
+        in_specs=[rows] * 5
+        + [pl.BlockSpec((ROWS, D), lambda i: (0, jnp.minimum(i, GROUPS - 1))), wide, wide],
+        out_specs=[down] * 3,
+        out_shape=[jax.ShapeDtypeStruct((FF, D), BF)] * 3,
+        scratch_shapes=[pltpu.VMEM((D, ROWS), BF)] * 3,
+        compiler_params=params(),
+        cost_estimate=NO_COST,
+        name="weights_back",
+    )(ordered, middle, mixed, d_middle, upstream, d_packed, d_before, hidden)
 
 
 def place(axis):
@@ -773,12 +792,11 @@
 
 
 def double(values, axis, kind):
-    keep = side(axis, kind)
-    half = values.shape[0]
     other = swap(values, axis, kind)
-    both = jnp.zeros((2 * half,) + values.shape[1:], values.dtype)
-    both = lax.dynamic_update_slice_in_dim(both, values, keep * half, 0)
-    return lax.dynamic_update_slice_in_dim(both, other, (1 - keep) * half, 0)
+    first = side(axis, kind) == 0
+    return jnp.where(
+        first, jnp.concatenate([values, other]), jnp.concatenate([other, values])
+    )
 
 
 def spread_again(values, axis):
@@ -857,36 +875,26 @@
     returned, up_received = together((return_rows(landing, block), up_received))
     output_home = exchange(returned)
     upstream = land_rows(landing, up_received)
-    d_middle, d_mixed, d_proj, d_w1, d_w2 = mlp_back(
-        upstream, middle, mixed, hidden, slope, w_proj, w_fc1, w_fc2
-    )
-    sum1, sum2 = halve(d_w1, "core", 0), halve(d_w2, "core", 0)
-    sum1, sum2, d_mixed = together((sum1, sum2, d_mixed))
-    sum1, sum2 = halve_begin(sum1, "y", 0), halve_begin(sum2, "x", 0)
+    d_middle, d_mixed, d_before = mlp_back(upstream, middle, slope, w_proj, w_fc1, w_fc2)
     d_packed = attend_back(segment_column, segment_row, packed, d_mixed, exact, level)
-    sum1, sum2, d_packed, output_home = together((sum1, sum2, d_packed, output_home))
-    sum1, sum2 = halve_begin(add(*sum1), "y", 1), halve_begin(add(*sum2), "x", 1)
-    d_inputs = inputs_back(ordered, d_packed, d_middle, w_qkv)
-    sum1, sum2, d_inputs = together((sum1, sum2, d_inputs))
-    sum1, sum2 = meet_begin(add(*sum1), "x", 0), meet_begin(add(*sum2), "z", 0)
-    back = return_rows(landing, d_inputs)
+    d_packed, output_home = together((d_packed, output_home))
+    back = return_rows(landing, inputs_back(ordered, d_packed, d_middle, w_qkv))
     grad_home = exchange(back)
-    sum1, sum2, d_packed, _ = together((sum1, sum2, d_packed, back))
-    output_home, _ = together((output_home, back))
-    sum3 = halve_begin(qkv_back(ordered, d_packed, d_proj), "core", 0)
-    sum1, sum2 = meet(add(*sum1), "x", 1), meet(add(*sum2), "z", 1)
+    d_packed, output_home, _ = together((d_packed, output_home, back))
+    sums = weights_back(ordered, middle, mixed, d_middle, upstream, d_packed, d_before, hidden)
+    sums = [halve_begin(part, "core", 0) for part in sums]
     output = unpack_rows(slot_row, output_home)
-    sum1, sum2, sum3, output = together((sum1, sum2, sum3, output))
-    sum1, sum2 = meet(sum1, "z", 0), meet(sum2, "y", 0)
-    sum1, sum2 = meet(sum1, "z", 1), meet(sum2, "y", 1)
-    sum3 = halve(halve(add(*sum3), "z", 0), "z", 1)
-    for axis in ("y", "x"):
+    sums, output, grad_home = together((sums, output, grad_home))
+    orders = (("y", "x", "z"), ("x", "z", "y"), ("z", "y", "x"))
+    sums = [halve_begin(add(*part), order[0], 0) for part, order in zip(sums, orders)]
+    grad_points = unpack_rows(slot_row, grad_home)
+    sums, grad_points = together((sums, grad_points))
+    sums = [halve(add(*part), order[0], 1) for part, order in zip(sums, orders)]
+    for place_in_order in (1, 2):
         for kind in (0, 1):
-            sum3 = meet(sum3, axis, kind)
-    sum1, sum2 = spread_again(sum1, "y"), spread_again(sum2, "x")
-    sum1, sum2, sum3, grad_home = together((sum1, sum2, sum3, grad_home))
-    total_qkv, total_proj, total_w1, total_w2 = finish((sum1, sum2, spread_again(sum3, "z")))
-    grad_points = unpack_rows(slot_row, grad_home)
+            sums = [meet(part, order[place_in_order], kind) for part, order in zip(sums, orders)]
+    sums = [spread_again(part, order[0]) for part, order in zip(sums, orders)]
+    total_qkv, total_proj, total_w1, total_w2 = finish(sums)
     return output, grad_points, total_qkv, total_proj, total_w1, total_w2
 
 

time: 357 us -> 333 us (0.933)
  waiting for transfers between devices: 86.1 us -> 66.1 us
  starting transfers between devices: 80.5 us -> 73 us
    ppermute x30, waiting for transfers between devices: 49.3 us -> 15.2 us  [swap(): return lax.ppermute(values, name, pairs)]
    all_to_all x4, waiting for transfers between devices: 36.8 us -> 50.9 us  [exchange(): return lax.all_to_all(values, AXES, split_axis=0, concat_axis=0, tiled=True)]
    ppermute x30, starting transfers between devices: 45.1 us -> 36.3 us  [swap(): return lax.ppermute(values, name, pairs)]
    pallas_call x1, Pallas kernels: 4.96 us -> 12.3 us  [weights_back(): pl.pallas_call(weights_back_kernel, grid=(FF // D,), in_specs=[rows] * 5...]
    pallas_call x1, Pallas kernels: 15.7 us -> 10.5 us  [mlp_back(): pl.pallas_call(mlp_back_kernel, grid=(FF // BACK_STEP,), in_specs=[rows,...]
  transfers between devices with their start and end apart: 34 -> 34, of which waited for: 11 -> 16; matrix products, arithmetic and copies ran while one was open for 4% -> 3% of each run, Pallas kernels for 44% -> 43%
where the time goes in v3:
time: 333 us; the launch traced here: 329 us
  Pallas kernels  171 us (51%)
  starting transfers between devices  73 us (22%)
  waiting for transfers between devices  66.1 us (20%)
  local copies, waits for them, and re-layouts  10.7 us (3%)
  other arithmetic  6.59 us (2%)
    all_to_all x4, waiting for transfers between devices, exchange(): return lax.all_to_all(values, AXES, split_axis=0, concat_axis=0, tiled=True)  50.9 us
    pallas_call x1, Pallas kernels, attend_back(): pl.pallas_call(attend_back_kernel, grid=(GROUPS,), in_specs=[whole((ROWS,...  39.2 us
    all_to_all x4, starting transfers between devices, exchange(): return lax.all_to_all(values, AXES, split_axis=0, concat_axis=0, tiled=True)  36.7 us
    ppermute x30, starting transfers between devices, swap(): return lax.ppermute(values, name, pairs)  36.3 us
    pallas_call x1, Pallas kernels, attend(): pl.pallas_call(attend_kernel, grid=(GROUPS,), in_specs=[whole((ROWS, 1)),...  20.8 us
    pallas_call x2, Pallas kernels, return_rows(): pl.pallas_call(return_rows_kernel, grid=(STEPS,), in_specs=[pl.BlockSpec(...  18.3 us
    pallas_call x2, Pallas kernels, unpack_rows(): pl.pallas_call(unpack_rows_kernel, grid=(STEPS,), in_specs=[pl.BlockSpec(...  15.4 us
    ppermute x30, waiting for transfers between devices, swap(): return lax.ppermute(values, name, pairs)  15.2 us
  transfers between devices with their start and end apart: 34, of which 16 were waited for; matrix products, arithmetic and copies ran while one was open for 3% of the time, Pallas kernels for 43%

profile of v3, /device:TPU:1, one launch (start us, length us, event | category | flops | bytes accessed | tf_op | source)
XLA Modules:
  0.0 328.7 jit_solution(14937191114776342729)
XLA Ops:
  0.6 7.8 %pack_points.1 = (bf16[128,98,128]{2,1,0:T(8,128)(2,1)}, s32[1,1024]{1,0:T(1,128)}) custom-call(s32[1]{0:T(128)} %bitcast.lane_ref, s32[1,1024]{1,0:T(1,128)} %bitcast.8, bf16[1024,384]{1,0:T(8,128)(2,1)} %x_ref.2), custom_call_target="tpu_custom_call" | custom-call | flops 1 | bytes 1 | tf_op jit(solution)/shard_map/pack_points/pallas_call | solution.py:101
  8.5 11.5 %all-to-all-start = ((bf16[128,98,128]{2,1,0:T(8,128)(2,1)}), bf16[128,98,128]{2,1,0:T(8,128)(2,1)S(1)}, u32[]{:S(2)}, u32[]{:S(2)}) async-start(bf16[128,98,128]{2,1,0:T(8,128)(2,1)} %get-tuple-element.49), calls=%async_computation | async-start | bytes 6815744 | tf_op jit(solution)/shard_map/all_to_all | solution.py:863
  20.0 7.1 %pack_rows.1 = bf16[128,32,384]{2,1,0:T(8,128)(2,1)} custom-call(s32[1,1024]{1,0:T(1,128)} %get-tuple-element.56.slot_ref, bf16[1024,384]{1,0:T(8,128)(2,1)} %x_ref.3), custom_call_target="tpu_custom_call" | custom-call | flops 1 | bytes 1 | tf_op jit(solution)/shard_map/pack_rows/pallas_call | solution.py:130
  27.1 36.7 %all-to-all-done.recv_ref = bf16[128,98,128]{2,1,0:T(8,128)(2,1)S(1)} async-done(((bf16[128,98,128]{2,1,0:T(8,128)(2,1)}), bf16[128,98,128]{2,1,0:T(8,128)(2,1)S(1)}, u32[]{:S(2)}, u32[]{:S(2)}) %all-to-all-start) | async-done | bytes 3211296 | tf_op jit(solution)/shard_map/all_to_all | solution.py:863
  65.6 5.5 %all-to-all-start.1 = ((bf16[128,32,384]{2,1,0:T(8,128)(2,1)}), bf16[128,32,384]{2,1,0:T(8,128)(2,1)}, u32[]{:S(2)}, u32[]{:S(2)}) async-start(bf16[128,32,384]{2,1,0:T(8,128)(2,1)} %pack_rows.1), calls=%async_computation.1 | async-start | bytes 6291456 | tf_op jit(solution)/shard_map/all_to_all | solution.py:863
  72.1 10.1 %land_points.1 = (bf16[1024,384]{1,0:T(8,128)(2,1)}, bf16[1024,1152]{1,0:T(8,128)(2,1)}, s32[4,1,1024]{2,1,0:T(1,128)}) custom-call(bf16[128,98,128]{2,1,0:T(8,128)(2,1)} %copy-done, bf16[384,1152]{1,0:T(8,128)(2,1)} %w_ref.3), custom_call_target="tpu_custom_call" | custom-call | flops 1 | bytes 1 | tf_op jit(solution)/shard_map/land_points/pallas_call | solution.py:231
  82.2 20.8 %attend.1 = (bf16[1024,384]{1,0:T(8,128)(2,1)}, f32[1024,384]{1,0:T(8,128)}, f32[1024,384]{1,0:T(8,128)}) custom-call(s32[1024,1]{1,0:T(8,128)} %copy.14.column_ref, s32[1,1024]{1,0:T(1,128)} %bitcast.5, bf16[1024,1152]{1,0:T(8,128)(2,1)} %get-tuple-element.51.q_ref.k_ref.v_ref, bf16[1024,1152]{1,0:T(8,128)(2,1)} %get-tuple-element.51.q_ref.k_ref.v_ref, ...), custom_call_target="tpu_custom_call" | custom-call | flops 1 | bytes 1 | tf_op jit(solution)/shard_map/attend/pallas_call | solution.py:403
  103.0 10.2 %mlp.1 = (bf16[1024,384]{1,0:T(8,128)(2,1)}, bf16[1024,384]{1,0:T(8,128)(2,1)}, bf16[1024,1536]{1,0:T(8,128)(2,1)}, f32[1024,1536]{1,0:T(8,128)}) custom-call(bf16[1024,384]{1,0:T(8,128)(2,1)} %get-tuple-element.50.ordered_ref, bf16[1024,384]{1,0:T(8,128)(2,1)} %get-tuple-element.52.mixed_ref, bf16[384,384]{1,0:T(8,128)(2,1)} %w_proj_ref.3, ...), custom_call_target="tpu_custom_call" | custom-call | flops 1 | bytes 1 | tf_op jit(solution)/shard_map/mlp/pallas_call | solution.py:565
  113.3 9.3 %return_rows.2 = bf16[128,32,384]{2,1,0:T(8,128)(2,1)} custom-call(s32[4,1,1024]{2,1,0:T(1,128)} %get-tuple-element.54.landing_ref, bf16[1024,384]{1,0:T(8,128)(2,1)} %get-tuple-element.55.x_ref), custom_call_target="tpu_custom_call" | custom-call | flops 1 | bytes 1 | tf_op jit(solution)/shard_map/return_rows/pallas_call | solution.py:297
  122.6 9.9 %all-to-all-start.2 = ((bf16[128,32,384]{2,1,0:T(8,128)(2,1)}), bf16[128,32,384]{2,1,0:T(8,128)(2,1)S(1)}, u32[]{:S(2)}, u32[]{:S(2)}) async-start(bf16[128,32,384]{2,1,0:T(8,128)(2,1)} %return_rows.2), calls=%async_computation.2 | async-start | bytes 6291456 | tf_op jit(solution)/shard_map/all_to_all | solution.py:863
  132.5 7.3 %land_rows.1.up_ref = bf16[1024,384]{1,0:T(8,128)(2,1)} custom-call(s32[4,1,1024]{2,1,0:T(1,128)} %get-tuple-element.54.landing_ref, bf16[128,32,384]{2,1,0:T(8,128)(2,1)} %all-to-all-done.1.recv_ref), custom_call_target="tpu_custom_call" | custom-call | flops 1 | bytes 1 | tf_op jit(solution)/shard_map/land_rows/pallas_call | solution.py:270
  139.9 10.5 %mlp_back.1 = (bf16[1024,384]{1,0:T(8,128)(2,1)}, bf16[1024,384]{1,0:T(8,128)(2,1)}, bf16[1024,1536]{1,0:T(8,128)(2,1)}) custom-call(bf16[1024,384]{1,0:T(8,128)(2,1)} %land_rows.1.up_ref, bf16[1024,384]{1,0:T(8,128)(2,1)} %get-tuple-element.53.middle_ref, f32[1024,1536]{1,0:T(8,128)} %get-tuple-element.58.slope_ref, bf16[384,384]{1,0:T(8,128)(2,1)} %w_proj_ref.3, ...), custom_call_target="tpu_custom_call" | custom-call | flops 1 | bytes 1 | tf_op jit(solution)/shard_map/mlp_back/pallas_call | solution.py:628
  150.3 39.2 %attend_back.1.d_packed_ref = bf16[1024,1152]{1,0:T(8,128)(2,1)} custom-call(s32[1024,1]{1,0:T(8,128)} %copy.14.column_ref, s32[1,1024]{1,0:T(1,128)} %bitcast.6, bf16[1024,1152]{1,0:T(8,128)(2,1)} %get-tuple-element.51.q_ref.k_ref.v_ref, bf16[1024,1152]{1,0:T(8,128)(2,1)} %get-tuple-element.51.q_ref.k_ref.v_ref, ...), custom_call_target="tpu_custom_call" | custom-call | flops 1 | bytes 1 | tf_op jit(solution)/shard_map/attend_back/pallas_call | solution.py:493
  189.5 6.5 %inputs_back.1.x_ref = bf16[1024,384]{1,0:T(8,128)(2,1)} custom-call(bf16[1024,384]{1,0:T(8,128)(2,1)} %get-tuple-element.50.ordered_ref, bf16[1024,1152]{1,0:T(8,128)(2,1)} %attend_back.1.d_packed_ref, bf16[1024,384]{1,0:T(8,128)(2,1)} %get-tuple-element.59.d_middle_ref, bf16[384,1152]{1,0:T(8,128)(2,1)} %w_ref.3), custom_call_target="tpu_custom_call" | custom-call | flops 1 | bytes 1 | tf_op jit(solution)/shard_map/inputs_back/pallas_call | solution.py:674
  196.0 8.9 %return_rows.3 = bf16[128,32,384]{2,1,0:T(8,128)(2,1)} custom-call(s32[4,1,1024]{2,1,0:T(1,128)} %get-tuple-element.54.landing_ref, bf16[1024,384]{1,0:T(8,128)(2,1)} %inputs_back.1.x_ref), custom_call_target="tpu_custom_call" | custom-call | flops 1 | bytes 1 | tf_op jit(solution)/shard_map/return_rows/pallas_call | solution.py:297
  204.9 9.8 %all-to-all-start.3 = ((bf16[128,32,384]{2,1,0:T(8,128)(2,1)}), bf16[128,32,384]{2,1,0:T(8,128)(2,1)S(1)}, u32[]{:S(2)}, u32[]{:S(2)}) async-start(bf16[128,32,384]{2,1,0:T(8,128)(2,1)} %return_rows.3), calls=%async_computation.3 | async-start | bytes 6291456 | tf_op jit(solution)/shard_map/all_to_all | solution.py:863
  214.7 12.3 %weights_back.1 = (bf16[1536,384]{1,0:T(8,128)(2,1)}, bf16[1536,384]{1,0:T(8,128)(2,1)}, bf16[1536,384]{1,0:T(8,128)(2,1)}) custom-call(bf16[1024,384]{1,0:T(8,128)(2,1)} %get-tuple-element.50.ordered_ref, bf16[1024,384]{1,0:T(8,128)(2,1)} %get-tuple-element.53.middle_ref, bf16[1024,384]{1,0:T(8,128)(2,1)} %get-tuple-element.52.mixed_ref, ...), custom_call_target="tpu_custom_call" | custom-call | flops 1 | bytes 1 | tf_op jit(solution)/shard_map/weights_back/pallas_call | solution.py:730
  227.0 2.5 constant_dynamic-slice_fusion.13
  233.9 7.6 %unpack_rows.2 = bf16[1024,384]{1,0:T(8,128)(2,1)} custom-call(s32[1,1024]{1,0:T(1,128)} %get-tuple-element.56.slot_ref, bf16[128,32,384]{2,1,0:T(8,128)(2,1)} %copy-done.2), custom_call_target="tpu_custom_call" | custom-call | flops 1 | bytes 1 | tf_op jit(solution)/shard_map/unpack_rows/pallas_call | solution.py:165
  241.5 14.1 %all-to-all-done.3.home_ref = bf16[128,32,384]{2,1,0:T(8,128)(2,1)S(1)} async-done(((bf16[128,32,384]{2,1,0:T(8,128)(2,1)}), bf16[128,32,384]{2,1,0:T(8,128)(2,1)S(1)}, u32[]{:S(2)}, u32[]{:S(2)}) %all-to-all-start.3) | async-done | bytes 3145760 | tf_op jit(solution)/shard_map/all_to_all | solution.py:863
  262.7 7.8 %unpack_rows.3 = bf16[1024,384]{1,0:T(8,128)(2,1)} custom-call(s32[1,1024]{1,0:T(1,128)} %get-tuple-element.56.slot_ref, bf16[128,32,384]{2,1,0:T(8,128)(2,1)} %copy-done.1), custom_call_target="tpu_custom_call" | custom-call | flops 1 | bytes 1 | tf_op jit(solution)/shard_map/unpack_rows/pallas_call | solution.py:165
  272.3 2.7 collective-permute-start.14
  308.5 8.3 %collective-permute-start.13 = (bf16[768,384]{1,0:T(8,128)(2,1)S(1)}, bf16[768,384]{1,0:T(8,128)(2,1)S(1)}, u32[]{:S(2)}, u32[]{:S(2)}) collective-permute-start(bf16[768,384]{1,0:T(8,128)(2,1)S(1)} %maximum_select_fusion.w1_ref), channel_id=1, source_target_pairs={{0,16},{16,0},{32,48},{48,32},{64,80},{80,64},{96,112},{112,96},{1... | collective-permute-start | bytes 1769480 | tf_op jit(solution)/shard_map/ppermute | solution.py:761
  322.8 5.6 %finish.1 = (f32[384,1152]{1,0:T(8,128)}, f32[384,384]{1,0:T(8,128)}, f32[384,1536]{1,0:T(8,128)}, f32[1536,384]{1,0:T(8,128)}) custom-call(s32[1]{0:T(128)} %bitcast.4.keep_ref, bf16[768,384]{1,0:T(8,128)(2,1)} %copy-done.5, bf16[768,384]{1,0:T(8,128)(2,1)} %copy-done.11, bf16[768,384]{1,0:T(8,128)(2,1)} %copy-done.6, bf16[768,384]{1,0:T(8,128)(2,1)} %copy-done.12, ...), custom_call_target="tpu_custom_call" | custom-call | flops 1 | bytes 1 | tf_op jit(solution)/shard_map/finish/pallas_call | solution.py:837
  (125 shorter events, 55.2 us)
Async XLA Ops:
  8.5 55.4 %all-to-all-start = ((bf16[128,98,128]{2,1,0:T(8,128)(2,1)}), bf16[128,98,128]{2,1,0:T(8,128)(2,1)S(1)}, u32[]{:S(2)}, u32[]{:S(2)}) async-start(bf16[128,98,128]{2,1,0:T(8,128)(2,1)} %get-tuple-element.49), calls=%async_computation | async-start | bytes 6815744 | tf_op jit(solution)/shard_map/all_to_all | solution.py:863
  65.6 57.0 %all-to-all-start.1 = ((bf16[128,32,384]{2,1,0:T(8,128)(2,1)}), bf16[128,32,384]{2,1,0:T(8,128)(2,1)}, u32[]{:S(2)}, u32[]{:S(2)}) async-start(bf16[128,32,384]{2,1,0:T(8,128)(2,1)} %pack_rows.1), calls=%async_computation.1 | async-start | bytes 6291456 | tf_op jit(solution)/shard_map/all_to_all | solution.py:863
  122.6 66.9 %all-to-all-start.2 = ((bf16[128,32,384]{2,1,0:T(8,128)(2,1)}), bf16[128,32,384]{2,1,0:T(8,128)(2,1)S(1)}, u32[]{:S(2)}, u32[]{:S(2)}) async-start(bf16[128,32,384]{2,1,0:T(8,128)(2,1)} %return_rows.2), calls=%async_computation.2 | async-start | bytes 6291456 | tf_op jit(solution)/shard_map/all_to_all | solution.py:863
  204.9 50.7 %all-to-all-start.3 = ((bf16[128,32,384]{2,1,0:T(8,128)(2,1)}), bf16[128,32,384]{2,1,0:T(8,128)(2,1)S(1)}, u32[]{:S(2)}, u32[]{:S(2)}) async-start(bf16[128,32,384]{2,1,0:T(8,128)(2,1)} %return_rows.3), calls=%async_computation.3 | async-start | bytes 6291456 | tf_op jit(solution)/shard_map/all_to_all | solution.py:863
  229.5 12.0 %collective-permute-start = (bf16[768,384]{1,0:T(8,128)(2,1)}, bf16[768,384]{1,0:T(8,128)(2,1)}, u32[]{:S(2)}, u32[]{:S(2)}) collective-permute-start(bf16[768,384]{1,0:T(8,128)(2,1)} %get-tuple-element.96), channel_id=1, source_target_pairs={{0,16},{16,0},{32,48},{48,32},{64,80},{80,64},{96,112},{112,96},{1... | collective-permute-start | bytes 1769480 | tf_op jit(solution)/shard_map/ppermute | solution.py:761
  233.4 8.1 %collective-permute-start.1 = (bf16[768,384]{1,0:T(8,128)(2,1)}, bf16[768,384]{1,0:T(8,128)(2,1)}, u32[]{:S(2)}, u32[]{:S(2)}) collective-permute-start(bf16[768,384]{1,0:T(8,128)(2,1)} %get-tuple-element.94), channel_id=1, source_target_pairs={{0,16},{16,0},{32,48},{48,32},{64,80},{80,64},{96,112},{112,96},{1... | collective-permute-start | bytes 1769480 | tf_op jit(solution)/shard_map/ppermute | solution.py:761
  233.4 8.1 %collective-permute-start.2 = (bf16[768,384]{1,0:T(8,128)(2,1)}, bf16[768,384]{1,0:T(8,128)(2,1)}, u32[]{:S(2)}, u32[]{:S(2)}) collective-permute-start(bf16[768,384]{1,0:T(8,128)(2,1)} %get-tuple-element.92), channel_id=1, source_target_pairs={{0,16},{16,0},{32,48},{48,32},{64,80},{80,64},{96,112},{112,96},{1... | collective-permute-start | bytes 1769480 | tf_op jit(solution)/shard_map/ppermute | solution.py:761
  258.9 11.6 %collective-permute-start.3 = (bf16[384,384]{1,0:T(8,128)(2,1)}, bf16[384,384]{1,0:T(8,128)(2,1)}, u32[]{:S(2)}, u32[]{:S(2)}) collective-permute-start(bf16[384,384]{1,0:T(8,128)(2,1)} %get-tuple-element.102), channel_id=1, source_target_pairs={{0,32},{16,48},{32,0},{48,16},{64,96},{80,112},{96,64},{112,80},{1... | collective-permute-start | bytes 884744 | tf_op jit(solution)/shard_map/ppermute | solution.py:761
  261.3 9.3 %collective-permute-start.5 = (bf16[384,384]{1,0:T(8,128)(2,1)}, bf16[384,384]{1,0:T(8,128)(2,1)S(1)}, u32[]{:S(2)}, u32[]{:S(2)}) collective-permute-start(bf16[384,384]{1,0:T(8,128)(2,1)} %get-tuple-element.98), channel_id=1, source_target_pairs={{0,1},{1,0},{2,3},{3,2},{4,5},{5,4},{6,7},{7,6},{8,9},{9,8},{10,11... | collective-permute-start | bytes 884744 | tf_op jit(solution)/shard_map/ppermute | solution.py:761
  262.1 8.4 %collective-permute-start.4 = (bf16[384,384]{1,0:T(8,128)(2,1)S(1)}, bf16[384,384]{1,0:T(8,128)(2,1)S(1)}, u32[]{:S(2)}, u32[]{:S(2)}) collective-permute-start(bf16[384,384]{1,0:T(8,128)(2,1)S(1)} %get-tuple-element.100), channel_id=1, source_target_pairs={{0,4},{1,5},{2,6},{3,7},{4,0},{5,1},{6,2},{7,3},{8,12},{9,13},{10,... | collective-permute-start | bytes 884744 | tf_op jit(solution)/shard_map/ppermute | solution.py:761
  271.6 5.3 %collective-permute-start.6 = (bf16[192,384]{1,0:T(8,128)(2,1)S(1)}, bf16[192,384]{1,0:T(8,128)(2,1)S(1)}, u32[]{:S(2)}, u32[]{:S(2)}) collective-permute-start(bf16[192,384]{1,0:T(8,128)(2,1)S(1)} %constant_dynamic-slice_fusion.2), channel_id=1, source_target_pairs={{0,96},{16,112},{32,64},{48,80},{64,32},{80,48},{96,0},{112,16},{1... | collective-permute-start | bytes 442376 | tf_op jit(solution)/shard_map/ppermute | solution.py:761
  272.3 5.7 %collective-permute-start.14 = (bf16[192,384]{1,0:T(8,128)(2,1)S(1)}, bf16[192,384]{1,0:T(8,128)(2,1)S(1)}, u32[]{:S(2)}, u32[]{:S(2)}) collective-permute-start(bf16[192,384]{1,0:T(8,128)(2,1)S(1)} %constant_dynamic-slice_fusion.1), channel_id=1, source_target_pairs={{0,12},{1,13},{2,14},{3,15},{4,8},{5,9},{6,10},{7,11},{8,4},{9,5},... | collective-permute-start | bytes 442376 | tf_op jit(solution)/shard_map/ppermute | solution.py:761
  275.1 5.6 %collective-permute-start.22 = (bf16[192,384]{1,0:T(8,128)(2,1)S(1)}, bf16[192,384]{1,0:T(8,128)(2,1)S(1)}, u32[]{:S(2)}, u32[]{:S(2)}) collective-permute-start(bf16[192,384]{1,0:T(8,128)(2,1)S(1)} %constant_dynamic-slice_fusion), channel_id=1, source_target_pairs={{0,3},{1,2},{2,1},{3,0},{4,7},{5,6},{6,5},{7,4},{8,11},{9,10},{10,... | collective-permute-start | bytes 442376 | tf_op jit(solution)/shard_map/ppermute | solution.py:761
  283.0 5.3 %collective-permute-start.16 = (bf16[192,384]{1,0:T(8,128)(2,1)S(1)}, bf16[192,384]{1,0:T(8,128)(2,1)S(1)}, u32[]{:S(2)}, u32[]{:S(2)}) collective-permute-start(bf16[192,384]{1,0:T(8,128)(2,1)S(1)} %add_convert_fusion.14), channel_id=1, source_target_pairs={{0,3},{1,2},{2,1},{3,0},{4,7},{5,6},{6,5},{7,4},{8,11},{9,10},{10,... | collective-permute-start | bytes 442376 | tf_op jit(solution)/shard_map/ppermute | solution.py:761
  285.3 5.6 %collective-permute-start.24 = (bf16[192,384]{1,0:T(8,128)(2,1)S(1)}, bf16[192,384]{1,0:T(8,128)(2,1)S(1)}, u32[]{:S(2)}, u32[]{:S(2)}) collective-permute-start(bf16[192,384]{1,0:T(8,128)(2,1)S(1)} %add_convert_fusion.9), channel_id=1, source_target_pairs={{0,96},{16,112},{32,64},{48,80},{64,32},{80,48},{96,0},{112,16},{1... | collective-permute-start | bytes 442376 | tf_op jit(solution)/shard_map/ppermute | solution.py:761
  291.1 5.5 %collective-permute-start.10 = (bf16[192,384]{1,0:T(8,128)(2,1)S(1)}, bf16[192,384]{1,0:T(8,128)(2,1)S(1)}, u32[]{:S(2)}, u32[]{:S(2)}) collective-permute-start(bf16[192,384]{1,0:T(8,128)(2,1)S(1)} %add_convert_fusion.17), channel_id=1, source_target_pairs={{0,3},{1,2},{2,1},{3,0},{4,7},{5,6},{6,5},{7,4},{8,11},{9,10},{10,... | collective-permute-start | bytes 442376 | tf_op jit(solution)/shard_map/ppermute | solution.py:761
  293.4 5.3 %collective-permute-start.18 = (bf16[192,384]{1,0:T(8,128)(2,1)S(1)}, bf16[192,384]{1,0:T(8,128)(2,1)S(1)}, u32[]{:S(2)}, u32[]{:S(2)}) collective-permute-start(bf16[192,384]{1,0:T(8,128)(2,1)S(1)} %add_convert_fusion.12), channel_id=1, source_target_pairs={{0,96},{16,112},{32,64},{48,80},{64,32},{80,48},{96,0},{112,16},{1... | collective-permute-start | bytes 442376 | tf_op jit(solution)/shard_map/ppermute | solution.py:761
  296.7 5.6 %collective-permute-start.11 = (bf16[192,384]{1,0:T(8,128)(2,1)S(1)}, bf16[192,384]{1,0:T(8,128)(2,1)S(1)}, u32[]{:S(2)}, u32[]{:S(2)}) collective-permute-start(bf16[192,384]{1,0:T(8,128)(2,1)S(1)} %add_convert_fusion.16), channel_id=1, source_target_pairs={{0,96},{16,112},{32,64},{48,80},{64,32},{80,48},{96,0},{112,16},{1... | collective-permute-start | bytes 442376 | tf_op jit(solution)/shard_map/ppermute | solution.py:761
  298.8 5.6 %collective-permute-start.19 = (bf16[192,384]{1,0:T(8,128)(2,1)S(1)}, bf16[192,384]{1,0:T(8,128)(2,1)S(1)}, u32[]{:S(2)}, u32[]{:S(2)}) collective-permute-start(bf16[192,384]{1,0:T(8,128)(2,1)S(1)} %add_convert_fusion.11), channel_id=1, source_target_pairs={{0,12},{1,13},{2,14},{3,15},{4,8},{5,9},{6,10},{7,11},{8,4},{9,5},... | collective-permute-start | bytes 442376 | tf_op jit(solution)/shard_map/ppermute | solution.py:761
  300.7 5.6 %collective-permute-start.27 = (bf16[192,384]{1,0:T(8,128)(2,1)S(1)}, bf16[192,384]{1,0:T(8,128)(2,1)S(1)}, u32[]{:S(2)}, u32[]{:S(2)}) collective-permute-start(bf16[192,384]{1,0:T(8,128)(2,1)S(1)} %add_convert_fusion.6), channel_id=1, source_target_pairs={{0,3},{1,2},{2,1},{3,0},{4,7},{5,6},{6,5},{7,4},{8,11},{9,10},{10,... | collective-permute-start | bytes 442376 | tf_op jit(solution)/shard_map/ppermute | solution.py:761
  302.3 5.9 %collective-permute-start.12 = (bf16[384,384]{1,0:T(8,128)(2,1)S(1)}, bf16[384,384]{1,0:T(8,128)(2,1)S(1)}, u32[]{:S(2)}, u32[]{:S(2)}) collective-permute-start(bf16[384,384]{1,0:T(8,128)(2,1)S(1)} %maximum_select_fusion.3), channel_id=1, source_target_pairs={{0,32},{16,48},{32,0},{48,16},{64,96},{80,112},{96,64},{112,80},{1... | collective-permute-start | bytes 884744 | tf_op jit(solution)/shard_map/ppermute | solution.py:761
  304.4 12.4 %collective-permute-start.20 = (bf16[384,384]{1,0:T(8,128)(2,1)S(1)}, bf16[384,384]{1,0:T(8,128)(2,1)S(1)}, u32[]{:S(2)}, u32[]{:S(2)}) collective-permute-start(bf16[384,384]{1,0:T(8,128)(2,1)S(1)} %maximum_select_fusion.4), channel_id=1, source_target_pairs={{0,4},{1,5},{2,6},{3,7},{4,0},{5,1},{6,2},{7,3},{8,12},{9,13},{10,... | collective-permute-start | bytes 884744 | tf_op jit(solution)/shard_map/ppermute | solution.py:761
  306.3 12.5 %collective-permute-start.28 = (bf16[384,384]{1,0:T(8,128)(2,1)S(1)}, bf16[384,384]{1,0:T(8,128)(2,1)S(1)}, u32[]{:S(2)}, u32[]{:S(2)}) collective-permute-start(bf16[384,384]{1,0:T(8,128)(2,1)S(1)} %maximum_select_fusion.5), channel_id=1, source_target_pairs={{0,1},{1,0},{2,3},{3,2},{4,5},{5,4},{6,7},{7,6},{8,9},{9,8},{10,11... | collective-permute-start | bytes 884744 | tf_op jit(solution)/shard_map/ppermute | solution.py:761
  308.5 11.9 %collective-permute-start.13 = (bf16[768,384]{1,0:T(8,128)(2,1)S(1)}, bf16[768,384]{1,0:T(8,128)(2,1)S(1)}, u32[]{:S(2)}, u32[]{:S(2)}) collective-permute-start(bf16[768,384]{1,0:T(8,128)(2,1)S(1)} %maximum_select_fusion.w1_ref), channel_id=1, source_target_pairs={{0,16},{16,0},{32,48},{48,32},{64,80},{80,64},{96,112},{112,96},{1... | collective-permute-start | bytes 1769480 | tf_op jit(solution)/shard_map/ppermute | solution.py:761
  (25 other events, 144.4 us)

commit v4 on v3

--- a/solution.py
+++ b/solution.py
@@ -18,7 +18,7 @@
 SHARDS = 128
 CAP = 32
 SLOTS = SHARDS * CAP
-STEP_SHARDS = 32
+STEP_SHARDS = 64
 STEP_SLOTS = STEP_SHARDS * CAP
 STEPS = SHARDS // STEP_SHARDS
 WIRE_ROWS = 3 * CAP + 2
@@ -29,7 +29,6 @@
 TILE = 256
 BF = jnp.bfloat16
 F32 = jnp.float32
-VMEM_LIMIT = 56 * 1024 * 1024
 
 NO_COST = pl.CostEstimate(flops=1, bytes_accessed=1, transcendentals=0)
 
@@ -48,9 +47,9 @@
     return lax.broadcasted_iota(jnp.int32, shape, axis)
 
 
-def params(grid_dims=1):
+def params(grid_dims=1, mib=56):
     return pltpu.CompilerParams(
-        vmem_limit_bytes=VMEM_LIMIT,
+        vmem_limit_bytes=mib * 1024 * 1024,
         dimension_semantics=("arbitrary",) * grid_dims,
     )
 
@@ -331,31 +330,40 @@
 def query_side(q, head, owner, shift=None):
     near, far = (head + 1) % HEADS_PER_GROUP, (head + 2) % HEADS_PER_GROUP
     high, middle, low = (part.astype(F32) for part in three_parts(q * (SCALING * LOG2E)))
-    first = jnp.where(owner == head, high, 0.0)
-    second = jnp.where(
-        owner == near,
-        roll_lanes(middle, HEAD_DIM),
-        jnp.where(owner == far, roll_lanes(low, 2 * HEAD_DIM), 0.0),
+    side = jnp.where(
+        owner == head,
+        high,
+        jnp.where(
+            owner == near,
+            roll_lanes(middle, HEAD_DIM),
+            jnp.where(owner == far, roll_lanes(low, 2 * HEAD_DIM), 0.0),
+        ),
     )
     if shift is not None:
-        lane = iota((ROWS, LANES), 1) - head * HEAD_DIM
-        parts = [part.astype(F32) for part in three_parts(-shift)]
-        for at, part in enumerate(parts):
-            second = jnp.where(lane == at, part, second)
-    return jnp.concatenate([first.astype(BF), second.astype(BF)], axis=1)
+        last = (head + 3) % HEADS_PER_GROUP
+        lane = iota((ROWS, LANES), 1) - last * HEAD_DIM
+        shift = roll_lanes(shift, 3 * HEAD_DIM)
+        for at, part in enumerate(three_parts(-shift)):
+            side = jnp.where(lane == at, part.astype(F32), side)
+    return side.astype(BF)
 
 
 def key_side(k, head, owner, shifted):
     near, far = (head + 1) % HEADS_PER_GROUP, (head + 2) % HEADS_PER_GROUP
-    second = jnp.where(
-        owner == near,
-        roll_lanes(k, HEAD_DIM),
-        jnp.where(owner == far, roll_lanes(k, 2 * HEAD_DIM), 0.0),
+    side = jnp.where(
+        owner == head,
+        k,
+        jnp.where(
+            owner == near,
+            roll_lanes(k, HEAD_DIM),
+            jnp.where(owner == far, roll_lanes(k, 2 * HEAD_DIM), 0.0),
+        ),
     )
     if shifted:
-        lane = iota((ROWS, LANES), 1) - head * HEAD_DIM
-        second = jnp.where((lane >= 0) & (lane < 3), 1.0, second)
-    return jnp.concatenate([k.astype(BF), second.astype(BF)], axis=1)
+        last = (head + 3) % HEADS_PER_GROUP
+        lane = iota((ROWS, LANES), 1) - last * HEAD_DIM
+        side = jnp.where((lane >= 0) & (lane < 3), 1.0, side)
+    return side.astype(BF)
 
 
 def attend_kernel(column_ref, row_ref, q_ref, k_ref, v_ref, mixed_ref, exact_ref, level_ref, bias_s):
@@ -466,24 +474,20 @@
         value_side = jnp.where((lane >= 0) & (lane < 3), 1.0, v).astype(BF)
         query_mine = jnp.where(mine, q, 0.0).astype(BF)
         head_rows = slice(head * HEAD_DIM, (head + 1) * HEAD_DIM)
+        dv_part = dk_part = 0.0
         for tile in range(ROWS // TILE):
-            rows = slice(tile * TILE, (tile + 1) * TILE)
-            weights = jnp.exp2(dot_nt(keys[rows], queries) + bias_s[rows, :])
-            pulled = weights * dot_nt(value_side[rows], up_side)
-            pulled = pulled.astype(BF)
-            dv_part = dot(weights.astype(BF), up_mine)
-            dk_part = dot(pulled, query_mine)
-            dq_part = dot(keys_t[head_rows, rows], pulled)
-            if head == 0:
-                dv_s[rows, :] = dv_part
-                dk_s[rows, :] = dk_part
-            else:
-                dv_s[rows, :] += dv_part
-                dk_s[rows, :] += dk_part
-            if tile == 0:
-                dqt_s[head_rows, :] = dq_part
-            else:
-                dqt_s[head_rows, :] += dq_part
+            at = slice(tile * TILE, (tile + 1) * TILE)
+            weights = jnp.exp2(dot_nt(keys, queries[at]) + bias_s[:, at])
+            pulled = (weights * dot_nt(value_side, up_side[at])).astype(BF)
+            dv_part = dv_part + dot(weights.astype(BF), up_mine[at])
+            dk_part = dk_part + dot(pulled, query_mine[at])
+            dqt_s[head_rows, at] = dot(keys_t[head_rows], pulled)
+        if head == 0:
+            dv_s[...] = dv_part
+            dk_s[...] = dk_part
+        else:
+            dv_s[...] += dv_part
+            dk_s[...] += dk_part
     out_ref[:, :LANES] = (dqt_s[...] * SCALING).T.astype(BF)
     out_ref[:, LANES : 2 * LANES] = (dk_s[...] * SCALING).astype(BF)
     out_ref[:, 2 * LANES :] = dv_s[...].astype(BF)
@@ -654,33 +658,47 @@
     return slice(first, first + LANES)
 
 
-def inputs_back_kernel(ordered_ref, d_packed_ref, d_middle_ref, w_ref, out_ref):
-    normed, scale = norm_parts(ordered_ref[...].astype(F32))
-    weights = jnp.concatenate(
-        [
-            w_ref[:, group_columns(part, group)]
-            for group in range(GROUPS)
-            for part in range(3)
-        ],
-        axis=1,
-    )
-    d_normed = dot_nt(d_packed_ref[...], weights)
-    pulled = norm_pull(normed, scale, d_normed.astype(BF).astype(F32)).astype(BF)
-    out_ref[...] = (d_middle_ref[...].astype(F32) + pulled.astype(F32)).astype(BF)
-
-
-def inputs_back(ordered, d_packed, d_middle, w_qkv):
+def inputs_back_kernel(
+    landing_ref, ordered_ref, d_packed_ref, d_middle_ref, w_ref, out_ref, d_inputs_s
+):
+    @pl.when(pl.program_id(0) == 0)
+    def _():
+        normed, scale = norm_parts(ordered_ref[...].astype(F32))
+        weights = jnp.concatenate(
+            [
+                w_ref[:, group_columns(part, group)]
+                for group in range(GROUPS)
+                for part in range(3)
+            ],
+            axis=1,
+        )
+        d_normed = dot_nt(d_packed_ref[...], weights)
+        pulled = norm_pull(normed, scale, d_normed.astype(BF).astype(F32)).astype(BF)
+        d_inputs_s[...] = (d_middle_ref[...].astype(F32) + pulled.astype(F32)).astype(BF)
+
+    picked = dot(return_one_hot(landing_ref[0]), d_inputs_s[...])
+    out_ref[...] = picked.astype(BF).reshape(STEP_SHARDS, CAP, D)
+
+
+def inputs_back(landing, ordered, d_packed, d_middle, w_qkv):
     rows = whole((ROWS, D))
     return pl.pallas_call(
         inputs_back_kernel,
-        grid=(1,),
-        in_specs=[rows, whole((ROWS, 3 * D)), rows, whole((D, 3 * D))],
-        out_specs=rows,
-        out_shape=jax.ShapeDtypeStruct((ROWS, D), BF),
+        grid=(STEPS,),
+        in_specs=[
+            pl.BlockSpec((1, 1, STEP_SLOTS), lambda i: (i, 0, 0)),
+            rows,
+            whole((ROWS, 3 * D)),
+            rows,
+            whole((D, 3 * D)),
+        ],
+        out_specs=pl.BlockSpec((STEP_SHARDS, CAP, D), lambda i: (i, 0, 0)),
+        out_shape=jax.ShapeDtypeStruct((SHARDS, CAP, D), BF),
+        scratch_shapes=[pltpu.VMEM((ROWS, D), BF)],
         compiler_params=params(),
         cost_estimate=NO_COST,
         name="inputs_back",
-    )(ordered, d_packed, d_middle, w_qkv)
+    )(landing, ordered, d_packed, d_middle, w_qkv)
 
 
 def transposed(values):
@@ -809,11 +827,10 @@
     keep_ref, w1_ref, w1_other_ref, w2_ref, w2_other_ref, rest_ref, rest_other_ref, qkv_ref, proj_ref, out1_ref, out2_ref
 ):
     step = pl.program_id(0)
-    rows = pl.ds(pl.multiple_of(lax.rem(step, 2) * D, D), D)
     own = step // 2 == keep_ref[0]
 
     def block(mine_ref, other_ref):
-        return jnp.where(own, mine_ref[rows, :].astype(F32), other_ref[rows, :].astype(F32))
+        return jnp.where(own, mine_ref[...].astype(F32), other_ref[...].astype(F32))
 
     out1_ref[...] = block(w1_ref, w1_other_ref)
     out2_ref[...] = block(w2_ref, w2_other_ref)
@@ -833,7 +850,7 @@
 def finish(sums):
     keep = side("core", 0).astype(jnp.int32).reshape(1)
     halves = [part for mine in sums for part in (mine, swap(mine, "core", 0))]
-    half = whole((FF // 2, D))
+    half = pl.BlockSpec((D, D), lambda i: (i % 2, 0))
     return pl.pallas_call(
         finish_kernel,
         grid=(FF // D,),
@@ -869,7 +886,8 @@
     segment_column = segment_ids.reshape(ROWS, 1)
     wire, slot_row = pack_points(first_lane, hilbert_pos.reshape(1, ROWS), points)
     ordered, packed, landing = land_points(exchange(wire), w_qkv)
-    up_received = exchange(pack_rows(slot_row, cotangent))
+    up_slots, segment_column = together((pack_rows(slot_row, cotangent), segment_column))
+    up_received = exchange(up_slots)
     mixed, exact, level = attend(segment_column, segment_row, packed)
     block, middle, hidden, slope = mlp(ordered, mixed, w_proj, w_fc1, w_fc2)
     returned, up_received = together((return_rows(landing, block), up_received))
@@ -878,7 +896,7 @@
     d_middle, d_mixed, d_before = mlp_back(upstream, middle, slope, w_proj, w_fc1, w_fc2)
     d_packed = attend_back(segment_column, segment_row, packed, d_mixed, exact, level)
     d_packed, output_home = together((d_packed, output_home))
-    back = return_rows(landing, inputs_back(ordered, d_packed, d_middle, w_qkv))
+    back = inputs_back(landing, ordered, d_packed, d_middle, w_qkv)
     grad_home = exchange(back)
     d_packed, output_home, _ = together((d_packed, output_home, back))
     sums = weights_back(ordered, middle, mixed, d_middle, upstream, d_packed, d_before, hidden)

time: 333 us -> 330 us (level)
  Pallas kernels: 171 us -> 166 us
    pallas_call x2 -> x1, Pallas kernels: 18.3 us -> 8.11 us  [return_rows(): pl.pallas_call(return_rows_kernel, grid=(STEPS,), in_specs=[pl.BlockSpec(...]
    pallas_call x1, Pallas kernels: 6.48 us -> 12.6 us  [inputs_back(): pl.pallas_call(inputs_back_kernel, grid=(STEPS,), in_specs=[pl.BlockSpec(...]
where the time goes in v4:
time: 330 us; the launch traced here: 324 us
  Pallas kernels  166 us (50%)
  starting transfers between devices  74.1 us (22%)
  waiting for transfers between devices  65.7 us (20%)
  local copies, waits for them, and re-layouts  10.7 us (3%)
  other arithmetic  6.58 us (2%)
    all_to_all x4, waiting for transfers between devices, exchange(): return lax.all_to_all(values, AXES, split_axis=0, concat_axis=0, tiled=True)  51 us
    pallas_call x1, Pallas kernels, attend_back(): pl.pallas_call(attend_back_kernel, grid=(GROUPS,), in_specs=[whole((ROWS,...  37.5 us
    ppermute x30, starting transfers between devices, swap(): return lax.ppermute(values, name, pairs)  37.1 us
    all_to_all x4, starting transfers between devices, exchange(): return lax.all_to_all(values, AXES, split_axis=0, concat_axis=0, tiled=True)  37 us
    pallas_call x1, Pallas kernels, attend(): pl.pallas_call(attend_kernel, grid=(GROUPS,), in_specs=[whole((ROWS, 1)),...  20.9 us
    pallas_call x2, Pallas kernels, unpack_rows(): pl.pallas_call(unpack_rows_kernel, grid=(STEPS,), in_specs=[pl.BlockSpec(...  15 us
    ppermute x30, waiting for transfers between devices, swap(): return lax.ppermute(values, name, pairs)  14.6 us
    pallas_call x1, Pallas kernels, inputs_back(): pl.pallas_call(inputs_back_kernel, grid=(STEPS,), in_specs=[pl.BlockSpec(...  12.6 us
  transfers between devices with their start and end apart: 34, of which 16 were waited for; matrix products, arithmetic and copies ran while one was open for 3% of the time, Pallas kernels for 43%

profile of v4, /device:TPU:1, one launch (start us, length us, event | category | flops | bytes accessed | tf_op | source)
XLA Modules:
  0.0 324.2 jit_solution(11784303766203628739)
XLA Ops:
  0.6 7.8 %pack_points.1 = (bf16[128,98,128]{2,1,0:T(8,128)(2,1)}, s32[1,1024]{1,0:T(1,128)}) custom-call(s32[1]{0:T(128)} %bitcast.lane_ref, s32[1,1024]{1,0:T(1,128)} %bitcast.8, bf16[1024,384]{1,0:T(8,128)(2,1)} %x_ref.2), custom_call_target="tpu_custom_call" | custom-call | flops 1 | bytes 1 | tf_op jit(solution)/shard_map/pack_points/pallas_call | solution.py:100
  8.4 11.5 %all-to-all-start = ((bf16[128,98,128]{2,1,0:T(8,128)(2,1)}), bf16[128,98,128]{2,1,0:T(8,128)(2,1)S(1)}, u32[]{:S(2)}, u32[]{:S(2)}) async-start(bf16[128,98,128]{2,1,0:T(8,128)(2,1)} %get-tuple-element.51), calls=%async_computation | async-start | bytes 6815744 | tf_op jit(solution)/shard_map/all_to_all | solution.py:880
  19.9 7.1 %pack_rows.1 = bf16[128,32,384]{2,1,0:T(8,128)(2,1)} custom-call(s32[1,1024]{1,0:T(1,128)} %get-tuple-element.53.slot_ref, bf16[1024,384]{1,0:T(8,128)(2,1)} %x_ref.3), custom_call_target="tpu_custom_call" | custom-call | flops 1 | bytes 1 | tf_op jit(solution)/shard_map/pack_rows/pallas_call | solution.py:129
  27.0 36.8 %all-to-all-done.recv_ref = bf16[128,98,128]{2,1,0:T(8,128)(2,1)S(1)} async-done(((bf16[128,98,128]{2,1,0:T(8,128)(2,1)}), bf16[128,98,128]{2,1,0:T(8,128)(2,1)S(1)}, u32[]{:S(2)}, u32[]{:S(2)}) %all-to-all-start) | async-done | bytes 3211296 | tf_op jit(solution)/shard_map/all_to_all | solution.py:880
  65.5 5.8 %all-to-all-start.1 = ((bf16[128,32,384]{2,1,0:T(8,128)(2,1)}), bf16[128,32,384]{2,1,0:T(8,128)(2,1)}, u32[]{:S(2)}, u32[]{:S(2)}) async-start(bf16[128,32,384]{2,1,0:T(8,128)(2,1)} %pack_rows.1), calls=%async_computation.1 | async-start | bytes 6291456 | tf_op jit(solution)/shard_map/all_to_all | solution.py:880
  72.4 9.9 %land_points.1 = (bf16[1024,384]{1,0:T(8,128)(2,1)}, bf16[1024,1152]{1,0:T(8,128)(2,1)}, s32[2,1,2048]{2,1,0:T(1,128)}) custom-call(bf16[128,98,128]{2,1,0:T(8,128)(2,1)} %copy-done, bf16[384,1152]{1,0:T(8,128)(2,1)} %w_ref.3), custom_call_target="tpu_custom_call" | custom-call | flops 1 | bytes 1 | tf_op jit(solution)/shard_map/land_points/pallas_call | solution.py:230
  82.3 20.9 %attend.1 = (bf16[1024,384]{1,0:T(8,128)(2,1)}, f32[1024,384]{1,0:T(8,128)}, f32[1024,384]{1,0:T(8,128)}) custom-call(s32[1024,1]{1,0:T(8,128)} %copy.14.column_ref, s32[1,1024]{1,0:T(1,128)} %bitcast.5, bf16[1024,1152]{1,0:T(8,128)(2,1)} %get-tuple-element.55.q_ref.k_ref.v_ref, bf16[1024,1152]{1,0:T(8,128)(2,1)} %get-tuple-element.55.q_ref.k_ref.v_ref, ...), custom_call_target="tpu_custom_call" | custom-call | flops 1 | bytes 1 | tf_op jit(solution)/shard_map/attend/pallas_call | solution.py:411
  103.2 10.4 %mlp.1 = (bf16[1024,384]{1,0:T(8,128)(2,1)}, bf16[1024,384]{1,0:T(8,128)(2,1)}, bf16[1024,1536]{1,0:T(8,128)(2,1)}, f32[1024,1536]{1,0:T(8,128)}) custom-call(bf16[1024,384]{1,0:T(8,128)(2,1)} %get-tuple-element.52.ordered_ref, bf16[1024,384]{1,0:T(8,128)(2,1)} %get-tuple-element.56.mixed_ref, bf16[384,384]{1,0:T(8,128)(2,1)} %w_proj_ref.3, ...), custom_call_target="tpu_custom_call" | custom-call | flops 1 | bytes 1 | tf_op jit(solution)/shard_map/mlp/pallas_call | solution.py:569
  113.6 8.1 %return_rows.1 = bf16[128,32,384]{2,1,0:T(8,128)(2,1)} custom-call(s32[2,1,2048]{2,1,0:T(1,128)} %get-tuple-element.58.landing_ref, bf16[1024,384]{1,0:T(8,128)(2,1)} %get-tuple-element.59.x_ref), custom_call_target="tpu_custom_call" | custom-call | flops 1 | bytes 1 | tf_op jit(solution)/shard_map/return_rows/pallas_call | solution.py:296
  121.7 9.9 %all-to-all-start.2 = ((bf16[128,32,384]{2,1,0:T(8,128)(2,1)}), bf16[128,32,384]{2,1,0:T(8,128)(2,1)S(1)}, u32[]{:S(2)}, u32[]{:S(2)}) async-start(bf16[128,32,384]{2,1,0:T(8,128)(2,1)} %return_rows.1), calls=%async_computation.2 | async-start | bytes 6291456 | tf_op jit(solution)/shard_map/all_to_all | solution.py:880
  131.6 7.3 %land_rows.1.up_ref = bf16[1024,384]{1,0:T(8,128)(2,1)} custom-call(s32[2,1,2048]{2,1,0:T(1,128)} %get-tuple-element.58.landing_ref, bf16[128,32,384]{2,1,0:T(8,128)(2,1)} %all-to-all-done.1.recv_ref), custom_call_target="tpu_custom_call" | custom-call | flops 1 | bytes 1 | tf_op jit(solution)/shard_map/land_rows/pallas_call | solution.py:269
  138.9 10.5 %mlp_back.1 = (bf16[1024,384]{1,0:T(8,128)(2,1)}, bf16[1024,384]{1,0:T(8,128)(2,1)}, bf16[1024,1536]{1,0:T(8,128)(2,1)}) custom-call(bf16[1024,384]{1,0:T(8,128)(2,1)} %land_rows.1.up_ref, bf16[1024,384]{1,0:T(8,128)(2,1)} %get-tuple-element.57.middle_ref, f32[1024,1536]{1,0:T(8,128)} %get-tuple-element.62.slope_ref, bf16[384,384]{1,0:T(8,128)(2,1)} %w_proj_ref.3, ...), custom_call_target="tpu_custom_call" | custom-call | flops 1 | bytes 1 | tf_op jit(solution)/shard_map/mlp_back/pallas_call | solution.py:632
  149.4 37.5 %attend_back.1.d_packed_ref = bf16[1024,1152]{1,0:T(8,128)(2,1)} custom-call(s32[1024,1]{1,0:T(8,128)} %copy.14.column_ref, s32[1,1024]{1,0:T(1,128)} %bitcast.6, bf16[1024,1152]{1,0:T(8,128)(2,1)} %get-tuple-element.55.q_ref.k_ref.v_ref, bf16[1024,1152]{1,0:T(8,128)(2,1)} %get-tuple-element.55.q_ref.k_ref.v_ref, ...), custom_call_target="tpu_custom_call" | custom-call | flops 1 | bytes 1 | tf_op jit(solution)/shard_map/attend_back/pallas_call | solution.py:497
  186.9 12.6 %inputs_back.1 = bf16[128,32,384]{2,1,0:T(8,128)(2,1)} custom-call(s32[2,1,2048]{2,1,0:T(1,128)} %get-tuple-element.58.landing_ref, bf16[1024,384]{1,0:T(8,128)(2,1)} %get-tuple-element.52.ordered_ref, bf16[1024,1152]{1,0:T(8,128)(2,1)} %attend_back.1.d_packed_ref, bf16[1024,384]{1,0:T(8,128)(2,1)} %get-tuple-element.63.d_middle_ref, bf16[384,1152]{1,0:T(8,128)(2,1)} %w_ref.3), custom_call_target="tpu_custom_call" | custom-call | flops 1 | bytes 1 | tf_op jit(solution)/shard_map/inputs_back/pallas_call | solution.py:685
  199.4 9.8 %all-to-all-start.3 = ((bf16[128,32,384]{2,1,0:T(8,128)(2,1)}), bf16[128,32,384]{2,1,0:T(8,128)(2,1)S(1)}, u32[]{:S(2)}, u32[]{:S(2)}) async-start(bf16[128,32,384]{2,1,0:T(8,128)(2,1)} %inputs_back.1), calls=%async_computation.3 | async-start | bytes 6291456 | tf_op jit(solution)/shard_map/all_to_all | solution.py:880
  209.2 12.3 %weights_back.1 = (bf16[1536,384]{1,0:T(8,128)(2,1)}, bf16[1536,384]{1,0:T(8,128)(2,1)}, bf16[1536,384]{1,0:T(8,128)(2,1)}) custom-call(bf16[1024,384]{1,0:T(8,128)(2,1)} %get-tuple-element.52.ordered_ref, bf16[1024,384]{1,0:T(8,128)(2,1)} %get-tuple-element.57.middle_ref, bf16[1024,384]{1,0:T(8,128)(2,1)} %get-tuple-element.56.mixed_ref, ...), custom_call_target="tpu_custom_call" | custom-call | flops 1 | bytes 1 | tf_op jit(solution)/shard_map/weights_back/pallas_call | solution.py:748
  221.5 2.5 constant_dynamic-slice_fusion.13
  228.4 7.5 %unpack_rows.2 = bf16[1024,384]{1,0:T(8,128)(2,1)} custom-call(s32[1,1024]{1,0:T(1,128)} %get-tuple-element.53.slot_ref, bf16[128,32,384]{2,1,0:T(8,128)(2,1)} %copy-done.2), custom_call_target="tpu_custom_call" | custom-call | flops 1 | bytes 1 | tf_op jit(solution)/shard_map/unpack_rows/pallas_call | solution.py:164
  235.9 14.2 %all-to-all-done.3.home_ref = bf16[128,32,384]{2,1,0:T(8,128)(2,1)S(1)} async-done(((bf16[128,32,384]{2,1,0:T(8,128)(2,1)}), bf16[128,32,384]{2,1,0:T(8,128)(2,1)S(1)}, u32[]{:S(2)}, u32[]{:S(2)}) %all-to-all-start.3) | async-done | bytes 3145760 | tf_op jit(solution)/shard_map/all_to_all | solution.py:880
  250.2 2.4 add_convert_fusion.2
  257.4 7.5 %unpack_rows.3 = bf16[1024,384]{1,0:T(8,128)(2,1)} custom-call(s32[1,1024]{1,0:T(1,128)} %get-tuple-element.53.slot_ref, bf16[128,32,384]{2,1,0:T(8,128)(2,1)} %copy-done.1), custom_call_target="tpu_custom_call" | custom-call | flops 1 | bytes 1 | tf_op jit(solution)/shard_map/unpack_rows/pallas_call | solution.py:164
  266.8 2.9 collective-permute-start.14
  303.2 8.0 %collective-permute-start.13 = (bf16[768,384]{1,0:T(8,128)(2,1)S(1)}, bf16[768,384]{1,0:T(8,128)(2,1)S(1)}, u32[]{:S(2)}, u32[]{:S(2)}) collective-permute-start(bf16[768,384]{1,0:T(8,128)(2,1)S(1)} %maximum_select_fusion.w1_ref), channel_id=1, source_target_pairs={{0,16},{16,0},{32,48},{48,32},{64,80},{80,64},{96,112},{112,96},{1... | collective-permute-start | bytes 1769480 | tf_op jit(solution)/shard_map/ppermute | solution.py:779
  317.4 6.6 %finish.1 = (f32[384,1152]{1,0:T(8,128)}, f32[384,384]{1,0:T(8,128)}, f32[384,1536]{1,0:T(8,128)}, f32[1536,384]{1,0:T(8,128)}) custom-call(s32[1]{0:T(128)} %bitcast.4.keep_ref, bf16[768,384]{1,0:T(8,128)(2,1)} %copy-done.5, bf16[768,384]{1,0:T(8,128)(2,1)} %copy-done.11, bf16[768,384]{1,0:T(8,128)(2,1)} %copy-done.6, bf16[768,384]{1,0:T(8,128)(2,1)} %copy-done.12, ...), custom_call_target="tpu_custom_call" | custom-call | flops 1 | bytes 1 | tf_op jit(solution)/shard_map/finish/pallas_call | solution.py:854
  (124 shorter events, 53.3 us)
Async XLA Ops:
  8.4 55.4 %all-to-all-start = ((bf16[128,98,128]{2,1,0:T(8,128)(2,1)}), bf16[128,98,128]{2,1,0:T(8,128)(2,1)S(1)}, u32[]{:S(2)}, u32[]{:S(2)}) async-start(bf16[128,98,128]{2,1,0:T(8,128)(2,1)} %get-tuple-element.51), calls=%async_computation | async-start | bytes 6815744 | tf_op jit(solution)/shard_map/all_to_all | solution.py:880
  65.5 56.2 %all-to-all-start.1 = ((bf16[128,32,384]{2,1,0:T(8,128)(2,1)}), bf16[128,32,384]{2,1,0:T(8,128)(2,1)}, u32[]{:S(2)}, u32[]{:S(2)}) async-start(bf16[128,32,384]{2,1,0:T(8,128)(2,1)} %pack_rows.1), calls=%async_computation.1 | async-start | bytes 6291456 | tf_op jit(solution)/shard_map/all_to_all | solution.py:880
  121.7 65.1 %all-to-all-start.2 = ((bf16[128,32,384]{2,1,0:T(8,128)(2,1)}), bf16[128,32,384]{2,1,0:T(8,128)(2,1)S(1)}, u32[]{:S(2)}, u32[]{:S(2)}) async-start(bf16[128,32,384]{2,1,0:T(8,128)(2,1)} %return_rows.1), calls=%async_computation.2 | async-start | bytes 6291456 | tf_op jit(solution)/shard_map/all_to_all | solution.py:880
  199.4 50.7 %all-to-all-start.3 = ((bf16[128,32,384]{2,1,0:T(8,128)(2,1)}), bf16[128,32,384]{2,1,0:T(8,128)(2,1)S(1)}, u32[]{:S(2)}, u32[]{:S(2)}) async-start(bf16[128,32,384]{2,1,0:T(8,128)(2,1)} %inputs_back.1), calls=%async_computation.3 | async-start | bytes 6291456 | tf_op jit(solution)/shard_map/all_to_all | solution.py:880
  224.0 11.9 %collective-permute-start = (bf16[768,384]{1,0:T(8,128)(2,1)}, bf16[768,384]{1,0:T(8,128)(2,1)}, u32[]{:S(2)}, u32[]{:S(2)}) collective-permute-start(bf16[768,384]{1,0:T(8,128)(2,1)} %get-tuple-element.100), channel_id=1, source_target_pairs={{0,16},{16,0},{32,48},{48,32},{64,80},{80,64},{96,112},{112,96},{1... | collective-permute-start | bytes 1769480 | tf_op jit(solution)/shard_map/ppermute | solution.py:779
  227.9 8.0 %collective-permute-start.1 = (bf16[768,384]{1,0:T(8,128)(2,1)}, bf16[768,384]{1,0:T(8,128)(2,1)}, u32[]{:S(2)}, u32[]{:S(2)}) collective-permute-start(bf16[768,384]{1,0:T(8,128)(2,1)} %get-tuple-element.98), channel_id=1, source_target_pairs={{0,16},{16,0},{32,48},{48,32},{64,80},{80,64},{96,112},{112,96},{1... | collective-permute-start | bytes 1769480 | tf_op jit(solution)/shard_map/ppermute | solution.py:779
  227.9 8.0 %collective-permute-start.2 = (bf16[768,384]{1,0:T(8,128)(2,1)}, bf16[768,384]{1,0:T(8,128)(2,1)}, u32[]{:S(2)}, u32[]{:S(2)}) collective-permute-start(bf16[768,384]{1,0:T(8,128)(2,1)} %get-tuple-element.96), channel_id=1, source_target_pairs={{0,16},{16,0},{32,48},{48,32},{64,80},{80,64},{96,112},{112,96},{1... | collective-permute-start | bytes 1769480 | tf_op jit(solution)/shard_map/ppermute | solution.py:779
  253.4 11.6 %collective-permute-start.3 = (bf16[384,384]{1,0:T(8,128)(2,1)}, bf16[384,384]{1,0:T(8,128)(2,1)}, u32[]{:S(2)}, u32[]{:S(2)}) collective-permute-start(bf16[384,384]{1,0:T(8,128)(2,1)} %get-tuple-element.106), channel_id=1, source_target_pairs={{0,32},{16,48},{32,0},{48,16},{64,96},{80,112},{96,64},{112,80},{1... | collective-permute-start | bytes 884744 | tf_op jit(solution)/shard_map/ppermute | solution.py:779
  256.0 9.0 %collective-permute-start.5 = (bf16[384,384]{1,0:T(8,128)(2,1)}, bf16[384,384]{1,0:T(8,128)(2,1)S(1)}, u32[]{:S(2)}, u32[]{:S(2)}) collective-permute-start(bf16[384,384]{1,0:T(8,128)(2,1)} %get-tuple-element.102), channel_id=1, source_target_pairs={{0,1},{1,0},{2,3},{3,2},{4,5},{5,4},{6,7},{7,6},{8,9},{9,8},{10,11... | collective-permute-start | bytes 884744 | tf_op jit(solution)/shard_map/ppermute | solution.py:779
  256.8 8.2 %collective-permute-start.4 = (bf16[384,384]{1,0:T(8,128)(2,1)S(1)}, bf16[384,384]{1,0:T(8,128)(2,1)S(1)}, u32[]{:S(2)}, u32[]{:S(2)}) collective-permute-start(bf16[384,384]{1,0:T(8,128)(2,1)S(1)} %get-tuple-element.104), channel_id=1, source_target_pairs={{0,4},{1,5},{2,6},{3,7},{4,0},{5,1},{6,2},{7,3},{8,12},{9,13},{10,... | collective-permute-start | bytes 884744 | tf_op jit(solution)/shard_map/ppermute | solution.py:779
  266.8 5.8 %collective-permute-start.14 = (bf16[192,384]{1,0:T(8,128)(2,1)S(1)}, bf16[192,384]{1,0:T(8,128)(2,1)S(1)}, u32[]{:S(2)}, u32[]{:S(2)}) collective-permute-start(bf16[192,384]{1,0:T(8,128)(2,1)S(1)} %constant_dynamic-slice_fusion.1), channel_id=1, source_target_pairs={{0,12},{1,13},{2,14},{3,15},{4,8},{5,9},{6,10},{7,11},{8,4},{9,5},... | collective-permute-start | bytes 442376 | tf_op jit(solution)/shard_map/ppermute | solution.py:779
  269.8 5.4 %collective-permute-start.22 = (bf16[192,384]{1,0:T(8,128)(2,1)S(1)}, bf16[192,384]{1,0:T(8,128)(2,1)S(1)}, u32[]{:S(2)}, u32[]{:S(2)}) collective-permute-start(bf16[192,384]{1,0:T(8,128)(2,1)S(1)} %constant_dynamic-slice_fusion), channel_id=1, source_target_pairs={{0,3},{1,2},{2,1},{3,0},{4,7},{5,6},{6,5},{7,4},{8,11},{9,10},{10,... | collective-permute-start | bytes 442376 | tf_op jit(solution)/shard_map/ppermute | solution.py:779
  275.8 5.3 %collective-permute-start.8 = (bf16[192,384]{1,0:T(8,128)(2,1)S(1)}, bf16[192,384]{1,0:T(8,128)(2,1)S(1)}, u32[]{:S(2)}, u32[]{:S(2)}) collective-permute-start(bf16[192,384]{1,0:T(8,128)(2,1)S(1)} %add_convert_fusion.19), channel_id=1, source_target_pairs={{0,12},{1,13},{2,14},{3,15},{4,8},{5,9},{6,10},{7,11},{8,4},{9,5},... | collective-permute-start | bytes 442376 | tf_op jit(solution)/shard_map/ppermute | solution.py:779
  277.5 5.3 %collective-permute-start.16 = (bf16[192,384]{1,0:T(8,128)(2,1)S(1)}, bf16[192,384]{1,0:T(8,128)(2,1)S(1)}, u32[]{:S(2)}, u32[]{:S(2)}) collective-permute-start(bf16[192,384]{1,0:T(8,128)(2,1)S(1)} %add_convert_fusion.14), channel_id=1, source_target_pairs={{0,3},{1,2},{2,1},{3,0},{4,7},{5,6},{6,5},{7,4},{8,11},{9,10},{10,... | collective-permute-start | bytes 442376 | tf_op jit(solution)/shard_map/ppermute | solution.py:779
  279.7 5.6 %collective-permute-start.24 = (bf16[192,384]{1,0:T(8,128)(2,1)S(1)}, bf16[192,384]{1,0:T(8,128)(2,1)S(1)}, u32[]{:S(2)}, u32[]{:S(2)}) collective-permute-start(bf16[192,384]{1,0:T(8,128)(2,1)S(1)} %add_convert_fusion.9), channel_id=1, source_target_pairs={{0,96},{16,112},{32,64},{48,80},{64,32},{80,48},{96,0},{112,16},{1... | collective-permute-start | bytes 442376 | tf_op jit(solution)/shard_map/ppermute | solution.py:779
  286.1 5.3 %collective-permute-start.10 = (bf16[192,384]{1,0:T(8,128)(2,1)S(1)}, bf16[192,384]{1,0:T(8,128)(2,1)S(1)}, u32[]{:S(2)}, u32[]{:S(2)}) collective-permute-start(bf16[192,384]{1,0:T(8,128)(2,1)S(1)} %add_convert_fusion.17), channel_id=1, source_target_pairs={{0,3},{1,2},{2,1},{3,0},{4,7},{5,6},{6,5},{7,4},{8,11},{9,10},{10,... | collective-permute-start | bytes 442376 | tf_op jit(solution)/shard_map/ppermute | solution.py:779
  288.0 5.3 %collective-permute-start.18 = (bf16[192,384]{1,0:T(8,128)(2,1)S(1)}, bf16[192,384]{1,0:T(8,128)(2,1)S(1)}, u32[]{:S(2)}, u32[]{:S(2)}) collective-permute-start(bf16[192,384]{1,0:T(8,128)(2,1)S(1)} %add_convert_fusion.12), channel_id=1, source_target_pairs={{0,96},{16,112},{32,64},{48,80},{64,32},{80,48},{96,0},{112,16},{1... | collective-permute-start | bytes 442376 | tf_op jit(solution)/shard_map/ppermute | solution.py:779
  291.4 5.6 %collective-permute-start.11 = (bf16[192,384]{1,0:T(8,128)(2,1)S(1)}, bf16[192,384]{1,0:T(8,128)(2,1)S(1)}, u32[]{:S(2)}, u32[]{:S(2)}) collective-permute-start(bf16[192,384]{1,0:T(8,128)(2,1)S(1)} %add_convert_fusion.16), channel_id=1, source_target_pairs={{0,96},{16,112},{32,64},{48,80},{64,32},{80,48},{96,0},{112,16},{1... | collective-permute-start | bytes 442376 | tf_op jit(solution)/shard_map/ppermute | solution.py:779
  293.4 5.6 %collective-permute-start.19 = (bf16[192,384]{1,0:T(8,128)(2,1)S(1)}, bf16[192,384]{1,0:T(8,128)(2,1)S(1)}, u32[]{:S(2)}, u32[]{:S(2)}) collective-permute-start(bf16[192,384]{1,0:T(8,128)(2,1)S(1)} %add_convert_fusion.11), channel_id=1, source_target_pairs={{0,12},{1,13},{2,14},{3,15},{4,8},{5,9},{6,10},{7,11},{8,4},{9,5},... | collective-permute-start | bytes 442376 | tf_op jit(solution)/shard_map/ppermute | solution.py:779
  295.3 5.6 %collective-permute-start.27 = (bf16[192,384]{1,0:T(8,128)(2,1)S(1)}, bf16[192,384]{1,0:T(8,128)(2,1)S(1)}, u32[]{:S(2)}, u32[]{:S(2)}) collective-permute-start(bf16[192,384]{1,0:T(8,128)(2,1)S(1)} %add_convert_fusion.6), channel_id=1, source_target_pairs={{0,3},{1,2},{2,1},{3,0},{4,7},{5,6},{6,5},{7,4},{8,11},{9,10},{10,... | collective-permute-start | bytes 442376 | tf_op jit(solution)/shard_map/ppermute | solution.py:779
  297.1 5.9 %collective-permute-start.12 = (bf16[384,384]{1,0:T(8,128)(2,1)S(1)}, bf16[384,384]{1,0:T(8,128)(2,1)S(1)}, u32[]{:S(2)}, u32[]{:S(2)}) collective-permute-start(bf16[384,384]{1,0:T(8,128)(2,1)S(1)} %maximum_select_fusion.3), channel_id=1, source_target_pairs={{0,32},{16,48},{32,0},{48,16},{64,96},{80,112},{96,64},{112,80},{1... | collective-permute-start | bytes 884744 | tf_op jit(solution)/shard_map/ppermute | solution.py:779
  299.0 12.2 %collective-permute-start.20 = (bf16[384,384]{1,0:T(8,128)(2,1)S(1)}, bf16[384,384]{1,0:T(8,128)(2,1)S(1)}, u32[]{:S(2)}, u32[]{:S(2)}) collective-permute-start(bf16[384,384]{1,0:T(8,128)(2,1)S(1)} %maximum_select_fusion.4), channel_id=1, source_target_pairs={{0,4},{1,5},{2,6},{3,7},{4,0},{5,1},{6,2},{7,3},{8,12},{9,13},{10,... | collective-permute-start | bytes 884744 | tf_op jit(solution)/shard_map/ppermute | solution.py:779
  301.0 12.3 %collective-permute-start.28 = (bf16[384,384]{1,0:T(8,128)(2,1)S(1)}, bf16[384,384]{1,0:T(8,128)(2,1)S(1)}, u32[]{:S(2)}, u32[]{:S(2)}) collective-permute-start(bf16[384,384]{1,0:T(8,128)(2,1)S(1)} %maximum_select_fusion.5), channel_id=1, source_target_pairs={{0,1},{1,0},{2,3},{3,2},{4,5},{5,4},{6,7},{7,6},{8,9},{9,8},{10,11... | collective-permute-start | bytes 884744 | tf_op jit(solution)/shard_map/ppermute | solution.py:779
  303.2 11.7 %collective-permute-start.13 = (bf16[768,384]{1,0:T(8,128)(2,1)S(1)}, bf16[768,384]{1,0:T(8,128)(2,1)S(1)}, u32[]{:S(2)}, u32[]{:S(2)}) collective-permute-start(bf16[768,384]{1,0:T(8,128)(2,1)S(1)} %maximum_select_fusion.w1_ref), channel_id=1, source_target_pairs={{0,16},{16,0},{32,48},{48,32},{64,80},{80,64},{96,112},{112,96},{1... | collective-permute-start | bytes 1769480 | tf_op jit(solution)/shard_map/ppermute | solution.py:779
  (25 other events, 152.2 us)

commit v5 on v4

--- a/solution.py
+++ b/solution.py
@@ -171,7 +171,7 @@
         out_specs=pl.BlockSpec((ROWS, D), lambda i: (0, 0)),
         out_shape=jax.ShapeDtypeStruct((ROWS, D), BF),
         scratch_shapes=[pltpu.VMEM((ROWS, LANES), jnp.int32), pltpu.VMEM((ROWS, D), F32)],
-        compiler_params=params(),
+        compiler_params=params(mib=36),
         cost_estimate=NO_COST,
         name="unpack_rows",
     )(slot_row, home)
@@ -753,7 +753,7 @@
         out_specs=[down] * 3,
         out_shape=[jax.ShapeDtypeStruct((FF, D), BF)] * 3,
         scratch_shapes=[pltpu.VMEM((D, ROWS), BF)] * 3,
-        compiler_params=params(),
+        compiler_params=params(mib=36),
         cost_estimate=NO_COST,
         name="weights_back",
     )(ordered, middle, mixed, d_middle, upstream, d_packed, d_before, hidden)
@@ -867,7 +867,7 @@
             jax.ShapeDtypeStruct((D, FF), F32),
             jax.ShapeDtypeStruct((FF, D), F32),
         ],
-        compiler_params=params(),
+        compiler_params=params(mib=36),
         cost_estimate=NO_COST,
         name="finish",
     )(keep, *halves)

time: 330 us -> 324 us (0.982)
  Pallas kernels: 166 us -> 158 us
  local copies, waits for them, and re-layouts: 10.7 us -> 16.5 us
    unnamed x30, local copies, waits for them, and re-layouts: 3.13 us -> 11.8 us
    pallas_call x1, Pallas kernels: 12.3 us -> 8.9 us  [weights_back(): pl.pallas_call(weights_back_kernel, grid=(FF // D,), in_specs=[rows] * 5...]
  transfers between devices with their start and end apart: 34 -> 34, of which waited for: 16 -> 16; matrix products, arithmetic and copies ran while one was open for 3% -> 2% of each run, Pallas kernels for 43% -> 42%
where the time goes in v5:
time: 324 us; the launch traced here: 318 us
  Pallas kernels  158 us (49%)
  starting transfers between devices  74.6 us (23%)
  waiting for transfers between devices  63.3 us (20%)
  local copies, waits for them, and re-layouts  16.5 us (5%)
  other arithmetic  4.74 us (1%)
    all_to_all x4, waiting for transfers between devices, exchange(): return lax.all_to_all(values, AXES, split_axis=0, concat_axis=0, tiled=True)  48.6 us
    pallas_call x1, Pallas kernels, attend_back(): pl.pallas_call(attend_back_kernel, grid=(GROUPS,), in_specs=[whole((ROWS,...  37.4 us
    ppermute x30, starting transfers between devices, swap(): return lax.ppermute(values, name, pairs)  37.4 us
    all_to_all x4, starting transfers between devices, exchange(): return lax.all_to_all(values, AXES, split_axis=0, concat_axis=0, tiled=True)  37.2 us
    pallas_call x1, Pallas kernels, attend(): pl.pallas_call(attend_kernel, grid=(GROUPS,), in_specs=[whole((ROWS, 1)),...  20.9 us
    ppermute x30, waiting for transfers between devices, swap(): return lax.ppermute(values, name, pairs)  14.7 us
    pallas_call x2, Pallas kernels, unpack_rows(): pl.pallas_call(unpack_rows_kernel, grid=(STEPS,), in_specs=[pl.BlockSpec(...  14 us
    unnamed x30, local copies, waits for them, and re-layouts  11.8 us
  transfers between devices with their start and end apart: 34, of which 16 were waited for; matrix products, arithmetic and copies ran while one was open for 2% of the time, Pallas kernels for 42%

profile of v5, /device:TPU:1, one launch (start us, length us, event | category | flops | bytes accessed | tf_op | source)
XLA Modules:
  0.0 318.5 jit_solution(4939848062280014237)
XLA Ops:
  0.6 7.8 %pack_points.1 = (bf16[128,98,128]{2,1,0:T(8,128)(2,1)}, s32[1,1024]{1,0:T(1,128)}) custom-call(s32[1]{0:T(128)} %bitcast.lane_ref, s32[1,1024]{1,0:T(1,128)} %bitcast.8, bf16[1024,384]{1,0:T(8,128)(2,1)} %x_ref.2), custom_call_target="tpu_custom_call" | custom-call | flops 1 | bytes 1 | tf_op jit(solution)/shard_map/pack_points/pallas_call | solution.py:100
  8.4 11.5 %all-to-all-start = ((bf16[128,98,128]{2,1,0:T(8,128)(2,1)}), bf16[128,98,128]{2,1,0:T(8,128)(2,1)S(1)}, u32[]{:S(2)}, u32[]{:S(2)}) async-start(bf16[128,98,128]{2,1,0:T(8,128)(2,1)} %get-tuple-element.51), calls=%async_computation | async-start | bytes 6815744 | tf_op jit(solution)/shard_map/all_to_all | solution.py:880
  19.9 7.1 %pack_rows.1 = bf16[128,32,384]{2,1,0:T(8,128)(2,1)} custom-call(s32[1,1024]{1,0:T(1,128)} %get-tuple-element.53.slot_ref, bf16[1024,384]{1,0:T(8,128)(2,1)} %x_ref.3), custom_call_target="tpu_custom_call" | custom-call | flops 1 | bytes 1 | tf_op jit(solution)/shard_map/pack_rows/pallas_call | solution.py:129
  27.0 36.8 %all-to-all-done.recv_ref = bf16[128,98,128]{2,1,0:T(8,128)(2,1)S(1)} async-done(((bf16[128,98,128]{2,1,0:T(8,128)(2,1)}), bf16[128,98,128]{2,1,0:T(8,128)(2,1)S(1)}, u32[]{:S(2)}, u32[]{:S(2)}) %all-to-all-start) | async-done | bytes 3211296 | tf_op jit(solution)/shard_map/all_to_all | solution.py:880
  65.5 5.6 %all-to-all-start.1 = ((bf16[128,32,384]{2,1,0:T(8,128)(2,1)}), bf16[128,32,384]{2,1,0:T(8,128)(2,1)}, u32[]{:S(2)}, u32[]{:S(2)}) async-start(bf16[128,32,384]{2,1,0:T(8,128)(2,1)} %pack_rows.1), calls=%async_computation.1 | async-start | bytes 6291456 | tf_op jit(solution)/shard_map/all_to_all | solution.py:880
  72.2 9.9 %land_points.1 = (bf16[1024,384]{1,0:T(8,128)(2,1)}, bf16[1024,1152]{1,0:T(8,128)(2,1)}, s32[2,1,2048]{2,1,0:T(1,128)}) custom-call(bf16[128,98,128]{2,1,0:T(8,128)(2,1)} %copy-done.11, bf16[384,1152]{1,0:T(8,128)(2,1)} %w_ref.3), custom_call_target="tpu_custom_call" | custom-call | flops 1 | bytes 1 | tf_op jit(solution)/shard_map/land_points/pallas_call | solution.py:230
  82.2 20.9 %attend.1 = (bf16[1024,384]{1,0:T(8,128)(2,1)}, f32[1024,384]{1,0:T(8,128)}, f32[1024,384]{1,0:T(8,128)}) custom-call(s32[1024,1]{1,0:T(8,128)} %copy.14.column_ref, s32[1,1024]{1,0:T(1,128)} %bitcast.5, bf16[1024,1152]{1,0:T(8,128)(2,1)} %get-tuple-element.55.q_ref.k_ref.v_ref, bf16[1024,1152]{1,0:T(8,128)(2,1)} %get-tuple-element.55.q_ref.k_ref.v_ref, ...), custom_call_target="tpu_custom_call" | custom-call | flops 1 | bytes 1 | tf_op jit(solution)/shard_map/attend/pallas_call | solution.py:411
  103.0 10.8 %mlp.1 = (bf16[1024,384]{1,0:T(8,128)(2,1)}, bf16[1024,384]{1,0:T(8,128)(2,1)}, bf16[1024,1536]{1,0:T(8,128)(2,1)}, f32[1024,1536]{1,0:T(8,128)}) custom-call(bf16[1024,384]{1,0:T(8,128)(2,1)} %get-tuple-element.52.ordered_ref, bf16[1024,384]{1,0:T(8,128)(2,1)} %get-tuple-element.56.mixed_ref, bf16[384,384]{1,0:T(8,128)(2,1)} %w_proj_ref.3, ...), custom_call_target="tpu_custom_call" | custom-call | flops 1 | bytes 1 | tf_op jit(solution)/shard_map/mlp/pallas_call | solution.py:569
  113.8 8.1 %return_rows.1 = bf16[128,32,384]{2,1,0:T(8,128)(2,1)} custom-call(s32[2,1,2048]{2,1,0:T(1,128)} %get-tuple-element.58.landing_ref, bf16[1024,384]{1,0:T(8,128)(2,1)} %get-tuple-element.59.x_ref), custom_call_target="tpu_custom_call" | custom-call | flops 1 | bytes 1 | tf_op jit(solution)/shard_map/return_rows/pallas_call | solution.py:296
  121.9 9.9 %all-to-all-start.2 = ((bf16[128,32,384]{2,1,0:T(8,128)(2,1)}), bf16[128,32,384]{2,1,0:T(8,128)(2,1)S(1)}, u32[]{:S(2)}, u32[]{:S(2)}) async-start(bf16[128,32,384]{2,1,0:T(8,128)(2,1)} %return_rows.1), calls=%async_computation.2 | async-start | bytes 6291456 | tf_op jit(solution)/shard_map/all_to_all | solution.py:880
  131.8 7.3 %land_rows.1.up_ref = bf16[1024,384]{1,0:T(8,128)(2,1)} custom-call(s32[2,1,2048]{2,1,0:T(1,128)} %get-tuple-element.58.landing_ref, bf16[128,32,384]{2,1,0:T(8,128)(2,1)} %all-to-all-done.1.recv_ref), custom_call_target="tpu_custom_call" | custom-call | flops 1 | bytes 1 | tf_op jit(solution)/shard_map/land_rows/pallas_call | solution.py:269
  139.1 10.6 %mlp_back.1 = (bf16[1024,384]{1,0:T(8,128)(2,1)}, bf16[1024,384]{1,0:T(8,128)(2,1)}, bf16[1024,1536]{1,0:T(8,128)(2,1)}) custom-call(bf16[1024,384]{1,0:T(8,128)(2,1)} %land_rows.1.up_ref, bf16[1024,384]{1,0:T(8,128)(2,1)} %get-tuple-element.57.middle_ref, f32[1024,1536]{1,0:T(8,128)} %get-tuple-element.62.slope_ref, bf16[384,384]{1,0:T(8,128)(2,1)} %w_proj_ref.3, ...), custom_call_target="tpu_custom_call" | custom-call | flops 1 | bytes 1 | tf_op jit(solution)/shard_map/mlp_back/pallas_call | solution.py:632
  149.7 37.4 %attend_back.1.d_packed_ref = bf16[1024,1152]{1,0:T(8,128)(2,1)} custom-call(s32[1024,1]{1,0:T(8,128)} %copy.14.column_ref, s32[1,1024]{1,0:T(1,128)} %bitcast.6, bf16[1024,1152]{1,0:T(8,128)(2,1)} %get-tuple-element.55.q_ref.k_ref.v_ref, bf16[1024,1152]{1,0:T(8,128)(2,1)} %get-tuple-element.55.q_ref.k_ref.v_ref, ...), custom_call_target="tpu_custom_call" | custom-call | flops 1 | bytes 1 | tf_op jit(solution)/shard_map/attend_back/pallas_call | solution.py:497
  188.9 11.7 %inputs_back.1 = bf16[128,32,384]{2,1,0:T(8,128)(2,1)} custom-call(s32[2,1,2048]{2,1,0:T(1,128)} %get-tuple-element.58.landing_ref, bf16[1024,384]{1,0:T(8,128)(2,1)} %get-tuple-element.52.ordered_ref, bf16[1024,1152]{1,0:T(8,128)(2,1)} %attend_back.1.d_packed_ref, bf16[1024,384]{1,0:T(8,128)(2,1)} %get-tuple-element.63.d_middle_ref, bf16[384,1152]{1,0:T(8,128)(2,1)} %w_ref.3), custom_call_target="tpu_custom_call" | custom-call | flops 1 | bytes 1 | tf_op jit(solution)/shard_map/inputs_back/pallas_call | solution.py:685
  200.6 10.2 %all-to-all-start.3 = ((bf16[128,32,384]{2,1,0:T(8,128)(2,1)}), bf16[128,32,384]{2,1,0:T(8,128)(2,1)}, u32[]{:S(2)}, u32[]{:S(2)}) async-start(bf16[128,32,384]{2,1,0:T(8,128)(2,1)} %inputs_back.1), calls=%async_computation.3 | async-start | bytes 6291456 | tf_op jit(solution)/shard_map/all_to_all | solution.py:880
  219.1 8.9 %weights_back.1 = (bf16[1536,384]{1,0:T(8,128)(2,1)S(1)}, bf16[1536,384]{1,0:T(8,128)(2,1)S(1)}, bf16[1536,384]{1,0:T(8,128)(2,1)S(1)}) custom-call(bf16[1024,384]{1,0:T(8,128)(2,1)S(1)} %copy-done.4, bf16[1024,384]{1,0:T(8,128)(2,1)S(1)} %copy-done.6, bf16[1024,384]{1,0:T(8,128)(2,1)S(1)} %copy-done.5, bf16[1024,384]{1,0:T(8,128)(2,1)S(1)} %copy-done.9, ...), custom_call_target="tpu_custom_call" | custom-call | flops 1 | bytes 1 | tf_op jit(solution)/shard_map/weights_back/pallas_call | solution.py:748
  233.1 6.5 %unpack_rows.2 = bf16[1024,384]{1,0:T(8,128)(2,1)} custom-call(s32[1,1024]{1,0:T(1,128)S(1)} %copy-done.10, bf16[128,32,384]{2,1,0:T(8,128)(2,1)S(1)} %copy-done.2), custom_call_target="tpu_custom_call" | custom-call | flops 1 | bytes 1 | tf_op jit(solution)/shard_map/unpack_rows/pallas_call | solution.py:164
  239.6 11.8 %all-to-all-done.3.home_ref = bf16[128,32,384]{2,1,0:T(8,128)(2,1)} async-done(((bf16[128,32,384]{2,1,0:T(8,128)(2,1)}), bf16[128,32,384]{2,1,0:T(8,128)(2,1)}, u32[]{:S(2)}, u32[]{:S(2)}) %all-to-all-start.3) | async-done | bytes 3145760 | tf_op jit(solution)/shard_map/all_to_all | solution.py:880
  256.3 7.5 %unpack_rows.3 = bf16[1024,384]{1,0:T(8,128)(2,1)} custom-call(s32[1,1024]{1,0:T(1,128)S(1)} %copy-done.10, bf16[128,32,384]{2,1,0:T(8,128)(2,1)} %all-to-all-done.3.home_ref), custom_call_target="tpu_custom_call" | custom-call | flops 1 | bytes 1 | tf_op jit(solution)/shard_map/unpack_rows/pallas_call | solution.py:164
  264.6 3.0 collective-permute-start.14
  285.8 2.0 collective-permute-start.18
  299.0 2.0 collective-permute-done.12
  301.2 8.1 %collective-permute-start.13 = (bf16[768,384]{1,0:T(8,128)(2,1)S(1)}, bf16[768,384]{1,0:T(8,128)(2,1)S(1)}, u32[]{:S(2)}, u32[]{:S(2)}) collective-permute-start(bf16[768,384]{1,0:T(8,128)(2,1)S(1)} %maximum_select_fusion.w1_ref), channel_id=1, source_target_pairs={{0,16},{16,0},{32,48},{48,32},{64,80},{80,64},{96,112},{112,96},{1... | collective-permute-start | bytes 1769480 | tf_op jit(solution)/shard_map/ppermute | solution.py:779
  314.6 3.7 %finish.1 = (f32[384,1152]{1,0:T(8,128)}, f32[384,384]{1,0:T(8,128)}, f32[384,1536]{1,0:T(8,128)}, f32[1536,384]{1,0:T(8,128)}) custom-call(s32[1]{0:T(128)} %bitcast.4.keep_ref, bf16[768,384]{1,0:T(8,128)(2,1)S(1)} %maximum_select_fusion.w1_ref, bf16[768,384]{1,0:T(8,128)(2,1)S(1)} %collective-permute-done.13.w1_other_ref, ...), custom_call_target="tpu_custom_call" | custom-call | flops 1 | bytes 1 | tf_op jit(solution)/shard_map/finish/pallas_call | solution.py:854
  (124 shorter events, 58.3 us)
Async XLA Ops:
  8.4 55.4 %all-to-all-start = ((bf16[128,98,128]{2,1,0:T(8,128)(2,1)}), bf16[128,98,128]{2,1,0:T(8,128)(2,1)S(1)}, u32[]{:S(2)}, u32[]{:S(2)}) async-start(bf16[128,98,128]{2,1,0:T(8,128)(2,1)} %get-tuple-element.51), calls=%async_computation | async-start | bytes 6815744 | tf_op jit(solution)/shard_map/all_to_all | solution.py:880
  65.5 56.4 %all-to-all-start.1 = ((bf16[128,32,384]{2,1,0:T(8,128)(2,1)}), bf16[128,32,384]{2,1,0:T(8,128)(2,1)}, u32[]{:S(2)}, u32[]{:S(2)}) async-start(bf16[128,32,384]{2,1,0:T(8,128)(2,1)} %pack_rows.1), calls=%async_computation.1 | async-start | bytes 6291456 | tf_op jit(solution)/shard_map/all_to_all | solution.py:880
  121.9 65.2 %all-to-all-start.2 = ((bf16[128,32,384]{2,1,0:T(8,128)(2,1)}), bf16[128,32,384]{2,1,0:T(8,128)(2,1)S(1)}, u32[]{:S(2)}, u32[]{:S(2)}) async-start(bf16[128,32,384]{2,1,0:T(8,128)(2,1)} %return_rows.1), calls=%async_computation.2 | async-start | bytes 6291456 | tf_op jit(solution)/shard_map/all_to_all | solution.py:880
  200.6 50.8 %all-to-all-start.3 = ((bf16[128,32,384]{2,1,0:T(8,128)(2,1)}), bf16[128,32,384]{2,1,0:T(8,128)(2,1)}, u32[]{:S(2)}, u32[]{:S(2)}) async-start(bf16[128,32,384]{2,1,0:T(8,128)(2,1)} %inputs_back.1), calls=%async_computation.3 | async-start | bytes 6291456 | tf_op jit(solution)/shard_map/all_to_all | solution.py:880
  229.1 10.5 %collective-permute-start = (bf16[768,384]{1,0:T(8,128)(2,1)}, bf16[768,384]{1,0:T(8,128)(2,1)}, u32[]{:S(2)}, u32[]{:S(2)}) collective-permute-start(bf16[768,384]{1,0:T(8,128)(2,1)} %get-tuple-element.100), channel_id=1, source_target_pairs={{0,16},{16,0},{32,48},{48,32},{64,80},{80,64},{96,112},{112,96},{1... | collective-permute-start | bytes 1769480 | tf_op jit(solution)/shard_map/ppermute | solution.py:779
  232.6 7.0 %collective-permute-start.1 = (bf16[768,384]{1,0:T(8,128)(2,1)}, bf16[768,384]{1,0:T(8,128)(2,1)}, u32[]{:S(2)}, u32[]{:S(2)}) collective-permute-start(bf16[768,384]{1,0:T(8,128)(2,1)} %get-tuple-element.98), channel_id=1, source_target_pairs={{0,16},{16,0},{32,48},{48,32},{64,80},{80,64},{96,112},{112,96},{1... | collective-permute-start | bytes 1769480 | tf_op jit(solution)/shard_map/ppermute | solution.py:779
  232.6 7.0 %collective-permute-start.2 = (bf16[768,384]{1,0:T(8,128)(2,1)}, bf16[768,384]{1,0:T(8,128)(2,1)}, u32[]{:S(2)}, u32[]{:S(2)}) collective-permute-start(bf16[768,384]{1,0:T(8,128)(2,1)} %get-tuple-element.96), channel_id=1, source_target_pairs={{0,16},{16,0},{32,48},{48,32},{64,80},{80,64},{96,112},{112,96},{1... | collective-permute-start | bytes 1769480 | tf_op jit(solution)/shard_map/ppermute | solution.py:779
  253.0 10.8 %collective-permute-start.3 = (bf16[384,384]{1,0:T(8,128)(2,1)S(1)}, bf16[384,384]{1,0:T(8,128)(2,1)S(1)}, u32[]{:S(2)}, u32[]{:S(2)}) collective-permute-start(bf16[384,384]{1,0:T(8,128)(2,1)S(1)} %get-tuple-element.106), channel_id=1, source_target_pairs={{0,32},{16,48},{32,0},{48,16},{64,96},{80,112},{96,64},{112,80},{1... | collective-permute-start | bytes 884744 | tf_op jit(solution)/shard_map/ppermute | solution.py:779
  254.7 9.1 %collective-permute-start.5 = (bf16[384,384]{1,0:T(8,128)(2,1)S(1)}, bf16[384,384]{1,0:T(8,128)(2,1)S(1)}, u32[]{:S(2)}, u32[]{:S(2)}) collective-permute-start(bf16[384,384]{1,0:T(8,128)(2,1)S(1)} %get-tuple-element.102), channel_id=1, source_target_pairs={{0,1},{1,0},{2,3},{3,2},{4,5},{5,4},{6,7},{7,6},{8,9},{9,8},{10,11... | collective-permute-start | bytes 884744 | tf_op jit(solution)/shard_map/ppermute | solution.py:779
  255.6 8.1 %collective-permute-start.4 = (bf16[384,384]{1,0:T(8,128)(2,1)S(1)}, bf16[384,384]{1,0:T(8,128)(2,1)S(1)}, u32[]{:S(2)}, u32[]{:S(2)}) collective-permute-start(bf16[384,384]{1,0:T(8,128)(2,1)S(1)} %get-tuple-element.104), channel_id=1, source_target_pairs={{0,4},{1,5},{2,6},{3,7},{4,0},{5,1},{6,2},{7,3},{8,12},{9,13},{10,... | collective-permute-start | bytes 884744 | tf_op jit(solution)/shard_map/ppermute | solution.py:779
  264.6 5.8 %collective-permute-start.14 = (bf16[192,384]{1,0:T(8,128)(2,1)S(1)}, bf16[192,384]{1,0:T(8,128)(2,1)S(1)}, u32[]{:S(2)}, u32[]{:S(2)}) collective-permute-start(bf16[192,384]{1,0:T(8,128)(2,1)S(1)} %constant_dynamic-slice_fusion.1), channel_id=1, source_target_pairs={{0,12},{1,13},{2,14},{3,15},{4,8},{5,9},{6,10},{7,11},{8,4},{9,5},... | collective-permute-start | bytes 442376 | tf_op jit(solution)/shard_map/ppermute | solution.py:779
  267.7 5.3 %collective-permute-start.22 = (bf16[192,384]{1,0:T(8,128)(2,1)S(1)}, bf16[192,384]{1,0:T(8,128)(2,1)S(1)}, u32[]{:S(2)}, u32[]{:S(2)}) collective-permute-start(bf16[192,384]{1,0:T(8,128)(2,1)S(1)} %constant_dynamic-slice_fusion), channel_id=1, source_target_pairs={{0,3},{1,2},{2,1},{3,0},{4,7},{5,6},{6,5},{7,4},{8,11},{9,10},{10,... | collective-permute-start | bytes 442376 | tf_op jit(solution)/shard_map/ppermute | solution.py:779
  273.6 5.3 %collective-permute-start.8 = (bf16[192,384]{1,0:T(8,128)(2,1)S(1)}, bf16[192,384]{1,0:T(8,128)(2,1)S(1)}, u32[]{:S(2)}, u32[]{:S(2)}) collective-permute-start(bf16[192,384]{1,0:T(8,128)(2,1)S(1)} %add_convert_fusion.19), channel_id=1, source_target_pairs={{0,12},{1,13},{2,14},{3,15},{4,8},{5,9},{6,10},{7,11},{8,4},{9,5},... | collective-permute-start | bytes 442376 | tf_op jit(solution)/shard_map/ppermute | solution.py:779
  275.3 5.3 %collective-permute-start.16 = (bf16[192,384]{1,0:T(8,128)(2,1)S(1)}, bf16[192,384]{1,0:T(8,128)(2,1)S(1)}, u32[]{:S(2)}, u32[]{:S(2)}) collective-permute-start(bf16[192,384]{1,0:T(8,128)(2,1)S(1)} %add_convert_fusion.14), channel_id=1, source_target_pairs={{0,3},{1,2},{2,1},{3,0},{4,7},{5,6},{6,5},{7,4},{8,11},{9,10},{10,... | collective-permute-start | bytes 442376 | tf_op jit(solution)/shard_map/ppermute | solution.py:779
  277.5 5.6 %collective-permute-start.24 = (bf16[192,384]{1,0:T(8,128)(2,1)S(1)}, bf16[192,384]{1,0:T(8,128)(2,1)S(1)}, u32[]{:S(2)}, u32[]{:S(2)}) collective-permute-start(bf16[192,384]{1,0:T(8,128)(2,1)S(1)} %add_convert_fusion.9), channel_id=1, source_target_pairs={{0,96},{16,112},{32,64},{48,80},{64,32},{80,48},{96,0},{112,16},{1... | collective-permute-start | bytes 442376 | tf_op jit(solution)/shard_map/ppermute | solution.py:779
  283.8 5.3 %collective-permute-start.10 = (bf16[192,384]{1,0:T(8,128)(2,1)S(1)}, bf16[192,384]{1,0:T(8,128)(2,1)S(1)}, u32[]{:S(2)}, u32[]{:S(2)}) collective-permute-start(bf16[192,384]{1,0:T(8,128)(2,1)S(1)} %add_convert_fusion.17), channel_id=1, source_target_pairs={{0,3},{1,2},{2,1},{3,0},{4,7},{5,6},{6,5},{7,4},{8,11},{9,10},{10,... | collective-permute-start | bytes 442376 | tf_op jit(solution)/shard_map/ppermute | solution.py:779
  287.9 5.6 %collective-permute-start.26 = (bf16[192,384]{1,0:T(8,128)(2,1)S(1)}, bf16[192,384]{1,0:T(8,128)(2,1)S(1)}, u32[]{:S(2)}, u32[]{:S(2)}) collective-permute-start(bf16[192,384]{1,0:T(8,128)(2,1)S(1)} %add_convert_fusion.7), channel_id=1, source_target_pairs={{0,12},{1,13},{2,14},{3,15},{4,8},{5,9},{6,10},{7,11},{8,4},{9,5},... | collective-permute-start | bytes 442376 | tf_op jit(solution)/shard_map/ppermute | solution.py:779
  289.2 5.8 %collective-permute-start.11 = (bf16[192,384]{1,0:T(8,128)(2,1)S(1)}, bf16[192,384]{1,0:T(8,128)(2,1)S(1)}, u32[]{:S(2)}, u32[]{:S(2)}) collective-permute-start(bf16[192,384]{1,0:T(8,128)(2,1)S(1)} %add_convert_fusion.16), channel_id=1, source_target_pairs={{0,96},{16,112},{32,64},{48,80},{64,32},{80,48},{96,0},{112,16},{1... | collective-permute-start | bytes 442376 | tf_op jit(solution)/shard_map/ppermute | solution.py:779
  291.1 5.6 %collective-permute-start.19 = (bf16[192,384]{1,0:T(8,128)(2,1)S(1)}, bf16[192,384]{1,0:T(8,128)(2,1)S(1)}, u32[]{:S(2)}, u32[]{:S(2)}) collective-permute-start(bf16[192,384]{1,0:T(8,128)(2,1)S(1)} %add_convert_fusion.11), channel_id=1, source_target_pairs={{0,12},{1,13},{2,14},{3,15},{4,8},{5,9},{6,10},{7,11},{8,4},{9,5},... | collective-permute-start | bytes 442376 | tf_op jit(solution)/shard_map/ppermute | solution.py:779
  293.5 5.3 %collective-permute-start.27 = (bf16[192,384]{1,0:T(8,128)(2,1)S(1)}, bf16[192,384]{1,0:T(8,128)(2,1)S(1)}, u32[]{:S(2)}, u32[]{:S(2)}) collective-permute-start(bf16[192,384]{1,0:T(8,128)(2,1)S(1)} %add_convert_fusion.6), channel_id=1, source_target_pairs={{0,3},{1,2},{2,1},{3,0},{4,7},{5,6},{6,5},{7,4},{8,11},{9,10},{10,... | collective-permute-start | bytes 442376 | tf_op jit(solution)/shard_map/ppermute | solution.py:779
  295.0 5.9 %collective-permute-start.12 = (bf16[384,384]{1,0:T(8,128)(2,1)S(1)}, bf16[384,384]{1,0:T(8,128)(2,1)S(1)}, u32[]{:S(2)}, u32[]{:S(2)}) collective-permute-start(bf16[384,384]{1,0:T(8,128)(2,1)S(1)} %maximum_select_fusion.3), channel_id=1, source_target_pairs={{0,32},{16,48},{32,0},{48,16},{64,96},{80,112},{96,64},{112,80},{1... | collective-permute-start | bytes 884744 | tf_op jit(solution)/shard_map/ppermute | solution.py:779
  296.8 12.4 %collective-permute-start.20 = (bf16[384,384]{1,0:T(8,128)(2,1)S(1)}, bf16[384,384]{1,0:T(8,128)(2,1)S(1)}, u32[]{:S(2)}, u32[]{:S(2)}) collective-permute-start(bf16[384,384]{1,0:T(8,128)(2,1)S(1)} %maximum_select_fusion.4), channel_id=1, source_target_pairs={{0,4},{1,5},{2,6},{3,7},{4,0},{5,1},{6,2},{7,3},{8,12},{9,13},{10,... | collective-permute-start | bytes 884744 | tf_op jit(solution)/shard_map/ppermute | solution.py:779
  298.9 12.2 %collective-permute-start.28 = (bf16[384,384]{1,0:T(8,128)(2,1)S(1)}, bf16[384,384]{1,0:T(8,128)(2,1)S(1)}, u32[]{:S(2)}, u32[]{:S(2)}) collective-permute-start(bf16[384,384]{1,0:T(8,128)(2,1)S(1)} %maximum_select_fusion.5), channel_id=1, source_target_pairs={{0,1},{1,0},{2,3},{3,2},{4,5},{5,4},{6,7},{7,6},{8,9},{9,8},{10,11... | collective-permute-start | bytes 884744 | tf_op jit(solution)/shard_map/ppermute | solution.py:779
  301.2 11.8 %collective-permute-start.13 = (bf16[768,384]{1,0:T(8,128)(2,1)S(1)}, bf16[768,384]{1,0:T(8,128)(2,1)S(1)}, u32[]{:S(2)}, u32[]{:S(2)}) collective-permute-start(bf16[768,384]{1,0:T(8,128)(2,1)S(1)} %maximum_select_fusion.w1_ref), channel_id=1, source_target_pairs={{0,16},{16,0},{32,48},{48,32},{64,80},{80,64},{96,112},{112,96},{1... | collective-permute-start | bytes 1769480 | tf_op jit(solution)/shard_map/ppermute | solution.py:779
  (25 other events, 129.8 us)
